TPU v7x, 32 devices: a whole 2x2x4 slice. The times are simulated.
32 devices in a mesh: grp: 2 (over y), exp: 16 (over z, x, core).
Axes of the slice: x: 2, y: 2, z: 4, core: 2. Of those that a mesh axis runs over, the one named last changes fastest.
Arguments:
- tokens: bfloat16 [4096, 1024], P(('grp', 'exp')), may hold values from -6 to 6
- w_in: bfloat16 [32, 1024, 768], P('exp', 'grp'), may hold values from -0.1875 to 0.1875
- w_out: bfloat16 [32, 384, 1024], P('exp', 'grp'), may hold values from -0.3125 to 0.3125
- moments_in: bfloat16 [32, 2, 1024, 768], P('exp', None, 'grp'), may hold values from -6 to 6
- moments_out: bfloat16 [32, 2, 384, 1024], P('exp', None, 'grp'), may hold values from -6 to 6
- expert_ids: int32 [4096, 8], P(('grp', 'exp')), may hold values from 0 to 23, all different within a row; in each aligned block of 128 rows (0 to 127, 128 to 255, ...) at most 64 rows name the same one
- route_weights: float32 [4096, 8], P(('grp', 'exp')), may hold values from 0.1 to 1
- old_plan: int32 [32], replicated, may hold values from 0 to 23, as said below
- new_plan: int32 [32], replicated, may hold values from 0 to 23, as said below
Outputs:
- mixed: bfloat16 [4096, 1024], P(('grp', 'exp'))
- new_w_in: bfloat16 [32, 1024, 768], P('exp', 'grp')
- new_w_out: bfloat16 [32, 384, 1024], P('exp', 'grp')
- new_moments_in: bfloat16 [32, 2, 1024, 768], P('exp', None, 'grp')
- new_moments_out: bfloat16 [32, 2, 384, 1024], P('exp', None, 'grp')
Inputs may be any that keep to these rules, and one draw needn't show every extreme that they name: `expert_ids`: each row names 8 different experts. Among the rows of one device no expert is named more than 64 times, and in every draw some device names some expert exactly 64 times. `old_plan`: every expert is held by one or two slots; exactly 8 experts are held by two. `new_plan`: every expert is held by one or two slots; exactly 8 experts are held by two.
All inputs are finite; a program needn't handle non-finite values.
Results may differ from a plain program's by a relative error of at most 0.0057.
Values may be sent and summed in bfloat16 or wider, within the bound.
No kernel may reach another device: no remote copies, remote signals or barrier semaphores. Data moves between devices by JAX's collectives and lax.ppermute only.
A program may use at most 64 MiB of HBM per device.

v0:
```python
import jax
import jax.numpy as jnp
from jax import lax
from jax.experimental import pallas as pl
from jax.experimental.pallas import tpu as pltpu
from jax.sharding import PartitionSpec as P

SUB = 8
LANE = 128
FIXED = 9


def to_tiles(x):
    slots, columns = x.shape[0], x.shape[-1]
    x = x.reshape(slots, -1, SUB, columns // LANE, LANE)
    return x.swapaxes(2, 3).reshape(slots, -1, SUB, LANE)


def from_tiles(x, shape):
    columns = shape[-1]
    x = x.reshape(shape[0], -1, columns // LANE, SUB, LANE)
    return x.swapaxes(2, 3).reshape(shape)


def pack(arrays, parts, after=None):
    tiles = [to_tiles(a) for a in arrays]
    slots = tiles[0].shape[0]
    extra = -sum(t.shape[1] for t in tiles) % parts
    if extra:
        tiles.append(jnp.zeros((slots, extra, SUB, LANE), tiles[0].dtype))
    packed = jnp.concatenate(tiles, axis=1) if len(tiles) > 1 else tiles[0]
    if after is not None:
        packed, after = lax.optimization_barrier((packed, after))
    return packed.reshape(slots, parts, -1, SUB, LANE).swapaxes(0, 1), after


def unpack(landed, arrays):
    slots = landed.shape[1]
    landed = landed.swapaxes(0, 1).reshape(slots, -1, SUB, LANE)
    outs, at = [], 0
    for a in arrays:
        count = a.size // (slots * SUB * LANE)
        outs.append(from_tiles(landed[:, at : at + count], a.shape))
        at += count
    return outs


def expert_kernel(first_ref, x_ref, *refs):
    *weight_refs, out_ref = refs
    width = out_ref.shape[1]
    half = (x_ref.shape[1] - width) // 2
    x = x_ref[:, :width]
    weights = x_ref[:, width:].astype(jnp.float32)
    lane = lax.broadcasted_iota(jnp.int32, weights.shape, 1)
    total = jnp.zeros(out_ref.shape, jnp.float32)
    for n in range(len(weight_refs) // 2):
        w_in_ref, w_out_ref = weight_refs[2 * n : 2 * n + 2]
        hidden_size = w_out_ref.shape[1]
        for j in range(w_in_ref.shape[0]):
            both = jnp.dot(x, w_in_ref[j], preferred_element_type=jnp.float32)
            gate, up = both[:, :hidden_size], both[:, hidden_size:]
            hidden = (gate / (1.0 + jnp.exp(-gate)) * up).astype(jnp.bfloat16)
            result = jnp.dot(hidden, w_out_ref[j], preferred_element_type=jnp.float32)
            result = result.astype(jnp.bfloat16).astype(jnp.float32)
            at = first_ref[n] + j
            mine = (lane == at) | (lane == at + half)
            weight = jnp.sum(jnp.where(mine, weights, 0.0), axis=1, keepdims=True)
            total = total + weight * result
    out_ref[...] = total.astype(out_ref.dtype)


def experts(x, first, weights):
    rows, columns = x.shape
    width = weights[0].shape[1]
    block = 256 if rows % 256 == 0 else rows
    return pl.pallas_call(
        expert_kernel,
        grid=(rows // block,),
        in_specs=[
            pl.BlockSpec(memory_space=pltpu.SMEM),
            pl.BlockSpec((block, columns), lambda i: (i, 0)),
        ]
        + [pl.BlockSpec(w.shape, lambda i: (0, 0, 0)) for w in weights],
        out_specs=pl.BlockSpec((block, width), lambda i: (i, 0)),
        out_shape=jax.ShapeDtypeStruct((rows, width), jnp.bfloat16),
        compiler_params=pltpu.CompilerParams(vmem_limit_bytes=40 * 1024 * 1024),
        cost_estimate=pl.CostEstimate(flops=0, bytes_accessed=0, transcendentals=0),
    )(first, x, *weights)


def plane_size(devices):
    size = 1
    while 4 * size * size <= devices:
        size *= 2
    return size


def swap(x, axis, groups=None):
    return lax.all_to_all(
        x, axis, split_axis=0, concat_axis=0, axis_index_groups=groups, tiled=True
    )


def flip(x, axis, bits):
    if bits == 0:
        return x
    return lax.ppermute(x, axis, [(d, d ^ bits) for d in range(lax.axis_size(axis))])


def add_up(blocks):
    return sum(x.astype(jnp.float32) for x in blocks).astype(jnp.bfloat16)


def weighted_rows(tokens, expert_ids, route_weights, old_plan):
    slot_count = old_plan.shape[0]
    slot_index = jnp.arange(slot_count, dtype=jnp.int32)
    share = route_weights / jnp.sum(route_weights, axis=1, keepdims=True)
    earlier = (old_plan[None, :] == old_plan[:, None]) & (slot_index[None, :] < slot_index[:, None])
    is_first = ~jnp.any(earlier, axis=1)
    chosen = (expert_ids[:, :, None] == old_plan[None, None, :]) & is_first[None, None, :]
    weight = jnp.sum(jnp.where(chosen, share[:, :, None], 0.0), axis=1)
    high = lax.reduce_precision(weight, exponent_bits=8, mantissa_bits=7)
    half = -(-2 * slot_count // LANE) * LANE // 2
    pad = jnp.zeros((tokens.shape[0], half - slot_count), jnp.bfloat16)
    return jnp.concatenate(
        [tokens, high.astype(jnp.bfloat16), pad, (weight - high).astype(jnp.bfloat16), pad], axis=1
    )


def crossing(old_plan, new_plan):
    slot_count = old_plan.shape[0]
    held = slot_count // 2
    slot_index = jnp.arange(slot_count, dtype=jnp.int32)
    same_expert = new_plan[:, None] == old_plan[None, :]
    source = jnp.min(jnp.where(same_expert, slot_index[None, :], slot_count), axis=1)
    apart = slot_index[:, None] // held != slot_index[None, :] // held
    cross = jnp.any((source[:, None] == slot_index[None, :]) & apart, axis=0)
    before = (~apart) & (slot_index[:, None] < slot_index[None, :])
    rank = jnp.sum((before & cross[:, None]).astype(jnp.int32), axis=0)
    number = jnp.max(jnp.where(cross, rank + 1, 0))
    return source, cross, rank, number


def exchange(x, devices):
    half = devices // 2
    return swap(x, "exp", [list(range(half)), list(range(half, devices))])


def places(plan, held, most):
    source, cross, rank = plan
    mine = lax.axis_index("exp") * 2 // lax.axis_size("exp")
    local = jnp.arange(held, dtype=jnp.int32)
    leaving = lax.dynamic_slice_in_dim(cross, mine * held, held)
    ranking = lax.dynamic_slice_in_dim(rank, mine * held, held)
    place = jnp.arange(most, dtype=jnp.int32)
    matches = leaving[None, :] & (ranking[None, :] == place[:, None])
    sent_index = jnp.sum(jnp.where(matches, local[None, :], 0), axis=1)
    wanted = lax.dynamic_slice_in_dim(source, mine * held, held)
    here = wanted // held == mine
    far = jnp.arange(source.shape[0], dtype=jnp.int32)[None, :] == wanted[:, None]
    far_rank = jnp.sum(jnp.where(far, rank[None, :], 0), axis=1)
    return sent_index, jnp.where(here, wanted - mine * held, held + far_rank)


def on_device(
    tokens, w_in, w_out, moments_in, moments_out, expert_ids, route_weights, old_plan, new_plan
):
    devices = lax.axis_size("exp")
    half = devices // 2
    slots = w_in.shape[0]
    held = half * slots
    chunk_a, chunk_b = (w_in, w_out, moments_out), (moments_in,)
    full_in = lax.all_gather(w_in, "grp", axis=1, tiled=True)
    full_out = lax.all_gather(w_out, "grp", axis=1, tiled=True)

    rows = weighted_rows(tokens, expert_ids, route_weights, old_plan)
    packed_a, rows = pack(chunk_a, half, after=rows)
    inner = plane_size(devices)
    outer = range(0, devices, inner)
    spread_a = exchange(packed_a, devices).reshape((held,) + packed_a.shape[2:])
    rows = jnp.concatenate([flip(rows, "exp", i) for i in outer], axis=0)

    *plan, number = crossing(old_plan, new_plan)
    most = -(-held * FIXED // 16)
    sent_index, index = places(plan, held, held)
    across = [(d, (d + half) % devices) for d in range(devices)]

    def cross_over(x):
        sent = jnp.take(x, sent_index[:most], axis=0, mode="clip")
        return sent, jnp.pad(x, [(0, held)] + [(0, 0)] * (x.ndim - 1))

    def picked(table, arrived):
        table = lax.dynamic_update_slice_in_dim(table, arrived, held, axis=0)
        out = jnp.take(table, index, axis=0, mode="clip")
        return out.reshape((half, slots) + out.shape[1:])

    packed_b, _ = pack(chunk_b, half)
    sent_a, table_a = cross_over(spread_a)
    sent_a, packed_b, rows = lax.optimization_barrier((sent_a, packed_b, rows))
    arrived_a = lax.ppermute(sent_a, "exp", across)
    spread_b = exchange(packed_b, devices).reshape((held,) + packed_b.shape[2:])
    sent_b, table_b = cross_over(spread_b)
    steps = range(0, inner, 2)
    blocks = [flip(rows, "exp", i) for i in steps]
    weights = [full_in, full_out, flip(full_in, "exp", 1), flip(full_out, "exp", 1)]
    me = lax.axis_index("exp").astype(jnp.int32)
    first = jnp.stack([me, me ^ 1]) * slots
    blocks[1:], sent_b, table_b, table_a = lax.optimization_barrier(
        (blocks[1:], sent_b, table_b, table_a)
    )
    parts = [experts(x, first, weights) for x in blocks]

    def more(state):
        place, *tables = state
        at = lax.dynamic_index_in_dim(sent_index, place, keepdims=False)
        out = []
        for spread, table in zip((spread_a, spread_b), tables):
            row = lax.dynamic_slice_in_dim(spread, at, 1, axis=0)
            row = lax.ppermute(row, "exp", across)
            out.append(lax.dynamic_update_slice_in_dim(table, row, held + place, axis=0))
        return place + 1, *out

    arrived_a, table_a, table_b, sent_b, parts = lax.optimization_barrier(
        (arrived_a, table_a, table_b, sent_b, parts)
    )
    _, table_a, table_b = lax.while_loop(
        lambda state: state[0] < number, more, (jnp.int32(most), table_a, table_b)
    )

    arrived_b = lax.ppermute(sent_b, "exp", across)
    landed_a = exchange(picked(table_a, arrived_a), devices)
    partial = add_up([flip(x, "exp", i) for i, x in zip(steps, parts)])
    arrived_b, partial = lax.optimization_barrier((arrived_b, partial))

    (new_moments_in,) = unpack(exchange(picked(table_b, arrived_b), devices), chunk_b)
    new_w_in, new_w_out, new_moments_out = unpack(landed_a, chunk_a)
    size = tokens.shape[0]
    mixed = add_up([flip(partial[n * size : (n + 1) * size], "exp", i) for n, i in enumerate(outer)])
    return mixed, new_w_in, new_w_out, new_moments_in, new_moments_out


def solution(mesh):
    return jax.shard_map(
        on_device,
        mesh=mesh,
        in_specs=(
            P(("grp", "exp"), None),
            P("exp", "grp", None),
            P("exp", "grp", None),
            P("exp", None, "grp", None),
            P("exp", None, "grp", None),
            P(("grp", "exp"), None),
            P(("grp", "exp"), None),
            P(),
            P(),
        ),
        out_specs=(
            P(("grp", "exp"), None),
            P("exp", "grp", None),
            P("exp", "grp", None),
            P("exp", None, "grp", None),
            P("exp", None, "grp", None),
        ),
        check_vma=False,
    )
```

profile of v0, /device:TPU:0, one launch (start us, length us, event | category | flops | bytes accessed | tf_op | source)
XLA Modules:
  0.0 380.6 jit_solution(5307584482256235012)
XLA Ops:
  8.6 0.9 fusion.1
  9.5 0.8 select_reduce_fusion
  10.5 3.6 pad_maximum_fusion
  14.3 4.3 %copy.41 = bf16[8,2,120,8,128]{4,3,2,1,0:T(8,128)(2,1)} copy(bf16[8,2,120,8,128]{4,3,2,0,1:T(8,128)(2,1)} %bitcast.61) | data formatting | bytes 7864320 | tf_op jit(solution)/shard_map/transpose | solution.py:34
  18.5 5.4 %all-to-all-start = ((bf16[8,2,120,8,128]{4,3,2,1,0:T(8,128)(2,1)}), bf16[8,2,120,8,128]{4,3,2,1,0:T(8,128)(2,1)}, u32[]{:S(2)}, u32[]{:S(2)}) async-start(bf16[8,2,120,8,128]{4,3,2,1,0:T(8,128)(2,1)} %copy.41), calls=%async_computation | async-start | bytes 7864320 | tf_op jit(solution)/shard_map/all_to_all | solution.py:99
  23.9 4.7 %collective-permute-start.4 = (bf16[128,1152]{1,0:T(8,128)(2,1)S(1)}, bf16[128,1152]{1,0:T(8,128)(2,1)}, u32[]{:S(2)}, u32[]{:S(2)}) collective-permute-start(bf16[128,1152]{1,0:T(8,128)(2,1)S(1)} %concatenate.10), channel_id=1, source_target_pairs={{0,12},{1,13},{2,14},{3,15},{4,8},{5,9},{6,10},{7,11},{8,4},{9,5},... | collective-permute-start | bytes 884744 | tf_op jit(solution)/shard_map/ppermute | solution.py:107
  30.0 48.9 %collective-permute-done.4 = bf16[128,1152]{1,0:T(8,128)(2,1)} collective-permute-done((bf16[128,1152]{1,0:T(8,128)(2,1)S(1)}, bf16[128,1152]{1,0:T(8,128)(2,1)}, u32[]{:S(2)}, u32[]{:S(2)}) %collective-permute-start.4) | collective-permute-done | bytes 294944 | tf_op jit(solution)/shard_map/ppermute | solution.py:107
  78.9 1.1 collective-permute-done.3
  80.0 8.4 %collective-permute-done.2 = bf16[128,1152]{1,0:T(8,128)(2,1)} collective-permute-done((bf16[128,1152]{1,0:T(8,128)(2,1)S(1)}, bf16[128,1152]{1,0:T(8,128)(2,1)}, u32[]{:S(2)}, u32[]{:S(2)}) %collective-permute-start.2) | collective-permute-done | bytes 294944 | tf_op jit(solution)/shard_map/ppermute | solution.py:107
  88.4 2.2 pad_maximum_fusion.1.x_ref
  90.6 4.5 %gather_fusion = bf16[9,120,8,128]{3,2,1,0:T(8,128)(2,1)} fusion(bf16[16,120,8,128]{3,2,1,0:T(8,128)(2,1)} %bitcast.12, s32[1024]{0:T(1024)S(1)} %pad_clamp_fusion.1), kind=kCustom, calls=%fused_computation | custom fusion | bytes 4423716 | tf_op jit(solution)/shard_map/jit(_take)/gather | solution.py:189
  95.1 1.9 copy.42
  96.9 4.4 %all-to-all-start.1 = ((bf16[8,2,96,8,128]{4,3,2,1,0:T(8,128)(2,1)}), bf16[8,2,96,8,128]{4,3,2,1,0:T(8,128)(2,1)}, u32[]{:S(2)}, u32[]{:S(2)}) async-start(bf16[8,2,96,8,128]{4,3,2,1,0:T(8,128)(2,1)} %copy.42), calls=%async_computation.1 | async-start | bytes 6291456 | tf_op jit(solution)/shard_map/all_to_all | solution.py:99
  102.6 3.2 collective-permute-start.5
  105.8 27.4 %all-gather.5.cloned.1.call-done.refs_1_ = bf16[2,384,1024]{2,1,0:T(8,128)(2,1)} async-done(((bf16[2,192,1024]{2,1,0:T(8,128)(2,1)}), bf16[2,384,1024]{2,1,0:T(8,128)(2,1)}) %all-gather.5.cloned.1.call-update) | async-done | bytes 1572880 | tf_op jit(solution)/shard_map/all_gather | solution.py:174
  133.2 1.5 collective-permute-start.6
  135.7 6.5 %pad.9 = bf16[32,120,8,128]{3,2,1,0:T(8,128)(2,1)} pad(bf16[16,120,8,128]{3,2,1,0:T(8,128)(2,1)} %bitcast.12, bf16[]{:T(256)} %constant.87.clone.1), padding=0_16x0_0x0_0x0_0 | pad | bytes 11796482 | tf_op jit(solution)/shard_map/jit(_pad)/pad | solution.py:190
  142.2 9.7 %shard_map.128 = bf16[512,1024]{1,0:T(8,128)(2,1)S(1)} custom-call(s32[2]{0:T(128)S(1)} %add_multiply_fusion.first_ref, bf16[512,1152]{1,0:T(8,128)(2,1)} %pad_maximum_fusion.1.x_ref, bf16[2,1024,768]{2,1,0:T(8,128)(2,1)S(1)} %copy-done, bf16[2,384,1024]{2,1,0:T(8,128)(2,1)S(1)} %copy-done.1, bf16[2,1024,768]{2,1,0:T(8,128)(2,1)} %collective-permute-done.7.refs_2_, ...), custom_call_target="tpu_custom_call" | custom-call | tf_op jit(solution)/shard_map/pallas_call | solution.py:76
  152.0 1.0 copy-done.3
  152.9 19.3 %all-to-all-done.1 = bf16[8,2,96,8,128]{4,3,2,1,0:T(8,128)(2,1)} async-done(((bf16[8,2,96,8,128]{4,3,2,1,0:T(8,128)(2,1)}), bf16[8,2,96,8,128]{4,3,2,1,0:T(8,128)(2,1)}, u32[]{:S(2)}, u32[]{:S(2)}) %all-to-all-start.1) | async-done | bytes 3145760 | tf_op jit(solution)/shard_map/all_to_all | solution.py:99
  172.3 4.0 %gather_fusion.1 = bf16[9,96,8,128]{3,2,1,0:T(8,128)(2,1)} fusion(bf16[16,96,8,128]{3,2,1,0:T(8,128)(2,1)} %bitcast.17, s32[1024]{0:T(1024)S(1)} %pad_clamp_fusion.1), kind=kCustom, calls=%fused_computation.1 | custom fusion | bytes 3538980 | tf_op jit(solution)/shard_map/jit(_take)/gather | solution.py:189
  176.3 5.6 %pad.8 = bf16[32,96,8,128]{3,2,1,0:T(8,128)(2,1)} pad(bf16[16,96,8,128]{3,2,1,0:T(8,128)(2,1)} %bitcast.17, bf16[]{:T(256)} %constant.87.clone.1), padding=0_16x0_0x0_0x0_0 | pad | bytes 9437186 | tf_op jit(solution)/shard_map/jit(_pad)/pad | solution.py:190
  181.9 9.7 %shard_map.129 = bf16[512,1024]{1,0:T(8,128)(2,1)S(1)} custom-call(s32[2]{0:T(128)S(1)} %add_multiply_fusion.first_ref, bf16[512,1152]{1,0:T(8,128)(2,1)} %collective-permute-done.6.x_ref, bf16[2,1024,768]{2,1,0:T(8,128)(2,1)S(1)} %copy-done, bf16[2,384,1024]{2,1,0:T(8,128)(2,1)S(1)} %copy-done.2, bf16[2,1024,768]{2,1,0:T(8,128)(2,1)} %collective-permute-done.7.refs_2_, ...), custom_call_target="tpu_custom_call" | custom-call | tf_op jit(solution)/shard_map/pallas_call | solution.py:76
  191.7 1.0 copy-done.5
  192.6 9.3 %collective-permute-done.5 = bf16[9,120,8,128]{3,2,1,0:T(8,128)(2,1)} collective-permute-done((bf16[9,120,8,128]{3,2,1,0:T(8,128)(2,1)}, bf16[9,120,8,128]{3,2,1,0:T(8,128)(2,1)}, u32[]{:S(2)}, u32[]{:S(2)}) %collective-permute-start.5) | collective-permute-done | bytes 2211872 | tf_op jit(solution)/shard_map/ppermute | solution.py:200
  202.6 3.1 constant_dynamic-update-slice_fusion.3
  205.7 6.2 %gather_fusion.2 = bf16[16,120,8,128]{3,2,1,0:T(8,128)(2,1)} fusion(bf16[32,120,8,128]{3,2,1,0:T(8,128)(2,1)} %constant_dynamic-update-slice_fusion.3, s32[1024]{0:T(1024)S(1)} %pad_clamp_fusion), kind=kCustom, calls=%fused_computation.2 | custom fusion | bytes 7864384 | tf_op jit(solution)/shard_map/jit(_take)/gather | solution.py:194
  211.9 4.8 %all-to-all-start.2 = ((bf16[8,2,120,8,128]{4,3,2,1,0:T(8,128)(2,1)}), bf16[8,2,120,8,128]{4,3,2,1,0:T(8,128)(2,1)}, u32[]{:S(2)}, u32[]{:S(2)}) async-start(bf16[8,2,120,8,128]{4,3,2,1,0:T(8,128)(2,1)} %bitcast.60), calls=%async_computation.2 | async-start | bytes 7864320 | tf_op jit(solution)/shard_map/all_to_all | solution.py:99
  216.7 2.0 collective-permute-start.9
  218.8 2.0 collective-permute-start.10
  220.8 46.8 %collective-permute-done.10 = bf16[512,1024]{1,0:T(8,128)(2,1)S(1)} collective-permute-done((bf16[512,1024]{1,0:T(8,128)(2,1)S(1)}, bf16[512,1024]{1,0:T(8,128)(2,1)S(1)}, u32[]{:S(2)}, u32[]{:S(2)}) %collective-permute-start.10) | collective-permute-done | bytes 1048608 | tf_op jit(solution)/shard_map/ppermute | solution.py:107
  267.6 1.4 add_convert_fusion
  269.0 28.9 %collective-permute-done.9 = bf16[9,96,8,128]{3,2,1,0:T(8,128)(2,1)S(1)} collective-permute-done((bf16[9,96,8,128]{3,2,1,0:T(8,128)(2,1)}, bf16[9,96,8,128]{3,2,1,0:T(8,128)(2,1)S(1)}, u32[]{:S(2)}, u32[]{:S(2)}) %collective-permute-start.9) | collective-permute-done | bytes 1769504 | tf_op jit(solution)/shard_map/ppermute | solution.py:230
  297.9 1.4 constant_dynamic-update-slice_fusion.2
  299.3 5.4 %gather_fusion.3 = bf16[16,96,8,128]{3,2,1,0:T(8,128)(2,1)} fusion(bf16[32,96,8,128]{3,2,1,0:T(8,128)(2,1)} %constant_dynamic-update-slice_fusion.2, s32[1024]{0:T(1024)S(1)} %pad_clamp_fusion), kind=kCustom, calls=%fused_computation.3 | custom fusion | bytes 6291520 | tf_op jit(solution)/shard_map/jit(_take)/gather | solution.py:194
  304.7 6.3 %all-to-all-start.3 = ((bf16[8,2,96,8,128]{4,3,2,1,0:T(8,128)(2,1)}), bf16[8,2,96,8,128]{4,3,2,1,0:T(8,128)(2,1)S(1)}, u32[]{:S(2)}, u32[]{:S(2)}) async-start(bf16[8,2,96,8,128]{4,3,2,1,0:T(8,128)(2,1)} %bitcast.29), calls=%async_computation.3 | async-start | bytes 6291456 | tf_op jit(solution)/shard_map/all_to_all | solution.py:99
  311.0 1.2 fusion.7
  312.2 2.1 collective-permute-start.13
  314.2 1.5 collective-permute-start.12
  315.7 0.9 collective-permute-start.11
  316.6 37.4 %collective-permute-done.13 = bf16[128,1024]{1,0:T(8,128)(2,1)S(1)} collective-permute-done((bf16[128,1024]{1,0:T(8,128)(2,1)S(1)}, bf16[128,1024]{1,0:T(8,128)(2,1)S(1)}, u32[]{:S(2)}, u32[]{:S(2)}) %collective-permute-start.13) | collective-permute-done | bytes 262176 | tf_op jit(solution)/shard_map/ppermute | solution.py:107
  354.1 3.2 collective-permute-done.12
  357.3 7.6 %collective-permute-done.11 = bf16[128,1024]{1,0:T(8,128)(2,1)S(1)} collective-permute-done((bf16[128,1024]{1,0:T(8,128)(2,1)S(1)}, bf16[128,1024]{1,0:T(8,128)(2,1)S(1)}, u32[]{:S(2)}, u32[]{:S(2)}) %collective-permute-start.11) | collective-permute-done | bytes 262176 | tf_op jit(solution)/shard_map/ppermute | solution.py:107
  364.8 1.8 add_convert_fusion.1
  366.7 2.4 copy.43
  369.1 0.9 slice.42
  370.0 1.9 fusion.6
  371.9 1.9 copy.44
  (59 shorter events, 6.0 us)
Async XLA Ops:
  10.5 3.6 copy-start.8
  18.5 10.7 %copy-start.9 = (s32[32]{0:T(128)S(1)}, s32[32]{0:T(128)}, u32[]{:S(2)}) copy-start(s32[32]{0:T(128)} %param.18) | copy-start | bytes 388
  18.5 10.7 %copy-start.10 = (s32[32]{0:T(128)S(1)}, s32[32]{0:T(128)}, u32[]{:S(2)}) copy-start(s32[32]{0:T(128)} %param.19) | copy-start | bytes 388
  18.5 72.1 %all-to-all-start = ((bf16[8,2,120,8,128]{4,3,2,1,0:T(8,128)(2,1)}), bf16[8,2,120,8,128]{4,3,2,1,0:T(8,128)(2,1)}, u32[]{:S(2)}, u32[]{:S(2)}) async-start(bf16[8,2,120,8,128]{4,3,2,1,0:T(8,128)(2,1)} %copy.41), calls=%async_computation | async-start | bytes 7864320 | tf_op jit(solution)/shard_map/all_to_all | solution.py:99
  23.9 78.3 %all-gather.3.cloned.1.call-start = ((), (), s32[]{:S(2)}) async-start(), calls=%async_computation.4 | async-start | bytes 4718592 | tf_op jit(solution)/shard_map/all_gather | solution.py:173
  23.9 54.9 %collective-permute-start.4 = (bf16[128,1152]{1,0:T(8,128)(2,1)S(1)}, bf16[128,1152]{1,0:T(8,128)(2,1)}, u32[]{:S(2)}, u32[]{:S(2)}) collective-permute-start(bf16[128,1152]{1,0:T(8,128)(2,1)S(1)} %concatenate.10), channel_id=1, source_target_pairs={{0,12},{1,13},{2,14},{3,15},{4,8},{5,9},{6,10},{7,11},{8,4},{9,5},... | collective-permute-start | bytes 884744 | tf_op jit(solution)/shard_map/ppermute | solution.py:107
  28.6 51.4 %collective-permute-start.3 = (bf16[128,1152]{1,0:T(8,128)(2,1)S(1)}, bf16[128,1152]{1,0:T(8,128)(2,1)}, u32[]{:S(2)}, u32[]{:S(2)}) collective-permute-start(bf16[128,1152]{1,0:T(8,128)(2,1)S(1)} %concatenate.10), channel_id=1, source_target_pairs={{0,8},{1,9},{2,10},{3,11},{4,12},{5,13},{6,14},{7,15},{8,0},{9,1},... | collective-permute-start | bytes 884744 | tf_op jit(solution)/shard_map/ppermute | solution.py:107
  28.6 59.8 %collective-permute-start.2 = (bf16[128,1152]{1,0:T(8,128)(2,1)S(1)}, bf16[128,1152]{1,0:T(8,128)(2,1)}, u32[]{:S(2)}, u32[]{:S(2)}) collective-permute-start(bf16[128,1152]{1,0:T(8,128)(2,1)S(1)} %concatenate.10), channel_id=1, source_target_pairs={{0,4},{1,5},{2,6},{3,7},{4,0},{5,1},{6,2},{7,3},{8,12},{9,13},{10,... | collective-permute-start | bytes 884744 | tf_op jit(solution)/shard_map/ppermute | solution.py:107
  30.0 65.1 %copy-start.7 = (bf16[2,2,512,768]{3,2,1,0:T(8,128)(2,1)S(1)}, bf16[2,2,512,768]{3,2,1,0:T(8,128)(2,1)}, u32[]{:S(2)}) copy-start(bf16[2,2,512,768]{3,2,1,0:T(8,128)(2,1)} %param.14) | copy-start | bytes 9437188
  96.9 75.3 %all-to-all-start.1 = ((bf16[8,2,96,8,128]{4,3,2,1,0:T(8,128)(2,1)}), bf16[8,2,96,8,128]{4,3,2,1,0:T(8,128)(2,1)}, u32[]{:S(2)}, u32[]{:S(2)}) async-start(bf16[8,2,96,8,128]{4,3,2,1,0:T(8,128)(2,1)} %copy.42), calls=%async_computation.1 | async-start | bytes 6291456 | tf_op jit(solution)/shard_map/all_to_all | solution.py:99
  101.4 31.8 %all-gather.5.cloned.1.call-start = ((), (), s32[]{:S(2)}) async-start(), calls=%async_computation.5 | async-start | bytes 2359296 | tf_op jit(solution)/shard_map/all_gather | solution.py:174
  102.2 40.0 %collective-permute-start.7 = (bf16[2,1024,768]{2,1,0:T(8,128)(2,1)}, bf16[2,1024,768]{2,1,0:T(8,128)(2,1)}, u32[]{:S(2)}, u32[]{:S(2)}) collective-permute-start(bf16[2,1024,768]{2,1,0:T(8,128)(2,1)} %all-gather.3.cloned.1.call-done.refs_0_), channel_id=1, source_target_pairs={{0,1},{1,0},{2,3},{3,2},{4,5},{5,4},{6,7},{7,6},{8,9},{9,8},{10,11... | collective-permute-start | bytes 9437192 | tf_op jit(solution)/shard_map/ppermute | solution.py:107
  102.6 99.3 %collective-permute-start.5 = (bf16[9,120,8,128]{3,2,1,0:T(8,128)(2,1)}, bf16[9,120,8,128]{3,2,1,0:T(8,128)(2,1)}, u32[]{:S(2)}, u32[]{:S(2)}) collective-permute-start(bf16[9,120,8,128]{3,2,1,0:T(8,128)(2,1)} %gather_fusion), channel_id=1, source_target_pairs={{0,8},{1,9},{2,10},{3,11},{4,12},{5,13},{6,14},{7,15},{8,0},{9,1},... | collective-permute-start | bytes 6635528 | tf_op jit(solution)/shard_map/ppermute | solution.py:200
  133.2 9.0 %collective-permute-start.8 = (bf16[2,384,1024]{2,1,0:T(8,128)(2,1)}, bf16[2,384,1024]{2,1,0:T(8,128)(2,1)}, u32[]{:S(2)}, u32[]{:S(2)}) collective-permute-start(bf16[2,384,1024]{2,1,0:T(8,128)(2,1)} %all-gather.5.cloned.1.call-done.refs_1_), channel_id=1, source_target_pairs={{0,1},{1,0},{2,3},{3,2},{4,5},{5,4},{6,7},{7,6},{8,9},{9,8},{10,11... | collective-permute-start | bytes 4718600 | tf_op jit(solution)/shard_map/ppermute | solution.py:107
  133.2 48.7 %collective-permute-start.6 = (bf16[512,1152]{1,0:T(8,128)(2,1)}, bf16[512,1152]{1,0:T(8,128)(2,1)}, u32[]{:S(2)}, u32[]{:S(2)}) collective-permute-start(bf16[512,1152]{1,0:T(8,128)(2,1)} %pad_maximum_fusion.1.x_ref), channel_id=1, source_target_pairs={{0,2},{1,3},{2,0},{3,1},{4,6},{5,7},{6,4},{7,5},{8,10},{9,11},{10,... | collective-permute-start | bytes 3538952 | tf_op jit(solution)/shard_map/ppermute | solution.py:107
  135.7 6.5 %copy-start = (bf16[2,1024,768]{2,1,0:T(8,128)(2,1)S(1)}, bf16[2,1024,768]{2,1,0:T(8,128)(2,1)}, u32[]{:S(2)}) copy-start(bf16[2,1024,768]{2,1,0:T(8,128)(2,1)} %all-gather.3.cloned.1.call-done.refs_0_) | copy-start | bytes 9437188
  135.7 6.5 %copy-start.1 = (bf16[2,384,1024]{2,1,0:T(8,128)(2,1)S(1)}, bf16[2,384,1024]{2,1,0:T(8,128)(2,1)}, u32[]{:S(2)}) copy-start(bf16[2,384,1024]{2,1,0:T(8,128)(2,1)} %all-gather.5.cloned.1.call-done.refs_1_) | copy-start | bytes 4718596
  152.0 1.0 copy-start.3
  176.3 5.6 %copy-start.2 = (bf16[2,384,1024]{2,1,0:T(8,128)(2,1)S(1)}, bf16[2,384,1024]{2,1,0:T(8,128)(2,1)}, u32[]{:S(2)}) copy-start(bf16[2,384,1024]{2,1,0:T(8,128)(2,1)} %all-gather.5.cloned.1.call-done.refs_1_) | copy-start | bytes 4718596
  191.6 1.0 copy-start.5
  211.9 6.9 %copy-start.6 = (bf16[512,1024]{1,0:T(8,128)(2,1)S(1)}, bf16[512,1024]{1,0:T(8,128)(2,1)}, u32[]{:S(2)}) copy-start(bf16[512,1024]{1,0:T(8,128)(2,1)} %copy-done.5) | copy-start | bytes 3145732
  211.9 55.7 %copy-start.4 = (bf16[512,1024]{1,0:T(8,128)(2,1)S(1)}, bf16[512,1024]{1,0:T(8,128)(2,1)}, u32[]{:S(2)}) copy-start(bf16[512,1024]{1,0:T(8,128)(2,1)} %copy-done.3) | copy-start | bytes 3145732
  211.9 92.8 %all-to-all-start.2 = ((bf16[8,2,120,8,128]{4,3,2,1,0:T(8,128)(2,1)}), bf16[8,2,120,8,128]{4,3,2,1,0:T(8,128)(2,1)}, u32[]{:S(2)}, u32[]{:S(2)}) async-start(bf16[8,2,120,8,128]{4,3,2,1,0:T(8,128)(2,1)} %bitcast.60), calls=%async_computation.2 | async-start | bytes 7864320 | tf_op jit(solution)/shard_map/all_to_all | solution.py:99
  216.7 81.2 %collective-permute-start.9 = (bf16[9,96,8,128]{3,2,1,0:T(8,128)(2,1)}, bf16[9,96,8,128]{3,2,1,0:T(8,128)(2,1)S(1)}, u32[]{:S(2)}, u32[]{:S(2)}) collective-permute-start(bf16[9,96,8,128]{3,2,1,0:T(8,128)(2,1)} %gather_fusion.1), channel_id=1, source_target_pairs={{0,8},{1,9},{2,10},{3,11},{4,12},{5,13},{6,14},{7,15},{8,0},{9,1},... | collective-permute-start | bytes 5308424 | tf_op jit(solution)/shard_map/ppermute | solution.py:230
  218.8 48.8 %collective-permute-start.10 = (bf16[512,1024]{1,0:T(8,128)(2,1)S(1)}, bf16[512,1024]{1,0:T(8,128)(2,1)S(1)}, u32[]{:S(2)}, u32[]{:S(2)}) collective-permute-start(bf16[512,1024]{1,0:T(8,128)(2,1)S(1)} %copy-done.6), channel_id=1, source_target_pairs={{0,2},{1,3},{2,0},{3,1},{4,6},{5,7},{6,4},{7,5},{8,10},{9,11},{10,... | collective-permute-start | bytes 3145736 | tf_op jit(solution)/shard_map/ppermute | solution.py:107
  304.7 67.1 %all-to-all-start.3 = ((bf16[8,2,96,8,128]{4,3,2,1,0:T(8,128)(2,1)}), bf16[8,2,96,8,128]{4,3,2,1,0:T(8,128)(2,1)S(1)}, u32[]{:S(2)}, u32[]{:S(2)}) async-start(bf16[8,2,96,8,128]{4,3,2,1,0:T(8,128)(2,1)} %bitcast.29), calls=%async_computation.3 | async-start | bytes 6291456 | tf_op jit(solution)/shard_map/all_to_all | solution.py:99
  312.2 41.9 %collective-permute-start.13 = (bf16[128,1024]{1,0:T(8,128)(2,1)S(1)}, bf16[128,1024]{1,0:T(8,128)(2,1)S(1)}, u32[]{:S(2)}, u32[]{:S(2)}) collective-permute-start(bf16[128,1024]{1,0:T(8,128)(2,1)S(1)} %get-tuple-element.151), channel_id=1, source_target_pairs={{0,12},{1,13},{2,14},{3,15},{4,8},{5,9},{6,10},{7,11},{8,4},{9,5},... | collective-permute-start | bytes 786440 | tf_op jit(solution)/shard_map/ppermute | solution.py:107
  314.2 43.0 %collective-permute-start.12 = (bf16[128,1024]{1,0:T(8,128)(2,1)S(1)}, bf16[128,1024]{1,0:T(8,128)(2,1)S(1)}, u32[]{:S(2)}, u32[]{:S(2)}) collective-permute-start(bf16[128,1024]{1,0:T(8,128)(2,1)S(1)} %get-tuple-element.152), channel_id=1, source_target_pairs={{0,8},{1,9},{2,10},{3,11},{4,12},{5,13},{6,14},{7,15},{8,0},{9,1},... | collective-permute-start | bytes 786440 | tf_op jit(solution)/shard_map/ppermute | solution.py:107
  315.7 49.1 %collective-permute-start.11 = (bf16[128,1024]{1,0:T(8,128)(2,1)S(1)}, bf16[128,1024]{1,0:T(8,128)(2,1)S(1)}, u32[]{:S(2)}, u32[]{:S(2)}) collective-permute-start(bf16[128,1024]{1,0:T(8,128)(2,1)S(1)} %get-tuple-element.150), channel_id=1, source_target_pairs={{0,4},{1,5},{2,6},{3,7},{4,0},{5,1},{6,2},{7,3},{8,12},{9,13},{10,... | collective-permute-start | bytes 786440 | tf_op jit(solution)/shard_map/ppermute | solution.py:107
Sparse Core Ops, SparseCore 0:
  29.4 46.3 all-gather.2
  103.8 29.3 all-gather.4
where the time goes:
time: 381 us
  waiting for transfers between devices  239 us (63%)
  local copies, waits for them, and re-layouts  53.5 us (14%)
  starting transfers between devices  39.9 us (10%)
  Pallas kernels  19.4 us (5%)
  between operations  14.3 us (4%)
  other arithmetic  13.7 us (4%)
    ppermute x10, waiting for transfers between devices, flip(): lax.ppermute(x, axis, [(d, d ^ bits) for d in range(lax.axis_size(axis))])  153 us
    ppermute x1, waiting for transfers between devices, on_device(): arrived_b = lax.ppermute(sent_b, 'exp', across)  28.9 us
    all_gather x1, waiting for transfers between devices, on_device(): full_out = lax.all_gather(w_out, 'grp', axis=1, tiled=True)  27.4 us
    all_to_all x4, starting transfers between devices, swap(): lax.all_to_all(x, axis, split_axis=0, concat_axis=0, axis_index_groups=gr...  20.9 us
    pallas_call x2, Pallas kernels, experts(): pl.pallas_call(expert_kernel, grid=(rows // block,), in_specs=[pl.BlockSp...  19.4 us
    all_to_all x4, waiting for transfers between devices, swap(): lax.all_to_all(x, axis, split_axis=0, concat_axis=0, axis_index_groups=gr...  19.4 us
    ppermute x10, starting transfers between devices, flip(): lax.ppermute(x, axis, [(d, d ^ bits) for d in range(lax.axis_size(axis))])  13.7 us
    pad x2, local copies, waits for them, and re-layouts, cross_over(): return (sent, jnp.pad(x, [(0, held)] + [(0, 0)] * (x.ndim - 1)))  12.1 us
  transfers between devices with their start and end apart: 18, of which 11 were waited for; matrix products, arithmetic and copies ran while one was open for 11% of the time, Pallas kernels for 5%

commit v1 on v0

--- a/solution.py
+++ b/solution.py
@@ -22,27 +22,75 @@
     return x.swapaxes(2, 3).reshape(shape)
 
 
-def pack(arrays, parts, after=None):
+def in_parts(tiles, parts):
+    return tiles.reshape(tiles.shape[0], parts, -1, SUB, LANE).swapaxes(0, 1)
+
+
+def pack(arrays, parts):
     tiles = [to_tiles(a) for a in arrays]
+    if all(t.shape[1] % parts == 0 for t in tiles):
+        return jnp.concatenate([in_parts(t, parts) for t in tiles], axis=2)
     slots = tiles[0].shape[0]
     extra = -sum(t.shape[1] for t in tiles) % parts
-    if extra:
-        tiles.append(jnp.zeros((slots, extra, SUB, LANE), tiles[0].dtype))
-    packed = jnp.concatenate(tiles, axis=1) if len(tiles) > 1 else tiles[0]
-    if after is not None:
-        packed, after = lax.optimization_barrier((packed, after))
-    return packed.reshape(slots, parts, -1, SUB, LANE).swapaxes(0, 1), after
+    tiles.append(jnp.zeros((slots, extra, SUB, LANE), tiles[0].dtype))
+    return in_parts(jnp.concatenate(tiles, axis=1), parts)
 
 
 def unpack(landed, arrays):
-    slots = landed.shape[1]
-    landed = landed.swapaxes(0, 1).reshape(slots, -1, SUB, LANE)
+    parts, slots = landed.shape[:2]
+    counts = [a.size // (slots * SUB * LANE) for a in arrays]
+    whole = all(count % parts == 0 for count in counts)
+    if not whole:
+        landed = landed.swapaxes(0, 1).reshape(slots, -1, SUB, LANE)
     outs, at = [], 0
-    for a in arrays:
-        count = a.size // (slots * SUB * LANE)
-        outs.append(from_tiles(landed[:, at : at + count], a.shape))
+    for a, count in zip(arrays, counts):
+        if whole:
+            part = landed[:, :, at // parts : (at + count) // parts].swapaxes(0, 1)
+            outs.append(from_tiles(part.reshape(slots, count, SUB, LANE), a.shape))
+        else:
+            outs.append(from_tiles(landed[:, at : at + count], a.shape))
         at += count
     return outs
+
+
+def pick_kernel(index_ref, *refs):
+    *tables, out_ref, rows, in_sems, out_sems = refs
+    count = out_ref.shape[0]
+    for d in range(count):
+        i = index_ref[d]
+        low = 0
+        for table in tables:
+            size = table.shape[0]
+
+            @pl.when((i >= low) & (i < low + size))
+            def _(table=table, low=low):
+                pltpu.make_async_copy(table.at[i - low], rows.at[d], in_sems.at[d]).start()
+
+            low += size
+    for d in range(count):
+        pltpu.make_async_copy(tables[0].at[0], rows.at[d], in_sems.at[d]).wait()
+        pltpu.make_async_copy(rows.at[d], out_ref.at[d], out_sems.at[d]).start()
+    for d in range(count):
+        pltpu.make_async_copy(rows.at[d], out_ref.at[d], out_sems.at[d]).wait()
+
+
+def pick(index, *tables):
+    count = index.shape[0]
+    shape = (count,) + tables[0].shape[1:]
+    return pl.pallas_call(
+        pick_kernel,
+        in_specs=[pl.BlockSpec(memory_space=pltpu.SMEM)]
+        + [pl.BlockSpec(memory_space=pl.ANY)] * len(tables),
+        out_specs=pl.BlockSpec(memory_space=pl.ANY),
+        out_shape=jax.ShapeDtypeStruct(shape, tables[0].dtype),
+        scratch_shapes=[
+            pltpu.VMEM(shape, tables[0].dtype),
+            pltpu.SemaphoreType.DMA((count,)),
+            pltpu.SemaphoreType.DMA((count,)),
+        ],
+        compiler_params=pltpu.CompilerParams(vmem_limit_bytes=16 * 1024 * 1024),
+        cost_estimate=pl.CostEstimate(flops=0, bytes_accessed=0, transcendentals=0),
+    )(index, *tables)
 
 
 def expert_kernel(first_ref, x_ref, *refs):
@@ -174,65 +222,59 @@
     full_out = lax.all_gather(w_out, "grp", axis=1, tiled=True)
 
     rows = weighted_rows(tokens, expert_ids, route_weights, old_plan)
-    packed_a, rows = pack(chunk_a, half, after=rows)
+    rows, *firsts = lax.optimization_barrier((rows, *chunk_a))
     inner = plane_size(devices)
     outer = range(0, devices, inner)
+    column = [flip(rows, "exp", i) for i in outer]
+    packed_a = pack(firsts, half)
     spread_a = exchange(packed_a, devices).reshape((held,) + packed_a.shape[2:])
-    rows = jnp.concatenate([flip(rows, "exp", i) for i in outer], axis=0)
 
     *plan, number = crossing(old_plan, new_plan)
     most = -(-held * FIXED // 16)
     sent_index, index = places(plan, held, held)
     across = [(d, (d + half) % devices) for d in range(devices)]
 
-    def cross_over(x):
-        sent = jnp.take(x, sent_index[:most], axis=0, mode="clip")
-        return sent, jnp.pad(x, [(0, held)] + [(0, 0)] * (x.ndim - 1))
-
-    def picked(table, arrived):
-        table = lax.dynamic_update_slice_in_dim(table, arrived, held, axis=0)
-        out = jnp.take(table, index, axis=0, mode="clip")
-        return out.reshape((half, slots) + out.shape[1:])
-
-    packed_b, _ = pack(chunk_b, half)
-    sent_a, table_a = cross_over(spread_a)
-    sent_a, packed_b, rows = lax.optimization_barrier((sent_a, packed_b, rows))
+    sent_a = pick(sent_index[:most], spread_a)
     arrived_a = lax.ppermute(sent_a, "exp", across)
+    packed_b = pack(chunk_b, half)
     spread_b = exchange(packed_b, devices).reshape((held,) + packed_b.shape[2:])
-    sent_b, table_b = cross_over(spread_b)
+    sent_b = pick(sent_index[:most], spread_b)
+    column, _ = lax.optimization_barrier((column, sent_a))
     steps = range(0, inner, 2)
+    rows = jnp.concatenate(column, axis=0)
     blocks = [flip(rows, "exp", i) for i in steps]
     weights = [full_in, full_out, flip(full_in, "exp", 1), flip(full_out, "exp", 1)]
     me = lax.axis_index("exp").astype(jnp.int32)
     first = jnp.stack([me, me ^ 1]) * slots
-    blocks[1:], sent_b, table_b, table_a = lax.optimization_barrier(
-        (blocks[1:], sent_b, table_b, table_a)
-    )
+    blocks[1:], sent_b = lax.optimization_barrier((blocks[1:], sent_b))
     parts = [experts(x, first, weights) for x in blocks]
 
     def more(state):
-        place, *tables = state
+        place, *extra = state
         at = lax.dynamic_index_in_dim(sent_index, place, keepdims=False)
         out = []
-        for spread, table in zip((spread_a, spread_b), tables):
+        for spread, table in zip((spread_a, spread_b), extra):
             row = lax.dynamic_slice_in_dim(spread, at, 1, axis=0)
             row = lax.ppermute(row, "exp", across)
-            out.append(lax.dynamic_update_slice_in_dim(table, row, held + place, axis=0))
+            out.append(lax.dynamic_update_slice_in_dim(table, row, place - most, axis=0))
         return place + 1, *out
 
-    arrived_a, table_a, table_b, sent_b, parts = lax.optimization_barrier(
-        (arrived_a, table_a, table_b, sent_b, parts)
+    arrived_a, sent_b, parts = lax.optimization_barrier((arrived_a, sent_b, parts))
+    extra = [
+        jnp.zeros((max(held - most, 1),) + x.shape[1:], x.dtype) for x in (spread_a, spread_b)
+    ]
+    _, *extra = lax.while_loop(
+        lambda state: state[0] < number, more, (jnp.int32(most), *extra)
     )
-    _, table_a, table_b = lax.while_loop(
-        lambda state: state[0] < number, more, (jnp.int32(most), table_a, table_b)
-    )
 
     arrived_b = lax.ppermute(sent_b, "exp", across)
-    landed_a = exchange(picked(table_a, arrived_a), devices)
+    picked_a = pick(index, spread_a, arrived_a, extra[0])
+    landed_a = exchange(picked_a.reshape(packed_a.shape), devices)
     partial = add_up([flip(x, "exp", i) for i, x in zip(steps, parts)])
     arrived_b, partial = lax.optimization_barrier((arrived_b, partial))
 
-    (new_moments_in,) = unpack(exchange(picked(table_b, arrived_b), devices), chunk_b)
+    picked_b = pick(index, spread_b, arrived_b, extra[1])
+    (new_moments_in,) = unpack(exchange(picked_b.reshape(packed_b.shape), devices), chunk_b)
     new_w_in, new_w_out, new_moments_out = unpack(landed_a, chunk_a)
     size = tokens.shape[0]
     mixed = add_up([flip(partial[n * size : (n + 1) * size], "exp", i) for n, i in enumerate(outer)])

time: 381 us -> 379 us (level)
  local copies, waits for them, and re-layouts: 53.5 us -> 27.8 us
  Pallas kernels: 19.4 us -> 36 us
  waiting for transfers between devices: 239 us -> 253 us
    all_gather x1, waiting for transfers between devices: 27.4 us -> 0.01 us  [on_device(): full_out = lax.all_gather(w_out, 'grp', axis=1, tiled=True)]
    ppermute x10, waiting for transfers between devices: 153 us -> 179 us  [flip(): lax.ppermute(x, axis, [(d, d ^ bits) for d in range(lax.axis_size(axis))])]
    all_to_all x4, waiting for transfers between devices: 19.4 us -> 42.8 us  [swap(): lax.all_to_all(x, axis, split_axis=0, concat_axis=0, axis_index_groups=gr...]
    gather x4 -> x0, local copies, waits for them, and re-layouts: 20 us -> none  [the longest x2 11.6 us: picked(): out = jnp.take(table, index, axis=0, mode='clip')]
    pallas_call x0 -> x4, Pallas kernels: none -> 18.6 us  [pick(): pl.pallas_call(pick_kernel, in_specs=[pl.BlockSpec(memory_space=pltpu.SME...]
    pad x2 -> x0, local copies, waits for them, and re-layouts: 12.1 us -> none  [cross_over(): return (sent, jnp.pad(x, [(0, held)] + [(0, 0)] * (x.ndim - 1)))]
    unnamed x22 -> x30, local copies, waits for them, and re-layouts: 1.97 us -> 12.7 us
    ppermute x1, waiting for transfers between devices: 9.34 us -> 1.1 us  [on_device(): arrived_a = lax.ppermute(sent_a, 'exp', across)]
  transfers between devices with their start and end apart: 18 -> 18, of which waited for: 11 -> 8; matrix products, arithmetic and copies ran while one was open for 11% -> 5% of each run, Pallas kernels for 5% -> 8%
where the time goes in v1:
time: 379 us; the launch traced here: 378 us
  waiting for transfers between devices  253 us (67%)
  starting transfers between devices  36.1 us (10%)
  Pallas kernels  36 us (9%)
  local copies, waits for them, and re-layouts  27.8 us (7%)
  between operations  14.3 us (4%)
  other arithmetic  10.1 us (3%)
    ppermute x10, waiting for transfers between devices, flip(): lax.ppermute(x, axis, [(d, d ^ bits) for d in range(lax.axis_size(axis))])  179 us
    all_to_all x4, waiting for transfers between devices, swap(): lax.all_to_all(x, axis, split_axis=0, concat_axis=0, axis_index_groups=gr...  42.8 us
    ppermute x1, waiting for transfers between devices, on_device(): arrived_b = lax.ppermute(sent_b, 'exp', across)  28.8 us
    all_to_all x4, starting transfers between devices, swap(): lax.all_to_all(x, axis, split_axis=0, concat_axis=0, axis_index_groups=gr...  20 us
    pallas_call x4, Pallas kernels, pick(): pl.pallas_call(pick_kernel, in_specs=[pl.BlockSpec(memory_space=pltpu.SME...  18.6 us
    pallas_call x2, Pallas kernels, experts(): pl.pallas_call(expert_kernel, grid=(rows // block,), in_specs=[pl.BlockSp...  17.4 us
    ppermute x10, starting transfers between devices, flip(): lax.ppermute(x, axis, [(d, d ^ bits) for d in range(lax.axis_size(axis))])  13.4 us
    unnamed x30, local copies, waits for them, and re-layouts  12.7 us
  transfers between devices with their start and end apart: 18, of which 8 were waited for; matrix products, arithmetic and copies ran while one was open for 5% of the time, Pallas kernels for 8%

profile of v1, /device:TPU:0, one launch (start us, length us, event | category | flops | bytes accessed | tf_op | source)
XLA Modules:
  0.0 378.4 jit_solution(9998455682421446912)
XLA Ops:
  8.6 0.9 fusion.4
  10.5 1.1 concatenate.9
  11.6 2.3 pad_maximum_fusion
  13.9 2.1 copy.41
  16.1 5.5 %all-to-all-start = ((bf16[8,2,120,8,128]{4,3,2,1,0:T(8,128)(2,1)}), bf16[8,2,120,8,128]{4,3,2,1,0:T(8,128)(2,1)}, u32[]{:S(2)}, u32[]{:S(2)}) async-start(bf16[8,2,120,8,128]{4,3,2,1,0:T(8,128)(2,1)} %copy.41), calls=%async_computation | async-start | bytes 7864320 | tf_op jit(solution)/shard_map/all_to_all | solution.py:147
  22.3 1.9 copy.42
  24.2 42.8 %all-to-all-done = bf16[8,2,120,8,128]{4,3,2,1,0:T(8,128)(2,1)} async-done(((bf16[8,2,120,8,128]{4,3,2,1,0:T(8,128)(2,1)}), bf16[8,2,120,8,128]{4,3,2,1,0:T(8,128)(2,1)}, u32[]{:S(2)}, u32[]{:S(2)}) %all-to-all-start) | async-done | bytes 3932192 | tf_op jit(solution)/shard_map/all_to_all | solution.py:147
  67.0 4.5 %all-to-all-start.1 = ((bf16[8,2,96,8,128]{4,3,2,1,0:T(8,128)(2,1)}), bf16[8,2,96,8,128]{4,3,2,1,0:T(8,128)(2,1)}, u32[]{:S(2)}, u32[]{:S(2)}) async-start(bf16[8,2,96,8,128]{4,3,2,1,0:T(8,128)(2,1)} %copy.42), calls=%async_computation.1 | async-start | bytes 6291456 | tf_op jit(solution)/shard_map/all_to_all | solution.py:147
  72.7 1.7 collective-permute-start.3
  74.4 3.2 collective-permute-start.4
  78.3 3.1 shard_map.128
  81.4 1.8 collective-permute-start.2
  83.3 70.3 %collective-permute-done.3 = bf16[128,1152]{1,0:T(8,128)(2,1)} collective-permute-done((bf16[128,1152]{1,0:T(8,128)(2,1)S(1)}, bf16[128,1152]{1,0:T(8,128)(2,1)}, u32[]{:S(2)}, u32[]{:S(2)}) %collective-permute-start.3) | collective-permute-done | bytes 294944 | tf_op jit(solution)/shard_map/ppermute | solution.py:155
  154.3 1.7 constant_dynamic-update-slice_fusion.4
  156.0 1.7 constant_dynamic-update-slice_fusion.3
  157.7 1.7 constant_dynamic-update-slice_fusion.2.x_ref
  159.4 1.5 collective-permute-start.6
  161.9 4.2 %shard_map.129 = bf16[9,96,8,128]{3,2,1,0:T(8,128)(2,1)S(1)} custom-call(s32[9]{0:T(128)S(1)} %bitcast.76, bf16[16,96,8,128]{3,2,1,0:T(8,128)(2,1)} %bitcast.18.refs_0_), custom_call_target="tpu_custom_call" | custom-call | tf_op jit(solution)/shard_map/pallas_call | solution.py:80
  166.1 1.2 copy-done.5
  167.3 8.7 %shard_map.130 = bf16[512,1024]{1,0:T(8,128)(2,1)S(1)} custom-call(s32[2]{0:T(128)S(1)} %add_multiply_fusion.first_ref, bf16[512,1152]{1,0:T(8,128)(2,1)} %constant_dynamic-update-slice_fusion.2.x_ref, bf16[2,1024,768]{2,1,0:T(8,128)(2,1)S(1)} %copy-done.1, bf16[2,384,1024]{2,1,0:T(8,128)(2,1)S(1)} %copy-done.2, ...), custom_call_target="tpu_custom_call" | custom-call | tf_op jit(solution)/shard_map/pallas_call | solution.py:124
  176.1 0.9 copy-done.3
  177.0 11.1 %collective-permute-done.6.x_ref = bf16[512,1152]{1,0:T(8,128)(2,1)} collective-permute-done((bf16[512,1152]{1,0:T(8,128)(2,1)}, bf16[512,1152]{1,0:T(8,128)(2,1)}, u32[]{:S(2)}, u32[]{:S(2)}) %collective-permute-start.6) | collective-permute-done | bytes 1179680 | tf_op jit(solution)/shard_map/ppermute | solution.py:155
  188.1 8.7 %shard_map.131 = bf16[512,1024]{1,0:T(8,128)(2,1)S(1)} custom-call(s32[2]{0:T(128)S(1)} %add_multiply_fusion.first_ref, bf16[512,1152]{1,0:T(8,128)(2,1)} %collective-permute-done.6.x_ref, bf16[2,1024,768]{2,1,0:T(8,128)(2,1)S(1)} %copy-done.1, bf16[2,384,1024]{2,1,0:T(8,128)(2,1)S(1)} %copy-done.2, ...), custom_call_target="tpu_custom_call" | custom-call | tf_op jit(solution)/shard_map/pallas_call | solution.py:124
  196.8 1.0 copy-done.7
  197.8 1.1 collective-permute-done.2.refs_1_
  199.1 1.3 broadcast_in_dim.104
  201.0 6.8 %shard_map.132 = bf16[16,120,8,128]{3,2,1,0:T(8,128)(2,1)S(1)} custom-call(s32[16]{0:T(128)S(1)} %compare_select_fusion.index_ref, bf16[16,120,8,128]{3,2,1,0:T(8,128)(2,1)} %bitcast.13.refs_0_, bf16[9,120,8,128]{3,2,1,0:T(8,128)(2,1)} %collective-permute-done.2.refs_1_, bf16[7,120,8,128]{3,2,1,0:T(8,128)(2,1)S(1)} %get-tuple-element.183.refs_2_), custom_call_target="tpu_custom_call" | custom-call | tf_op jit(solution)/shard_map/pallas_call | solution.py:80
  207.9 2.0 copy-done
  209.8 4.8 %all-to-all-start.2 = ((bf16[8,2,120,8,128]{4,3,2,1,0:T(8,128)(2,1)}), bf16[8,2,120,8,128]{4,3,2,1,0:T(8,128)(2,1)}, u32[]{:S(2)}, u32[]{:S(2)}) async-start(bf16[8,2,120,8,128]{4,3,2,1,0:T(8,128)(2,1)} %bitcast.66), calls=%async_computation.2 | async-start | bytes 7864320 | tf_op jit(solution)/shard_map/all_to_all | solution.py:147
  214.7 0.9 collective-permute-start.9
  215.6 2.0 collective-permute-start.10
  217.6 47.9 %collective-permute-done.10 = bf16[512,1024]{1,0:T(8,128)(2,1)S(1)} collective-permute-done((bf16[512,1024]{1,0:T(8,128)(2,1)}, bf16[512,1024]{1,0:T(8,128)(2,1)S(1)}, u32[]{:S(2)}, u32[]{:S(2)}) %collective-permute-start.10) | collective-permute-done | bytes 1048608 | tf_op jit(solution)/shard_map/ppermute | solution.py:155
  265.5 1.4 add_convert_fusion
  266.9 28.8 %collective-permute-done.9.refs_1_ = bf16[9,96,8,128]{3,2,1,0:T(8,128)(2,1)S(1)} collective-permute-done((bf16[9,96,8,128]{3,2,1,0:T(8,128)(2,1)S(1)}, bf16[9,96,8,128]{3,2,1,0:T(8,128)(2,1)S(1)}, u32[]{:S(2)}, u32[]{:S(2)}) %collective-permute-start.9) | collective-permute-done | bytes 1769504 | tf_op jit(solution)/shard_map/ppermute | solution.py:270
  295.7 4.5 %shard_map.133 = bf16[16,96,8,128]{3,2,1,0:T(8,128)(2,1)} custom-call(s32[16]{0:T(128)S(1)} %compare_select_fusion.index_ref, bf16[16,96,8,128]{3,2,1,0:T(8,128)(2,1)} %bitcast.18.refs_0_, bf16[9,96,8,128]{3,2,1,0:T(8,128)(2,1)S(1)} %collective-permute-done.9.refs_1_, bf16[7,96,8,128]{3,2,1,0:T(8,128)(2,1)S(1)} %copy-done.8), custom_call_target="tpu_custom_call" | custom-call | tf_op jit(solution)/shard_map/pallas_call | solution.py:80
  300.2 5.2 %all-to-all-start.3 = ((bf16[8,2,96,8,128]{4,3,2,1,0:T(8,128)(2,1)}), bf16[8,2,96,8,128]{4,3,2,1,0:T(8,128)(2,1)S(1)}, u32[]{:S(2)}, u32[]{:S(2)}) async-start(bf16[8,2,96,8,128]{4,3,2,1,0:T(8,128)(2,1)} %bitcast.30), calls=%async_computation.3 | async-start | bytes 6291456 | tf_op jit(solution)/shard_map/all_to_all | solution.py:147
  305.5 1.2 fusion.7
  306.6 2.1 collective-permute-start.11
  308.7 2.3 collective-permute-start.12
  311.1 42.5 %collective-permute-done.11 = bf16[128,1024]{1,0:T(8,128)(2,1)S(1)} collective-permute-done((bf16[128,1024]{1,0:T(8,128)(2,1)S(1)}, bf16[128,1024]{1,0:T(8,128)(2,1)S(1)}, u32[]{:S(2)}, u32[]{:S(2)}) %collective-permute-start.11) | collective-permute-done | bytes 262176 | tf_op jit(solution)/shard_map/ppermute | solution.py:155
  353.7 7.3 %collective-permute-done.13 = bf16[128,1024]{1,0:T(8,128)(2,1)S(1)} collective-permute-done((bf16[128,1024]{1,0:T(8,128)(2,1)S(1)}, bf16[128,1024]{1,0:T(8,128)(2,1)S(1)}, u32[]{:S(2)}, u32[]{:S(2)}) %collective-permute-start.13) | collective-permute-done | bytes 262176 | tf_op jit(solution)/shard_map/ppermute | solution.py:155
  360.9 1.8 add_convert_fusion.1
  362.8 2.2 fusion.6
  365.0 1.3 copy.47
  366.3 1.3 copy.49
  367.5 1.2 slice.34
  368.7 0.9 copy.48
  369.6 1.9 copy.45
  (62 shorter events, 7.9 us)
Async XLA Ops:
  16.1 6.2 %copy-start.9 = (bf16[2,2,512,768]{3,2,1,0:T(8,128)(2,1)S(1)}, bf16[2,2,512,768]{3,2,1,0:T(8,128)(2,1)}, u32[]{:S(2)}) copy-start(bf16[2,2,512,768]{3,2,1,0:T(8,128)(2,1)} %param.14) | copy-start | bytes 9437188
  16.1 51.0 %all-to-all-start = ((bf16[8,2,120,8,128]{4,3,2,1,0:T(8,128)(2,1)}), bf16[8,2,120,8,128]{4,3,2,1,0:T(8,128)(2,1)}, u32[]{:S(2)}, u32[]{:S(2)}) async-start(bf16[8,2,120,8,128]{4,3,2,1,0:T(8,128)(2,1)} %copy.41), calls=%async_computation | async-start | bytes 7864320 | tf_op jit(solution)/shard_map/all_to_all | solution.py:147
  21.5 50.7 %all-gather.3.cloned.1.call-start = ((), (), s32[]{:S(2)}) async-start(), calls=%async_computation.4 | async-start | bytes 4718592 | tf_op jit(solution)/shard_map/all_gather | solution.py:221
  24.2 53.5 %copy-start.10 = (s32[32]{0:T(128)S(1)}, s32[32]{0:T(128)}, u32[]{:S(2)}) copy-start(s32[32]{0:T(128)} %param.18) | copy-start | bytes 388
  24.2 53.5 %copy-start.11 = (s32[32]{0:T(128)S(1)}, s32[32]{0:T(128)}, u32[]{:S(2)}) copy-start(s32[32]{0:T(128)} %param.19) | copy-start | bytes 388
  67.0 94.9 %all-to-all-start.1 = ((bf16[8,2,96,8,128]{4,3,2,1,0:T(8,128)(2,1)}), bf16[8,2,96,8,128]{4,3,2,1,0:T(8,128)(2,1)}, u32[]{:S(2)}, u32[]{:S(2)}) async-start(bf16[8,2,96,8,128]{4,3,2,1,0:T(8,128)(2,1)} %copy.42), calls=%async_computation.1 | async-start | bytes 6291456 | tf_op jit(solution)/shard_map/all_to_all | solution.py:147
  71.5 82.1 %all-gather.5.cloned.1.call-start = ((), (), s32[]{:S(2)}) async-start(), calls=%async_computation.5 | async-start | bytes 2359296 | tf_op jit(solution)/shard_map/all_gather | solution.py:222
  72.3 95.1 %collective-permute-start.7 = (bf16[2,1024,768]{2,1,0:T(8,128)(2,1)}, bf16[2,1024,768]{2,1,0:T(8,128)(2,1)S(1)}, u32[]{:S(2)}, u32[]{:S(2)}) collective-permute-start(bf16[2,1024,768]{2,1,0:T(8,128)(2,1)} %all-gather.3.cloned.1.call-done.refs_0_), channel_id=1, source_target_pairs={{0,1},{1,0},{2,3},{3,2},{4,5},{5,4},{6,7},{7,6},{8,9},{9,8},{10,11... | collective-permute-start | bytes 9437192 | tf_op jit(solution)/shard_map/ppermute | solution.py:155
  72.7 80.9 %collective-permute-start.3 = (bf16[128,1152]{1,0:T(8,128)(2,1)S(1)}, bf16[128,1152]{1,0:T(8,128)(2,1)}, u32[]{:S(2)}, u32[]{:S(2)}) collective-permute-start(bf16[128,1152]{1,0:T(8,128)(2,1)S(1)} %concatenate.9), channel_id=1, source_target_pairs={{0,4},{1,5},{2,6},{3,7},{4,0},{5,1},{6,2},{7,3},{8,12},{9,13},{10,... | collective-permute-start | bytes 884744 | tf_op jit(solution)/shard_map/ppermute | solution.py:155
  74.4 79.2 %collective-permute-start.4 = (bf16[128,1152]{1,0:T(8,128)(2,1)S(1)}, bf16[128,1152]{1,0:T(8,128)(2,1)}, u32[]{:S(2)}, u32[]{:S(2)}) collective-permute-start(bf16[128,1152]{1,0:T(8,128)(2,1)S(1)} %concatenate.9), channel_id=1, source_target_pairs={{0,8},{1,9},{2,10},{3,11},{4,12},{5,13},{6,14},{7,15},{8,0},{9,1},... | collective-permute-start | bytes 884744 | tf_op jit(solution)/shard_map/ppermute | solution.py:155
  77.6 75.9 %collective-permute-start.5 = (bf16[128,1152]{1,0:T(8,128)(2,1)S(1)}, bf16[128,1152]{1,0:T(8,128)(2,1)}, u32[]{:S(2)}, u32[]{:S(2)}) collective-permute-start(bf16[128,1152]{1,0:T(8,128)(2,1)S(1)} %concatenate.9), channel_id=1, source_target_pairs={{0,12},{1,13},{2,14},{3,15},{4,8},{5,9},{6,10},{7,11},{8,4},{9,5},... | collective-permute-start | bytes 884744 | tf_op jit(solution)/shard_map/ppermute | solution.py:155
  81.4 117.4 %collective-permute-start.2 = (bf16[9,120,8,128]{3,2,1,0:T(8,128)(2,1)}, bf16[9,120,8,128]{3,2,1,0:T(8,128)(2,1)}, u32[]{:S(2)}, u32[]{:S(2)}) collective-permute-start(bf16[9,120,8,128]{3,2,1,0:T(8,128)(2,1)} %shard_map.128), channel_id=1, source_target_pairs={{0,8},{1,9},{2,10},{3,11},{4,12},{5,13},{6,14},{7,15},{8,0},{9,1},... | collective-permute-start | bytes 6635528 | tf_op jit(solution)/shard_map/ppermute | solution.py:238
  153.5 13.8 %collective-permute-start.8 = (bf16[2,384,1024]{2,1,0:T(8,128)(2,1)}, bf16[2,384,1024]{2,1,0:T(8,128)(2,1)}, u32[]{:S(2)}, u32[]{:S(2)}) collective-permute-start(bf16[2,384,1024]{2,1,0:T(8,128)(2,1)} %all-gather.5.cloned.1.call-done.refs_1_), channel_id=1, source_target_pairs={{0,1},{1,0},{2,3},{3,2},{4,5},{5,4},{6,7},{7,6},{8,9},{9,8},{10,11... | collective-permute-start | bytes 4718600 | tf_op jit(solution)/shard_map/ppermute | solution.py:155
  159.4 28.7 %collective-permute-start.6 = (bf16[512,1152]{1,0:T(8,128)(2,1)}, bf16[512,1152]{1,0:T(8,128)(2,1)}, u32[]{:S(2)}, u32[]{:S(2)}) collective-permute-start(bf16[512,1152]{1,0:T(8,128)(2,1)} %constant_dynamic-update-slice_fusion.2.x_ref), channel_id=1, source_target_pairs={{0,2},{1,3},{2,0},{3,1},{4,6},{5,7},{6,4},{7,5},{8,10},{9,11},{10,... | collective-permute-start | bytes 3538952 | tf_op jit(solution)/shard_map/ppermute | solution.py:155
  161.9 5.4 %copy-start.1 = (bf16[2,1024,768]{2,1,0:T(8,128)(2,1)S(1)}, bf16[2,1024,768]{2,1,0:T(8,128)(2,1)}, u32[]{:S(2)}) copy-start(bf16[2,1024,768]{2,1,0:T(8,128)(2,1)} %all-gather.3.cloned.1.call-done.refs_0_) | copy-start | bytes 9437188
  161.9 5.4 %copy-start.2 = (bf16[2,384,1024]{2,1,0:T(8,128)(2,1)S(1)}, bf16[2,384,1024]{2,1,0:T(8,128)(2,1)}, u32[]{:S(2)}) copy-start(bf16[2,384,1024]{2,1,0:T(8,128)(2,1)} %all-gather.5.cloned.1.call-done.refs_1_) | copy-start | bytes 4718596
  166.1 1.2 copy-start.5
  176.1 1.0 copy-start.3
  196.8 1.0 copy-start.7
  207.9 2.0 copy-start
  209.8 4.8 %copy-start.6 = (bf16[9,96,8,128]{3,2,1,0:T(8,128)(2,1)S(1)}, bf16[9,96,8,128]{3,2,1,0:T(8,128)(2,1)}, u32[]{:S(2)}) copy-start(bf16[9,96,8,128]{3,2,1,0:T(8,128)(2,1)} %copy-done.5) | copy-start | bytes 5308420
  209.8 55.7 %copy-start.4 = (bf16[512,1024]{1,0:T(8,128)(2,1)S(1)}, bf16[512,1024]{1,0:T(8,128)(2,1)}, u32[]{:S(2)}) copy-start(bf16[512,1024]{1,0:T(8,128)(2,1)} %copy-done.3) | copy-start | bytes 3145732
  209.8 90.4 %all-to-all-start.2 = ((bf16[8,2,120,8,128]{4,3,2,1,0:T(8,128)(2,1)}), bf16[8,2,120,8,128]{4,3,2,1,0:T(8,128)(2,1)}, u32[]{:S(2)}, u32[]{:S(2)}) async-start(bf16[8,2,120,8,128]{4,3,2,1,0:T(8,128)(2,1)} %bitcast.66), calls=%async_computation.2 | async-start | bytes 7864320 | tf_op jit(solution)/shard_map/all_to_all | solution.py:147
  214.7 81.1 %copy-start.8 = (bf16[7,96,8,128]{3,2,1,0:T(8,128)(2,1)S(1)}, bf16[7,96,8,128]{3,2,1,0:T(8,128)(2,1)}, u32[]{:S(2)}) copy-start(bf16[7,96,8,128]{3,2,1,0:T(8,128)(2,1)} %get-tuple-element.185.refs_2_) | copy-start | bytes 4128772
  214.7 81.1 %collective-permute-start.9 = (bf16[9,96,8,128]{3,2,1,0:T(8,128)(2,1)S(1)}, bf16[9,96,8,128]{3,2,1,0:T(8,128)(2,1)S(1)}, u32[]{:S(2)}, u32[]{:S(2)}) collective-permute-start(bf16[9,96,8,128]{3,2,1,0:T(8,128)(2,1)S(1)} %copy-done.6), channel_id=1, source_target_pairs={{0,8},{1,9},{2,10},{3,11},{4,12},{5,13},{6,14},{7,15},{8,0},{9,1},... | collective-permute-start | bytes 5308424 | tf_op jit(solution)/shard_map/ppermute | solution.py:270
  215.6 49.9 %collective-permute-start.10 = (bf16[512,1024]{1,0:T(8,128)(2,1)}, bf16[512,1024]{1,0:T(8,128)(2,1)S(1)}, u32[]{:S(2)}, u32[]{:S(2)}) collective-permute-start(bf16[512,1024]{1,0:T(8,128)(2,1)} %copy-done.7), channel_id=1, source_target_pairs={{0,2},{1,3},{2,0},{3,1},{4,6},{5,7},{6,4},{7,5},{8,10},{9,11},{10,... | collective-permute-start | bytes 3145736 | tf_op jit(solution)/shard_map/ppermute | solution.py:155
  300.2 69.4 %all-to-all-start.3 = ((bf16[8,2,96,8,128]{4,3,2,1,0:T(8,128)(2,1)}), bf16[8,2,96,8,128]{4,3,2,1,0:T(8,128)(2,1)S(1)}, u32[]{:S(2)}, u32[]{:S(2)}) async-start(bf16[8,2,96,8,128]{4,3,2,1,0:T(8,128)(2,1)} %bitcast.30), calls=%async_computation.3 | async-start | bytes 6291456 | tf_op jit(solution)/shard_map/all_to_all | solution.py:147
  306.6 47.1 %collective-permute-start.11 = (bf16[128,1024]{1,0:T(8,128)(2,1)S(1)}, bf16[128,1024]{1,0:T(8,128)(2,1)S(1)}, u32[]{:S(2)}, u32[]{:S(2)}) collective-permute-start(bf16[128,1024]{1,0:T(8,128)(2,1)S(1)} %get-tuple-element.202), channel_id=1, source_target_pairs={{0,4},{1,5},{2,6},{3,7},{4,0},{5,1},{6,2},{7,3},{8,12},{9,13},{10,... | collective-permute-start | bytes 786440 | tf_op jit(solution)/shard_map/ppermute | solution.py:155
  308.7 45.0 %collective-permute-start.12 = (bf16[128,1024]{1,0:T(8,128)(2,1)S(1)}, bf16[128,1024]{1,0:T(8,128)(2,1)S(1)}, u32[]{:S(2)}, u32[]{:S(2)}) collective-permute-start(bf16[128,1024]{1,0:T(8,128)(2,1)S(1)} %get-tuple-element.204), channel_id=1, source_target_pairs={{0,8},{1,9},{2,10},{3,11},{4,12},{5,13},{6,14},{7,15},{8,0},{9,1},... | collective-permute-start | bytes 786440 | tf_op jit(solution)/shard_map/ppermute | solution.py:155
  311.0 50.0 %collective-permute-start.13 = (bf16[128,1024]{1,0:T(8,128)(2,1)S(1)}, bf16[128,1024]{1,0:T(8,128)(2,1)S(1)}, u32[]{:S(2)}, u32[]{:S(2)}) collective-permute-start(bf16[128,1024]{1,0:T(8,128)(2,1)S(1)} %get-tuple-element.203), channel_id=1, source_target_pairs={{0,12},{1,13},{2,14},{3,15},{4,8},{5,9},{6,10},{7,11},{8,4},{9,5},... | collective-permute-start | bytes 786440 | tf_op jit(solution)/shard_map/ppermute | solution.py:155
Sparse Core Ops, SparseCore 0:
  23.9 47.2 all-gather.2
  73.9 29.4 all-gather.4

commit v2 on v1

--- a/solution.py
+++ b/solution.py
@@ -26,13 +26,53 @@
     return tiles.reshape(tiles.shape[0], parts, -1, SUB, LANE).swapaxes(0, 1)
 
 
+def pack_kernel(*refs):
+    *sources, out_ref, rows, in_sems, out_sems = refs
+    parts, slots = out_ref.shape[:2]
+
+    def copies(p):
+        at = 0
+        for n, source in enumerate(sources):
+            count = source.shape[1] // parts
+            for s in range(slots):
+                yield pltpu.make_async_copy(
+                    source.at[s, pl.ds(p * count, count)],
+                    rows.at[p, s, pl.ds(at, count)],
+                    in_sems.at[p, n, s],
+                )
+            at += count
+
+    for p in range(parts):
+        for copy in copies(p):
+            copy.start()
+    for p in range(parts):
+        for copy in copies(p):
+            copy.wait()
+        pltpu.make_async_copy(rows.at[p], out_ref.at[p], out_sems.at[p]).start()
+    for p in range(parts):
+        pltpu.make_async_copy(rows.at[p], out_ref.at[p], out_sems.at[p]).wait()
+
+
 def pack(arrays, parts):
     tiles = [to_tiles(a) for a in arrays]
+    slots = tiles[0].shape[0]
+    total = sum(t.shape[1] for t in tiles)
     if all(t.shape[1] % parts == 0 for t in tiles):
-        return jnp.concatenate([in_parts(t, parts) for t in tiles], axis=2)
-    slots = tiles[0].shape[0]
-    extra = -sum(t.shape[1] for t in tiles) % parts
-    tiles.append(jnp.zeros((slots, extra, SUB, LANE), tiles[0].dtype))
+        shape = (parts, slots, total // parts, SUB, LANE)
+        return pl.pallas_call(
+            pack_kernel,
+            in_specs=[pl.BlockSpec(memory_space=pl.ANY)] * len(tiles),
+            out_specs=pl.BlockSpec(memory_space=pl.ANY),
+            out_shape=jax.ShapeDtypeStruct(shape, tiles[0].dtype),
+            scratch_shapes=[
+                pltpu.VMEM(shape, tiles[0].dtype),
+                pltpu.SemaphoreType.DMA((parts, len(tiles), slots)),
+                pltpu.SemaphoreType.DMA((parts,)),
+            ],
+            compiler_params=pltpu.CompilerParams(vmem_limit_bytes=16 * 1024 * 1024),
+            cost_estimate=pl.CostEstimate(flops=0, bytes_accessed=0, transcendentals=0),
+        )(*tiles)
+    tiles.append(jnp.zeros((slots, -total % parts, SUB, LANE), tiles[0].dtype))
     return in_parts(jnp.concatenate(tiles, axis=1), parts)
 
 
@@ -93,12 +133,16 @@
     )(index, *tables)
 
 
-def expert_kernel(first_ref, x_ref, *refs):
+def lay(blocks):
+    laid = pick(jnp.arange(len(blocks), dtype=jnp.int32), *(x[None] for x in blocks))
+    return laid.reshape((-1,) + blocks[0].shape[1:])
+
+
+def expert_kernel(first_ref, x_ref, share_ref, *refs):
     *weight_refs, out_ref = refs
-    width = out_ref.shape[1]
-    half = (x_ref.shape[1] - width) // 2
-    x = x_ref[:, :width]
-    weights = x_ref[:, width:].astype(jnp.float32)
+    half = share_ref.shape[1] // 2
+    x = x_ref[...]
+    weights = share_ref[...].astype(jnp.float32)
     lane = lax.broadcasted_iota(jnp.int32, weights.shape, 1)
     total = jnp.zeros(out_ref.shape, jnp.float32)
     for n in range(len(weight_refs) // 2):
@@ -117,23 +161,23 @@
     out_ref[...] = total.astype(out_ref.dtype)
 
 
-def experts(x, first, weights):
-    rows, columns = x.shape
-    width = weights[0].shape[1]
+def experts(x, shares, first, weights):
+    rows, width = x.shape
     block = 256 if rows % 256 == 0 else rows
     return pl.pallas_call(
         expert_kernel,
         grid=(rows // block,),
         in_specs=[
             pl.BlockSpec(memory_space=pltpu.SMEM),
-            pl.BlockSpec((block, columns), lambda i: (i, 0)),
+            pl.BlockSpec((block, width), lambda i: (i, 0)),
+            pl.BlockSpec((block, shares.shape[1]), lambda i: (i, 0)),
         ]
         + [pl.BlockSpec(w.shape, lambda i: (0, 0, 0)) for w in weights],
         out_specs=pl.BlockSpec((block, width), lambda i: (i, 0)),
         out_shape=jax.ShapeDtypeStruct((rows, width), jnp.bfloat16),
         compiler_params=pltpu.CompilerParams(vmem_limit_bytes=40 * 1024 * 1024),
         cost_estimate=pl.CostEstimate(flops=0, bytes_accessed=0, transcendentals=0),
-    )(first, x, *weights)
+    )(first, x, shares, *weights)
 
 
 def plane_size(devices):
@@ -159,7 +203,7 @@
     return sum(x.astype(jnp.float32) for x in blocks).astype(jnp.bfloat16)
 
 
-def weighted_rows(tokens, expert_ids, route_weights, old_plan):
+def slot_shares(expert_ids, route_weights, old_plan):
     slot_count = old_plan.shape[0]
     slot_index = jnp.arange(slot_count, dtype=jnp.int32)
     share = route_weights / jnp.sum(route_weights, axis=1, keepdims=True)
@@ -169,9 +213,9 @@
     weight = jnp.sum(jnp.where(chosen, share[:, :, None], 0.0), axis=1)
     high = lax.reduce_precision(weight, exponent_bits=8, mantissa_bits=7)
     half = -(-2 * slot_count // LANE) * LANE // 2
-    pad = jnp.zeros((tokens.shape[0], half - slot_count), jnp.bfloat16)
+    pad = jnp.zeros((weight.shape[0], half - slot_count), jnp.bfloat16)
     return jnp.concatenate(
-        [tokens, high.astype(jnp.bfloat16), pad, (weight - high).astype(jnp.bfloat16), pad], axis=1
+        [high.astype(jnp.bfloat16), pad, (weight - high).astype(jnp.bfloat16), pad], axis=1
     )
 
 
@@ -221,13 +265,13 @@
     full_in = lax.all_gather(w_in, "grp", axis=1, tiled=True)
     full_out = lax.all_gather(w_out, "grp", axis=1, tiled=True)
 
-    rows = weighted_rows(tokens, expert_ids, route_weights, old_plan)
-    rows, *firsts = lax.optimization_barrier((rows, *chunk_a))
+    shares = slot_shares(expert_ids, route_weights, old_plan)
     inner = plane_size(devices)
     outer = range(0, devices, inner)
-    column = [flip(rows, "exp", i) for i in outer]
-    packed_a = pack(firsts, half)
+    column = [[flip(x, "exp", i) for i in outer] for x in (tokens, shares)]
+    packed_a, column = lax.optimization_barrier((pack(chunk_a, half), column))
     spread_a = exchange(packed_a, devices).reshape((held,) + packed_a.shape[2:])
+    rows = [lay(x) for x in column]
 
     *plan, number = crossing(old_plan, new_plan)
     most = -(-held * FIXED // 16)
@@ -239,15 +283,13 @@
     packed_b = pack(chunk_b, half)
     spread_b = exchange(packed_b, devices).reshape((held,) + packed_b.shape[2:])
     sent_b = pick(sent_index[:most], spread_b)
-    column, _ = lax.optimization_barrier((column, sent_a))
     steps = range(0, inner, 2)
-    rows = jnp.concatenate(column, axis=0)
-    blocks = [flip(rows, "exp", i) for i in steps]
+    blocks = [[flip(x, "exp", i) for x in rows] for i in steps]
     weights = [full_in, full_out, flip(full_in, "exp", 1), flip(full_out, "exp", 1)]
     me = lax.axis_index("exp").astype(jnp.int32)
     first = jnp.stack([me, me ^ 1]) * slots
     blocks[1:], sent_b = lax.optimization_barrier((blocks[1:], sent_b))
-    parts = [experts(x, first, weights) for x in blocks]
+    parts = [experts(*x, first, weights) for x in blocks]
 
     def more(state):
         place, *extra = state
@@ -259,10 +301,10 @@
             out.append(lax.dynamic_update_slice_in_dim(table, row, place - most, axis=0))
         return place + 1, *out
 
-    arrived_a, sent_b, parts = lax.optimization_barrier((arrived_a, sent_b, parts))
     extra = [
         jnp.zeros((max(held - most, 1),) + x.shape[1:], x.dtype) for x in (spread_a, spread_b)
     ]
+    arrived_a, sent_b, parts, extra = lax.optimization_barrier((arrived_a, sent_b, parts, extra))
     _, *extra = lax.while_loop(
         lambda state: state[0] < number, more, (jnp.int32(most), *extra)
     )
@@ -271,11 +313,12 @@
     picked_a = pick(index, spread_a, arrived_a, extra[0])
     landed_a = exchange(picked_a.reshape(packed_a.shape), devices)
     partial = add_up([flip(x, "exp", i) for i, x in zip(steps, parts)])
-    arrived_b, partial = lax.optimization_barrier((arrived_b, partial))
+    outs_a = unpack(landed_a, chunk_a)
+    arrived_b, partial, outs_a = lax.optimization_barrier((arrived_b, partial, outs_a))
 
     picked_b = pick(index, spread_b, arrived_b, extra[1])
     (new_moments_in,) = unpack(exchange(picked_b.reshape(packed_b.shape), devices), chunk_b)
-    new_w_in, new_w_out, new_moments_out = unpack(landed_a, chunk_a)
+    new_w_in, new_w_out, new_moments_out = outs_a
     size = tokens.shape[0]
     mixed = add_up([flip(partial[n * size : (n + 1) * size], "exp", i) for n, i in enumerate(outer)])
     return mixed, new_w_in, new_w_out, new_moments_in, new_moments_out

time: 379 us -> 384 us (1.013)
  Pallas kernels: 36 us -> 52.3 us
  waiting for transfers between devices: 253 us -> 238 us
  starting transfers between devices: 36.1 us -> 42 us
    ppermute x10 -> x14, waiting for transfers between devices: 179 us -> 110 us  [flip(): lax.ppermute(x, axis, [(d, d ^ bits) for d in range(lax.axis_size(axis))])]
    all_to_all x4, waiting for transfers between devices: 42.8 us -> 95.9 us  [swap(): lax.all_to_all(x, axis, split_axis=0, concat_axis=0, axis_index_groups=gr...]
    ppermute x1, waiting for transfers between devices: 28.8 us -> 0.01 us  [on_device(): arrived_b = lax.ppermute(sent_b, 'exp', across)]
    all_gather x1, waiting for transfers between devices: 0.01 us -> 23.5 us  [on_device(): full_out = lax.all_gather(w_out, 'grp', axis=1, tiled=True)]
    pallas_call x0 -> x2, Pallas kernels: none -> 14 us  [pack(): pl.pallas_call(pack_kernel, in_specs=[pl.BlockSpec(memory_space=pl.ANY)]...]
    ppermute x10 -> x14, starting transfers between devices: 13.4 us -> 21.6 us  [flip(): lax.ppermute(x, axis, [(d, d ^ bits) for d in range(lax.axis_size(axis))])]
    unnamed x30 -> x51, local copies, waits for them, and re-layouts: 12.7 us -> 19.3 us
    ppermute x1, waiting for transfers between devices: 1.1 us -> 7.22 us  [on_device(): arrived_a = lax.ppermute(sent_a, 'exp', across)]
  transfers between devices with their start and end apart: 18 -> 22, of which waited for: 8 -> 9; matrix products, arithmetic and copies ran while one was open for 5% -> 4% of each run, Pallas kernels for 8% -> 11%
where the time goes in v2:
time: 384 us; the launch traced here: 383 us
  waiting for transfers between devices  238 us (62%)
  Pallas kernels  52.3 us (14%)
  starting transfers between devices  42 us (11%)
  local copies, waits for them, and re-layouts  27.7 us (7%)
  between operations  14.4 us (4%)
  other arithmetic  8.6 us (2%)
    ppermute x14, waiting for transfers between devices, flip(): lax.ppermute(x, axis, [(d, d ^ bits) for d in range(lax.axis_size(axis))])  110 us
    all_to_all x4, waiting for transfers between devices, swap(): lax.all_to_all(x, axis, split_axis=0, concat_axis=0, axis_index_groups=gr...  95.9 us
    all_gather x1, waiting for transfers between devices, on_device(): full_out = lax.all_gather(w_out, 'grp', axis=1, tiled=True)  23.5 us
    ppermute x14, starting transfers between devices, flip(): lax.ppermute(x, axis, [(d, d ^ bits) for d in range(lax.axis_size(axis))])  21.6 us
    pallas_call x6, Pallas kernels, pick(): pl.pallas_call(pick_kernel, in_specs=[pl.BlockSpec(memory_space=pltpu.SME...  20.9 us
    unnamed x51, local copies, waits for them, and re-layouts  19.3 us
    all_to_all x4, starting transfers between devices, swap(): lax.all_to_all(x, axis, split_axis=0, concat_axis=0, axis_index_groups=gr...  17.9 us
    pallas_call x2, Pallas kernels, experts(): pl.pallas_call(expert_kernel, grid=(rows // block,), in_specs=[pl.BlockSp...  17.4 us
  transfers between devices with their start and end apart: 22, of which 9 were waited for; matrix products, arithmetic and copies ran while one was open for 4% of the time, Pallas kernels for 11%

profile of v2, /device:TPU:0, one launch (start us, length us, event | category | flops | bytes accessed | tf_op | source)
XLA Modules:
  0.0 383.3 jit_solution(10618638041574205349)
XLA Ops:
  7.2 3.1 collective-permute-start.2
  10.3 2.6 collective-permute-start.3
  17.3 3.5 collective-permute-start.6
  20.8 7.6 %collective-permute-done.5 = bf16[128,128]{1,0:T(8,128)(2,1)S(1)} collective-permute-done((bf16[128,128]{1,0:T(8,128)(2,1)S(1)}, bf16[128,128]{1,0:T(8,128)(2,1)S(1)}, u32[]{:S(2)}, u32[]{:S(2)}) %collective-permute-start.5) | collective-permute-done | bytes 32800 | tf_op jit(solution)/shard_map/ppermute | solution.py:199
  28.4 2.5 collective-permute-start.7
  30.8 1.4 copy-done.3
  32.2 1.1 copy-done.8
  33.4 1.4 copy-done.11
  34.8 8.1 %shard_map.128 = bf16[8,2,120,8,128]{4,3,2,1,0:T(8,128)(2,1)S(1)} custom-call(bf16[2,384,8,128]{3,2,1,0:T(8,128)(2,1)S(1)} %bitcast.69, bf16[2,192,8,128]{3,2,1,0:T(8,128)(2,1)S(1)} %bitcast.71, bf16[2,384,8,128]{3,2,1,0:T(8,128)(2,1)S(1)} %bitcast.72), custom_call_target="tpu_custom_call" | custom-call | tf_op jit(solution)/shard_map/pallas_call | solution.py:62
  42.9 1.8 copy-done
  46.9 4.8 %all-to-all-start = ((bf16[8,2,120,8,128]{4,3,2,1,0:T(8,128)(2,1)}), bf16[8,2,120,8,128]{4,3,2,1,0:T(8,128)(2,1)}, u32[]{:S(2)}, u32[]{:S(2)}) async-start(bf16[8,2,120,8,128]{4,3,2,1,0:T(8,128)(2,1)} %copy-done), calls=%async_computation | async-start | bytes 7864320 | tf_op jit(solution)/shard_map/all_to_all | solution.py:191
  52.4 5.9 %shard_map.132 = bf16[8,2,96,8,128]{4,3,2,1,0:T(8,128)(2,1)} custom-call(bf16[2,768,8,128]{3,2,1,0:T(8,128)(2,1)S(1)} %bitcast.70), custom_call_target="tpu_custom_call" | custom-call | tf_op jit(solution)/shard_map/pallas_call | solution.py:62
  58.4 38.7 %all-to-all-done = bf16[8,2,120,8,128]{4,3,2,1,0:T(8,128)(2,1)} async-done(((bf16[8,2,120,8,128]{4,3,2,1,0:T(8,128)(2,1)}), bf16[8,2,120,8,128]{4,3,2,1,0:T(8,128)(2,1)}, u32[]{:S(2)}, u32[]{:S(2)}) %all-to-all-start) | async-done | bytes 3932192 | tf_op jit(solution)/shard_map/all_to_all | solution.py:191
  97.1 4.4 %all-to-all-start.1 = ((bf16[8,2,96,8,128]{4,3,2,1,0:T(8,128)(2,1)}), bf16[8,2,96,8,128]{4,3,2,1,0:T(8,128)(2,1)}, u32[]{:S(2)}, u32[]{:S(2)}) async-start(bf16[8,2,96,8,128]{4,3,2,1,0:T(8,128)(2,1)} %shard_map.132), calls=%async_computation.1 | async-start | bytes 6291456 | tf_op jit(solution)/shard_map/all_to_all | solution.py:191
  103.4 3.1 shard_map.129
  106.5 1.5 collective-permute-start.8
  108.1 23.5 %all-gather.5.cloned.1.call-done.refs_1_ = bf16[2,384,1024]{2,1,0:T(8,128)(2,1)} async-done(((bf16[2,192,1024]{2,1,0:T(8,128)(2,1)}), bf16[2,384,1024]{2,1,0:T(8,128)(2,1)}) %all-gather.5.cloned.1.call-update) | async-done | bytes 1572880 | tf_op jit(solution)/shard_map/all_gather | solution.py:266
  134.4 1.7 shard_map.130
  136.2 1.5 collective-permute-start.9
  138.1 1.1 shard_map.131
  139.8 1.3 select_reduce_fusion.4
  141.1 26.2 %all-to-all-done.1 = bf16[8,2,96,8,128]{4,3,2,1,0:T(8,128)(2,1)} async-done(((bf16[8,2,96,8,128]{4,3,2,1,0:T(8,128)(2,1)}), bf16[8,2,96,8,128]{4,3,2,1,0:T(8,128)(2,1)}, u32[]{:S(2)}, u32[]{:S(2)}) %all-to-all-start.1) | async-done | bytes 3145760 | tf_op jit(solution)/shard_map/all_to_all | solution.py:191
  167.3 4.2 %shard_map.133 = bf16[9,96,8,128]{3,2,1,0:T(8,128)(2,1)S(1)} custom-call(s32[9]{0:T(128)S(1)} %bitcast.88, bf16[16,96,8,128]{3,2,1,0:T(8,128)(2,1)} %bitcast.24.refs_0_), custom_call_target="tpu_custom_call" | custom-call | tf_op jit(solution)/shard_map/pallas_call | solution.py:120
  171.5 1.2 copy-done.9
  172.7 6.0 %collective-permute-done.10.share_ref = bf16[512,128]{1,0:T(8,128)(2,1)S(1)} collective-permute-done((bf16[512,128]{1,0:T(8,128)(2,1)S(1)}, bf16[512,128]{1,0:T(8,128)(2,1)S(1)}, u32[]{:S(2)}, u32[]{:S(2)}) %collective-permute-start.10) | collective-permute-done | bytes 131104 | tf_op jit(solution)/shard_map/ppermute | solution.py:199
  178.8 8.7 %shard_map.134 = bf16[512,1024]{1,0:T(8,128)(2,1)S(1)} custom-call(s32[2]{0:T(128)S(1)} %add_multiply_fusion.first_ref, bf16[512,1024]{1,0:T(8,128)(2,1)} %bitcast.15.x_ref, bf16[512,128]{1,0:T(8,128)(2,1)S(1)} %bitcast.74, bf16[2,1024,768]{2,1,0:T(8,128)(2,1)S(1)} %copy-done.2, bf16[2,384,1024]{2,1,0:T(8,128)(2,1)S(1)} %copy-done.4, ...), custom_call_target="tpu_custom_call" | custom-call | tf_op jit(solution)/shard_map/pallas_call | solution.py:167
  188.5 8.7 %shard_map.135 = bf16[512,1024]{1,0:T(8,128)(2,1)S(1)} custom-call(s32[2]{0:T(128)S(1)} %add_multiply_fusion.first_ref, bf16[512,1024]{1,0:T(8,128)(2,1)} %collective-permute-done.9.x_ref, bf16[512,128]{1,0:T(8,128)(2,1)S(1)} %collective-permute-done.10.share_ref, bf16[2,1024,768]{2,1,0:T(8,128)(2,1)S(1)} %copy-done.2, bf16[2,384,1024]{2,1,0:T(8,128)(2,1)S(1)} %copy-done.4, ...), custom_call_target="tpu_custom_call" | custom-call | tf_op jit(solution)/shard_map/pallas_call | solution.py:167
  198.2 7.2 %collective-permute-done.8.refs_1_ = bf16[9,120,8,128]{3,2,1,0:T(8,128)(2,1)} collective-permute-done((bf16[9,120,8,128]{3,2,1,0:T(8,128)(2,1)}, bf16[9,120,8,128]{3,2,1,0:T(8,128)(2,1)}, u32[]{:S(2)}, u32[]{:S(2)}) %collective-permute-start.8) | collective-permute-done | bytes 2211872 | tf_op jit(solution)/shard_map/ppermute | solution.py:282
  205.6 1.3 broadcast_in_dim.134
  207.6 6.8 %shard_map.136 = bf16[16,120,8,128]{3,2,1,0:T(8,128)(2,1)S(1)} custom-call(s32[16]{0:T(128)S(1)} %compare_select_fusion.index_ref, bf16[16,120,8,128]{3,2,1,0:T(8,128)(2,1)} %bitcast.10.refs_0_, bf16[9,120,8,128]{3,2,1,0:T(8,128)(2,1)} %collective-permute-done.8.refs_1_, bf16[7,120,8,128]{3,2,1,0:T(8,128)(2,1)S(1)} %get-tuple-element.193.refs_2_), custom_call_target="tpu_custom_call" | custom-call | tf_op jit(solution)/shard_map/pallas_call | solution.py:120
  214.4 1.9 copy-done.1
  216.3 5.0 %all-to-all-start.2 = ((bf16[8,2,120,8,128]{4,3,2,1,0:T(8,128)(2,1)}), bf16[8,2,120,8,128]{4,3,2,1,0:T(8,128)(2,1)}, u32[]{:S(2)}, u32[]{:S(2)}) async-start(bf16[8,2,120,8,128]{4,3,2,1,0:T(8,128)(2,1)} %bitcast.68), calls=%async_computation.2 | async-start | bytes 7864320 | tf_op jit(solution)/shard_map/all_to_all | solution.py:191
  222.2 2.0 collective-permute-start.14
  224.1 47.8 %collective-permute-done.14 = bf16[512,1024]{1,0:T(8,128)(2,1)S(1)} collective-permute-done((bf16[512,1024]{1,0:T(8,128)(2,1)}, bf16[512,1024]{1,0:T(8,128)(2,1)S(1)}, u32[]{:S(2)}, u32[]{:S(2)}) %collective-permute-start.14) | collective-permute-done | bytes 1048608 | tf_op jit(solution)/shard_map/ppermute | solution.py:199
  271.9 1.4 add_convert_fusion
  273.3 31.0 %all-to-all-done.2 = bf16[8,2,120,8,128]{4,3,2,1,0:T(8,128)(2,1)} async-done(((bf16[8,2,120,8,128]{4,3,2,1,0:T(8,128)(2,1)}), bf16[8,2,120,8,128]{4,3,2,1,0:T(8,128)(2,1)}, u32[]{:S(2)}, u32[]{:S(2)}) %all-to-all-start.2) | async-done | bytes 3932192 | tf_op jit(solution)/shard_map/all_to_all | solution.py:191
  304.4 2.2 fusion.6
  306.6 1.3 copy.39
  307.9 1.3 copy.41
  309.1 1.3 slice.34
  311.4 3.9 %shard_map.137 = bf16[16,96,8,128]{3,2,1,0:T(8,128)(2,1)} custom-call(s32[16]{0:T(128)S(1)} %compare_select_fusion.index_ref, bf16[16,96,8,128]{3,2,1,0:T(8,128)(2,1)} %bitcast.24.refs_0_, bf16[9,96,8,128]{3,2,1,0:T(8,128)(2,1)} %collective-permute-done.13.refs_1_, bf16[7,96,8,128]{3,2,1,0:T(8,128)(2,1)S(1)} %copy-done.20), custom_call_target="tpu_custom_call" | custom-call | tf_op jit(solution)/shard_map/pallas_call | solution.py:120
  315.3 3.7 all-to-all-start.3
  319.0 1.2 fusion.7
  320.1 2.0 collective-permute-start.15
  322.3 2.3 collective-permute-start.17
  324.6 48.1 %collective-permute-done.15 = bf16[128,1024]{1,0:T(8,128)(2,1)S(1)} collective-permute-done((bf16[128,1024]{1,0:T(8,128)(2,1)S(1)}, bf16[128,1024]{1,0:T(8,128)(2,1)S(1)}, u32[]{:S(2)}, u32[]{:S(2)}) %collective-permute-start.15) | collective-permute-done | bytes 262176 | tf_op jit(solution)/shard_map/ppermute | solution.py:199
  372.7 1.8 add_convert_fusion.1
  374.6 1.9 copy.38
  (93 shorter events, 17.8 us)
Async XLA Ops:
  7.2 37.6 %collective-permute-start.2 = (bf16[128,1024]{1,0:T(8,128)(2,1)}, bf16[128,1024]{1,0:T(8,128)(2,1)S(1)}, u32[]{:S(2)}, u32[]{:S(2)}) collective-permute-start(bf16[128,1024]{1,0:T(8,128)(2,1)} %param.11), channel_id=1, source_target_pairs={{0,4},{1,5},{2,6},{3,7},{4,0},{5,1},{6,2},{7,3},{8,12},{9,13},{10,... | collective-permute-start | bytes 786440 | tf_op jit(solution)/shard_map/ppermute | solution.py:199
  10.3 35.2 %collective-permute-start.3 = (bf16[128,1024]{1,0:T(8,128)(2,1)}, bf16[128,1024]{1,0:T(8,128)(2,1)S(1)}, u32[]{:S(2)}, u32[]{:S(2)}) collective-permute-start(bf16[128,1024]{1,0:T(8,128)(2,1)} %param.11), channel_id=1, source_target_pairs={{0,8},{1,9},{2,10},{3,11},{4,12},{5,13},{6,14},{7,15},{8,0},{9,1},... | collective-permute-start | bytes 786440 | tf_op jit(solution)/shard_map/ppermute | solution.py:199
  12.8 33.3 %collective-permute-start.4 = (bf16[128,1024]{1,0:T(8,128)(2,1)}, bf16[128,1024]{1,0:T(8,128)(2,1)S(1)}, u32[]{:S(2)}, u32[]{:S(2)}) collective-permute-start(bf16[128,1024]{1,0:T(8,128)(2,1)} %param.11), channel_id=1, source_target_pairs={{0,12},{1,13},{2,14},{3,15},{4,8},{5,9},{6,10},{7,11},{8,4},{9,5},... | collective-permute-start | bytes 786440 | tf_op jit(solution)/shard_map/ppermute | solution.py:199
  16.3 12.1 %collective-permute-start.5 = (bf16[128,128]{1,0:T(8,128)(2,1)S(1)}, bf16[128,128]{1,0:T(8,128)(2,1)S(1)}, u32[]{:S(2)}, u32[]{:S(2)}) collective-permute-start(bf16[128,128]{1,0:T(8,128)(2,1)S(1)} %pad_maximum_fusion), channel_id=1, source_target_pairs={{0,4},{1,5},{2,6},{3,7},{4,0},{5,1},{6,2},{7,3},{8,12},{9,13},{10,... | collective-permute-start | bytes 98312 | tf_op jit(solution)/shard_map/ppermute | solution.py:199
  17.3 27.5 %collective-permute-start.6 = (bf16[128,128]{1,0:T(8,128)(2,1)S(1)}, bf16[128,128]{1,0:T(8,128)(2,1)S(1)}, u32[]{:S(2)}, u32[]{:S(2)}) collective-permute-start(bf16[128,128]{1,0:T(8,128)(2,1)S(1)} %pad_maximum_fusion), channel_id=1, source_target_pairs={{0,8},{1,9},{2,10},{3,11},{4,12},{5,13},{6,14},{7,15},{8,0},{9,1},... | collective-permute-start | bytes 98312 | tf_op jit(solution)/shard_map/ppermute | solution.py:199
  28.4 16.4 %collective-permute-start.7 = (bf16[128,128]{1,0:T(8,128)(2,1)S(1)}, bf16[128,128]{1,0:T(8,128)(2,1)S(1)}, u32[]{:S(2)}, u32[]{:S(2)}) collective-permute-start(bf16[128,128]{1,0:T(8,128)(2,1)S(1)} %pad_maximum_fusion), channel_id=1, source_target_pairs={{0,12},{1,13},{2,14},{3,15},{4,8},{5,9},{6,10},{7,11},{8,4},{9,5},... | collective-permute-start | bytes 98312 | tf_op jit(solution)/shard_map/ppermute | solution.py:199
  30.8 1.4 copy-start.3
  32.2 1.1 copy-start.8
  33.4 1.4 copy-start.11
  42.9 1.9 copy-start
  44.8 0.7 copy-start.14
  45.5 0.7 copy-start.16
  46.2 0.7 copy-start.18
  46.9 5.6 %copy-start.7 = (bf16[2,2,512,768]{3,2,1,0:T(8,128)(2,1)S(1)}, bf16[2,2,512,768]{3,2,1,0:T(8,128)(2,1)}, u32[]{:S(2)}) copy-start(bf16[2,2,512,768]{3,2,1,0:T(8,128)(2,1)} %param.14) | copy-start | bytes 9437188
  46.9 50.2 %all-to-all-start = ((bf16[8,2,120,8,128]{4,3,2,1,0:T(8,128)(2,1)}), bf16[8,2,120,8,128]{4,3,2,1,0:T(8,128)(2,1)}, u32[]{:S(2)}, u32[]{:S(2)}) async-start(bf16[8,2,120,8,128]{4,3,2,1,0:T(8,128)(2,1)} %copy-done), calls=%async_computation | async-start | bytes 7864320 | tf_op jit(solution)/shard_map/all_to_all | solution.py:191
  51.7 50.6 %all-gather.3.cloned.1.call-start = ((), (), s32[]{:S(2)}) async-start(), calls=%async_computation.4 | async-start | bytes 4718592 | tf_op jit(solution)/shard_map/all_gather | solution.py:265
  58.4 44.4 %copy-start.21 = (s32[32]{0:T(128)S(1)}, s32[32]{0:T(128)}, u32[]{:S(2)}) copy-start(s32[32]{0:T(128)} %param.18) | copy-start | bytes 388
  58.4 44.3 %copy-start.23 = (s32[32]{0:T(128)S(1)}, s32[32]{0:T(128)}, u32[]{:S(2)}) copy-start(s32[32]{0:T(128)} %param.19) | copy-start | bytes 388
  97.1 70.3 %all-to-all-start.1 = ((bf16[8,2,96,8,128]{4,3,2,1,0:T(8,128)(2,1)}), bf16[8,2,96,8,128]{4,3,2,1,0:T(8,128)(2,1)}, u32[]{:S(2)}, u32[]{:S(2)}) async-start(bf16[8,2,96,8,128]{4,3,2,1,0:T(8,128)(2,1)} %shard_map.132), calls=%async_computation.1 | async-start | bytes 6291456 | tf_op jit(solution)/shard_map/all_to_all | solution.py:191
  101.5 30.1 %all-gather.5.cloned.1.call-start = ((), (), s32[]{:S(2)}) async-start(), calls=%async_computation.5 | async-start | bytes 2359296 | tf_op jit(solution)/shard_map/all_gather | solution.py:266
  102.3 76.5 %collective-permute-start.11 = (bf16[2,1024,768]{2,1,0:T(8,128)(2,1)}, bf16[2,1024,768]{2,1,0:T(8,128)(2,1)S(1)}, u32[]{:S(2)}, u32[]{:S(2)}) collective-permute-start(bf16[2,1024,768]{2,1,0:T(8,128)(2,1)} %all-gather.3.cloned.1.call-done.refs_0_), channel_id=1, source_target_pairs={{0,1},{1,0},{2,3},{3,2},{4,5},{5,4},{6,7},{7,6},{8,9},{9,8},{10,11... | collective-permute-start | bytes 9437192 | tf_op jit(solution)/shard_map/ppermute | solution.py:199
  103.2 34.6 %copy-start.22 = (s32[32]{0:T(128)}, s32[32]{0:T(128)S(1)}, u32[]{:S(2)}) copy-start(s32[32]{0:T(128)S(1)} %convert_reduce_fusion) | copy-start | bytes 388
  103.4 28.2 %copy-start.13 = (bf16[128,1024]{1,0:T(8,128)(2,1)S(1)}, bf16[128,1024]{1,0:T(8,128)(2,1)}, u32[]{:S(2)}) copy-start(bf16[128,1024]{1,0:T(8,128)(2,1)} %param.11) | copy-start | bytes 786436
  106.5 98.9 %collective-permute-start.8 = (bf16[9,120,8,128]{3,2,1,0:T(8,128)(2,1)}, bf16[9,120,8,128]{3,2,1,0:T(8,128)(2,1)}, u32[]{:S(2)}, u32[]{:S(2)}) collective-permute-start(bf16[9,120,8,128]{3,2,1,0:T(8,128)(2,1)} %shard_map.129), channel_id=1, source_target_pairs={{0,8},{1,9},{2,10},{3,11},{4,12},{5,13},{6,14},{7,15},{8,0},{9,1},... | collective-permute-start | bytes 6635528 | tf_op jit(solution)/shard_map/ppermute | solution.py:282
  131.6 47.2 %collective-permute-start.12 = (bf16[2,384,1024]{2,1,0:T(8,128)(2,1)}, bf16[2,384,1024]{2,1,0:T(8,128)(2,1)}, u32[]{:S(2)}, u32[]{:S(2)}) collective-permute-start(bf16[2,384,1024]{2,1,0:T(8,128)(2,1)} %all-gather.5.cloned.1.call-done.refs_1_), channel_id=1, source_target_pairs={{0,1},{1,0},{2,3},{3,2},{4,5},{5,4},{6,7},{7,6},{8,9},{9,8},{10,11... | collective-permute-start | bytes 4718600 | tf_op jit(solution)/shard_map/ppermute | solution.py:199
  131.6 1.0 copy-start.15
  132.5 0.9 copy-start.17
  133.5 0.9 copy-start.19
  136.2 42.6 %collective-permute-start.9 = (bf16[512,1024]{1,0:T(8,128)(2,1)}, bf16[512,1024]{1,0:T(8,128)(2,1)}, u32[]{:S(2)}, u32[]{:S(2)}) collective-permute-start(bf16[512,1024]{1,0:T(8,128)(2,1)} %bitcast.15.x_ref), channel_id=1, source_target_pairs={{0,2},{1,3},{2,0},{3,1},{4,6},{5,7},{6,4},{7,5},{8,10},{9,11},{10,... | collective-permute-start | bytes 3145736 | tf_op jit(solution)/shard_map/ppermute | solution.py:199
  139.1 39.6 %collective-permute-start.10 = (bf16[512,128]{1,0:T(8,128)(2,1)S(1)}, bf16[512,128]{1,0:T(8,128)(2,1)S(1)}, u32[]{:S(2)}, u32[]{:S(2)}) collective-permute-start(bf16[512,128]{1,0:T(8,128)(2,1)S(1)} %bitcast.73), channel_id=1, source_target_pairs={{0,2},{1,3},{2,0},{3,1},{4,6},{5,7},{6,4},{7,5},{8,10},{9,11},{10,... | collective-permute-start | bytes 393224 | tf_op jit(solution)/shard_map/ppermute | solution.py:199
  167.3 11.4 %copy-start.2 = (bf16[2,1024,768]{2,1,0:T(8,128)(2,1)S(1)}, bf16[2,1024,768]{2,1,0:T(8,128)(2,1)}, u32[]{:S(2)}) copy-start(bf16[2,1024,768]{2,1,0:T(8,128)(2,1)} %all-gather.3.cloned.1.call-done.refs_0_) | copy-start | bytes 9437188
  167.3 11.5 %copy-start.4 = (bf16[2,384,1024]{2,1,0:T(8,128)(2,1)S(1)}, bf16[2,384,1024]{2,1,0:T(8,128)(2,1)}, u32[]{:S(2)}) copy-start(bf16[2,384,1024]{2,1,0:T(8,128)(2,1)} %all-gather.5.cloned.1.call-done.refs_1_) | copy-start | bytes 4718596
  171.5 1.2 copy-start.9
  187.5 1.0 copy-start.5
  197.2 1.0 copy-start.12
  214.4 1.9 copy-start.1
  216.3 5.0 %copy-start.10 = (bf16[9,96,8,128]{3,2,1,0:T(8,128)(2,1)S(1)}, bf16[9,96,8,128]{3,2,1,0:T(8,128)(2,1)}, u32[]{:S(2)}) copy-start(bf16[9,96,8,128]{3,2,1,0:T(8,128)(2,1)} %copy-done.9) | copy-start | bytes 5308420
  216.3 55.6 %copy-start.6 = (bf16[512,1024]{1,0:T(8,128)(2,1)S(1)}, bf16[512,1024]{1,0:T(8,128)(2,1)}, u32[]{:S(2)}) copy-start(bf16[512,1024]{1,0:T(8,128)(2,1)} %copy-done.5) | copy-start | bytes 3145732
  216.3 88.1 %all-to-all-start.2 = ((bf16[8,2,120,8,128]{4,3,2,1,0:T(8,128)(2,1)}), bf16[8,2,120,8,128]{4,3,2,1,0:T(8,128)(2,1)}, u32[]{:S(2)}, u32[]{:S(2)}) async-start(bf16[8,2,120,8,128]{4,3,2,1,0:T(8,128)(2,1)} %bitcast.68), calls=%async_computation.2 | async-start | bytes 7864320 | tf_op jit(solution)/shard_map/all_to_all | solution.py:191
  221.3 90.1 %collective-permute-start.13 = (bf16[9,96,8,128]{3,2,1,0:T(8,128)(2,1)S(1)}, bf16[9,96,8,128]{3,2,1,0:T(8,128)(2,1)}, u32[]{:S(2)}, u32[]{:S(2)}) collective-permute-start(bf16[9,96,8,128]{3,2,1,0:T(8,128)(2,1)S(1)} %copy-done.10), channel_id=1, source_target_pairs={{0,8},{1,9},{2,10},{3,11},{4,12},{5,13},{6,14},{7,15},{8,0},{9,1},... | collective-permute-start | bytes 5308424 | tf_op jit(solution)/shard_map/ppermute | solution.py:312
  222.2 49.8 %collective-permute-start.14 = (bf16[512,1024]{1,0:T(8,128)(2,1)}, bf16[512,1024]{1,0:T(8,128)(2,1)S(1)}, u32[]{:S(2)}, u32[]{:S(2)}) collective-permute-start(bf16[512,1024]{1,0:T(8,128)(2,1)} %copy-done.12), channel_id=1, source_target_pairs={{0,2},{1,3},{2,0},{3,1},{4,6},{5,7},{6,4},{7,5},{8,10},{9,11},{10,... | collective-permute-start | bytes 3145736 | tf_op jit(solution)/shard_map/ppermute | solution.py:199
  309.1 2.2 copy-start.20
  315.3 59.3 %all-to-all-start.3 = ((bf16[8,2,96,8,128]{4,3,2,1,0:T(8,128)(2,1)}), bf16[8,2,96,8,128]{4,3,2,1,0:T(8,128)(2,1)S(1)}, u32[]{:S(2)}, u32[]{:S(2)}) async-start(bf16[8,2,96,8,128]{4,3,2,1,0:T(8,128)(2,1)} %bitcast.40), calls=%async_computation.3 | async-start | bytes 6291456 | tf_op jit(solution)/shard_map/all_to_all | solution.py:191
  320.1 52.6 %collective-permute-start.15 = (bf16[128,1024]{1,0:T(8,128)(2,1)S(1)}, bf16[128,1024]{1,0:T(8,128)(2,1)S(1)}, u32[]{:S(2)}, u32[]{:S(2)}) collective-permute-start(bf16[128,1024]{1,0:T(8,128)(2,1)S(1)} %get-tuple-element.216), channel_id=1, source_target_pairs={{0,4},{1,5},{2,6},{3,7},{4,0},{5,1},{6,2},{7,3},{8,12},{9,13},{10,... | collective-permute-start | bytes 786440 | tf_op jit(solution)/shard_map/ppermute | solution.py:199
  322.1 50.6 %collective-permute-start.16 = (bf16[128,1024]{1,0:T(8,128)(2,1)S(1)}, bf16[128,1024]{1,0:T(8,128)(2,1)S(1)}, u32[]{:S(2)}, u32[]{:S(2)}) collective-permute-start(bf16[128,1024]{1,0:T(8,128)(2,1)S(1)} %get-tuple-element.218), channel_id=1, source_target_pairs={{0,8},{1,9},{2,10},{3,11},{4,12},{5,13},{6,14},{7,15},{8,0},{9,1},... | collective-permute-start | bytes 786440 | tf_op jit(solution)/shard_map/ppermute | solution.py:199
  322.3 50.4 %collective-permute-start.17 = (bf16[128,1024]{1,0:T(8,128)(2,1)S(1)}, bf16[128,1024]{1,0:T(8,128)(2,1)S(1)}, u32[]{:S(2)}, u32[]{:S(2)}) collective-permute-start(bf16[128,1024]{1,0:T(8,128)(2,1)S(1)} %get-tuple-element.217), channel_id=1, source_target_pairs={{0,12},{1,13},{2,14},{3,15},{4,8},{5,9},{6,10},{7,11},{8,4},{9,5},... | collective-permute-start | bytes 786440 | tf_op jit(solution)/shard_map/ppermute | solution.py:199
Sparse Core Ops, SparseCore 0:
  54.1 45.3 all-gather.2
  103.9 27.6 all-gather.4

commit v3 on v1

--- a/solution.py
+++ b/solution.py
@@ -91,6 +91,11 @@
         compiler_params=pltpu.CompilerParams(vmem_limit_bytes=16 * 1024 * 1024),
         cost_estimate=pl.CostEstimate(flops=0, bytes_accessed=0, transcendentals=0),
     )(index, *tables)
+
+
+def lay(blocks):
+    laid = pick(jnp.arange(len(blocks), dtype=jnp.int32), *(x[None] for x in blocks))
+    return laid.reshape((-1,) + blocks[0].shape[1:])
 
 
 def expert_kernel(first_ref, x_ref, *refs):
@@ -217,67 +222,82 @@
     half = devices // 2
     slots = w_in.shape[0]
     held = half * slots
-    chunk_a, chunk_b = (w_in, w_out, moments_out), (moments_in,)
+    chunk_a, chunk_b, chunk_c = (w_in, w_out), (moments_in,), (moments_out,)
     full_in = lax.all_gather(w_in, "grp", axis=1, tiled=True)
     full_out = lax.all_gather(w_out, "grp", axis=1, tiled=True)
-
-    rows = weighted_rows(tokens, expert_ids, route_weights, old_plan)
-    rows, *firsts = lax.optimization_barrier((rows, *chunk_a))
-    inner = plane_size(devices)
-    outer = range(0, devices, inner)
-    column = [flip(rows, "exp", i) for i in outer]
-    packed_a = pack(firsts, half)
-    spread_a = exchange(packed_a, devices).reshape((held,) + packed_a.shape[2:])
-
     *plan, number = crossing(old_plan, new_plan)
     most = -(-held * FIXED // 16)
     sent_index, index = places(plan, held, held)
     across = [(d, (d + half) % devices) for d in range(devices)]
 
-    sent_a = pick(sent_index[:most], spread_a)
-    arrived_a = lax.ppermute(sent_a, "exp", across)
-    packed_b = pack(chunk_b, half)
-    spread_b = exchange(packed_b, devices).reshape((held,) + packed_b.shape[2:])
-    sent_b = pick(sent_index[:most], spread_b)
-    column, _ = lax.optimization_barrier((column, sent_a))
+    def leave(spread):
+        return pick(sent_index[:most], spread)
+
+    def spread_out(packed):
+        return exchange(packed, devices).reshape((held,) + packed.shape[2:])
+
+    def collect(spread, arrived, extra):
+        picked = pick(index, spread, arrived, extra)
+        return exchange(picked.reshape((half, slots) + picked.shape[1:]), devices)
+
+    def beyond(*spreads):
+        def more(state):
+            place, *extra = state
+            at = lax.dynamic_index_in_dim(sent_index, place, keepdims=False)
+            out = []
+            for spread, table in zip(spreads, extra):
+                row = lax.dynamic_slice_in_dim(spread, at, 1, axis=0)
+                row = lax.ppermute(row, "exp", across)
+                out.append(lax.dynamic_update_slice_in_dim(table, row, place - most, axis=0))
+            return place + 1, *out
+
+        extra = [x[: max(held - most, 1)] for x in spreads]
+        state = lax.while_loop(
+            lambda state: state[0] < number, more, (jnp.int32(most), *extra)
+        )
+        return state[1:]
+
+    rows = weighted_rows(tokens, expert_ids, route_weights, old_plan)
+    inner = plane_size(devices)
+    outer = range(0, devices, inner)
+    column = [flip(rows, "exp", i) for i in outer]
+    packed_a, column = lax.optimization_barrier((pack(chunk_a, half), column))
+    spread_a, packed_b, packed_c = lax.optimization_barrier(
+        (spread_out(packed_a), pack(chunk_b, half), pack(chunk_c, half))
+    )
+    rows = lay(column)
+
+    arrived_a = lax.ppermute(leave(spread_a), "exp", across)
+    spread_b, packed_c = lax.optimization_barrier((spread_out(packed_b), packed_c))
+    sent_b = leave(spread_b)
+    spread_c = spread_out(packed_c)
     steps = range(0, inner, 2)
-    rows = jnp.concatenate(column, axis=0)
     blocks = [flip(rows, "exp", i) for i in steps]
     weights = [full_in, full_out, flip(full_in, "exp", 1), flip(full_out, "exp", 1)]
+    arrived_a, sent_b, blocks = lax.optimization_barrier((arrived_a, sent_b, blocks))
+
+    extra_a, extra_b = beyond(spread_a, spread_b)
+    arrived_b = lax.ppermute(sent_b, "exp", across)
+    landed_a = collect(spread_a, arrived_a, extra_a)
     me = lax.axis_index("exp").astype(jnp.int32)
     first = jnp.stack([me, me ^ 1]) * slots
-    blocks[1:], sent_b = lax.optimization_barrier((blocks[1:], sent_b))
     parts = [experts(x, first, weights) for x in blocks]
-
-    def more(state):
-        place, *extra = state
-        at = lax.dynamic_index_in_dim(sent_index, place, keepdims=False)
-        out = []
-        for spread, table in zip((spread_a, spread_b), extra):
-            row = lax.dynamic_slice_in_dim(spread, at, 1, axis=0)
-            row = lax.ppermute(row, "exp", across)
-            out.append(lax.dynamic_update_slice_in_dim(table, row, place - most, axis=0))
-        return place + 1, *out
-
-    arrived_a, sent_b, parts = lax.optimization_barrier((arrived_a, sent_b, parts))
-    extra = [
-        jnp.zeros((max(held - most, 1),) + x.shape[1:], x.dtype) for x in (spread_a, spread_b)
-    ]
-    _, *extra = lax.while_loop(
-        lambda state: state[0] < number, more, (jnp.int32(most), *extra)
-    )
-
-    arrived_b = lax.ppermute(sent_b, "exp", across)
-    picked_a = pick(index, spread_a, arrived_a, extra[0])
-    landed_a = exchange(picked_a.reshape(packed_a.shape), devices)
+    arrived_b, sent_c, parts = lax.optimization_barrier((arrived_b, leave(spread_c), parts))
+
+    (extra_c,) = beyond(spread_c)
+    arrived_c = lax.ppermute(sent_c, "exp", across)
+    landed_b = collect(spread_b, arrived_b, extra_b)
     partial = add_up([flip(x, "exp", i) for i, x in zip(steps, parts)])
-    arrived_b, partial = lax.optimization_barrier((arrived_b, partial))
-
-    picked_b = pick(index, spread_b, arrived_b, extra[1])
-    (new_moments_in,) = unpack(exchange(picked_b.reshape(packed_b.shape), devices), chunk_b)
-    new_w_in, new_w_out, new_moments_out = unpack(landed_a, chunk_a)
+    arrived_c, partial = lax.optimization_barrier((arrived_c, partial))
+
+    landed_c = collect(spread_c, arrived_c, extra_c)
     size = tokens.shape[0]
-    mixed = add_up([flip(partial[n * size : (n + 1) * size], "exp", i) for n, i in enumerate(outer)])
+    pieces = [partial[n * size : (n + 1) * size] for n in range(len(outer))]
+    outs_a, pieces[1] = lax.optimization_barrier((unpack(landed_a, chunk_a), pieces[1]))
+    mixed = add_up([flip(x, "exp", i) for i, x in zip(outer, pieces)])
+    new_w_in, new_w_out = outs_a
+    (new_moments_in,) = unpack(landed_b, chunk_b)
+    (new_moments_out,) = unpack(landed_c, chunk_c)
     return mixed, new_w_in, new_w_out, new_moments_in, new_moments_out
 
 

time: 379 us -> 400 us (1.055)
  blocking collectives: 0 us -> 36.7 us
  waiting for transfers between devices: 253 us -> 227 us
  Pallas kernels: 36 us -> 43.3 us
    ppermute x10, waiting for transfers between devices: 179 us -> 88 us  [flip(): lax.ppermute(x, axis, [(d, d ^ bits) for d in range(lax.axis_size(axis))])]
    all_to_all x0 -> x1, blocking collectives: none -> 36.7 us  [swap(): lax.all_to_all(x, axis, split_axis=0, concat_axis=0, axis_index_groups=gr...]
    all_to_all x4 -> x5, waiting for transfers between devices: 42.8 us -> 71.3 us  [swap(): lax.all_to_all(x, axis, split_axis=0, concat_axis=0, axis_index_groups=gr...]
    ppermute x1, waiting for transfers between devices: 28.8 us -> 47.4 us  [on_device(): arrived_b = lax.ppermute(sent_b, 'exp', across)]
    ppermute x1 -> x2, waiting for transfers between devices: 1.1 us -> 15 us  [the longest x1 15 us: on_device(): arrived_c = lax.ppermute(sent_c, 'exp', across)]
    slice x1 -> x4, local copies, waits for them, and re-layouts: 1.16 us -> 7.17 us  [the longest x3 6.01 us: beyond(): extra = [x[:max(held - most, 1)] for x in spreads]]
    pallas_call x4 -> x7, Pallas kernels: 18.6 us -> 24.2 us  [pick(): pl.pallas_call(pick_kernel, in_specs=[pl.BlockSpec(memory_space=pltpu.SME...]
    optimization_barrier x0 -> x3, local copies, waits for them, and re-layouts: none -> 4.81 us  [the longest x1 2.7 us: on_device(): lax.optimization_barrier((spread_out(packed_b), packed_c))]
  transfers between devices with their start and end apart: 18 -> 20, of which waited for: 8 -> 13; matrix products, arithmetic and copies ran while one was open for 5% -> 6% of each run, Pallas kernels for 8% -> 11%
where the time goes in v3:
time: 400 us; the launch traced here: 399 us
  waiting for transfers between devices  227 us (57%)
  Pallas kernels  43.3 us (11%)
  starting transfers between devices  37.3 us (9%)
  blocking collectives  36.7 us (9%)
  local copies, waits for them, and re-layouts  28.5 us (7%)
  between operations  14.4 us (4%)
  other arithmetic  9.58 us (2%)
    ppermute x10, waiting for transfers between devices, flip(): lax.ppermute(x, axis, [(d, d ^ bits) for d in range(lax.axis_size(axis))])  88 us
    all_to_all x5, waiting for transfers between devices, swap(): lax.all_to_all(x, axis, split_axis=0, concat_axis=0, axis_index_groups=gr...  71.3 us
    ppermute x1, waiting for transfers between devices, on_device(): arrived_b = lax.ppermute(sent_b, 'exp', across)  47.4 us
    all_to_all x1, blocking collectives, swap(): lax.all_to_all(x, axis, split_axis=0, concat_axis=0, axis_index_groups=gr...  36.7 us
    pallas_call x7, Pallas kernels, pick(): pl.pallas_call(pick_kernel, in_specs=[pl.BlockSpec(memory_space=pltpu.SME...  24.2 us
    all_to_all x5, starting transfers between devices, swap(): lax.all_to_all(x, axis, split_axis=0, concat_axis=0, axis_index_groups=gr...  20.9 us
    pallas_call x2, Pallas kernels, experts(): pl.pallas_call(expert_kernel, grid=(rows // block,), in_specs=[pl.BlockSp...  19.1 us
    ppermute x1, waiting for transfers between devices, on_device(): arrived_c = lax.ppermute(sent_c, 'exp', across)  15 us
  transfers between devices with their start and end apart: 20, of which 13 were waited for; matrix products, arithmetic and copies ran while one was open for 6% of the time, Pallas kernels for 11%

profile of v3, /device:TPU:0, one launch (start us, length us, event | category | flops | bytes accessed | tf_op | source)
XLA Modules:
  0.0 398.6 jit_solution(16890578386145718213)
XLA Ops:
  11.7 3.1 collective-permute-start.3
  14.8 2.6 collective-permute-start.4
  17.4 1.6 pad_maximum_fusion
  19.0 8.3 %collective-permute-done.3 = bf16[128,1152]{1,0:T(8,128)(2,1)S(1)} collective-permute-done((bf16[128,1152]{1,0:T(8,128)(2,1)S(1)}, bf16[128,1152]{1,0:T(8,128)(2,1)S(1)}, u32[]{:S(2)}, u32[]{:S(2)}) %collective-permute-start.3) | collective-permute-done | bytes 294944 | tf_op jit(solution)/shard_map/ppermute | solution.py:160
  27.3 10.9 %collective-permute-done.4 = bf16[128,1152]{1,0:T(8,128)(2,1)S(1)} collective-permute-done((bf16[128,1152]{1,0:T(8,128)(2,1)S(1)}, bf16[128,1152]{1,0:T(8,128)(2,1)S(1)}, u32[]{:S(2)}, u32[]{:S(2)}) %collective-permute-start.4) | collective-permute-done | bytes 294944 | tf_op jit(solution)/shard_map/ppermute | solution.py:160
  39.0 36.7 %all_to_all.30 = bf16[8,2,72,8,128]{4,3,2,1,0:T(8,128)(2,1)} all-to-all(bf16[8,2,72,8,128]{4,3,2,1,0:T(8,128)(2,1)S(1)} %copy.45), channel_id=1, replica_groups={{0,1,2,3,4,5,6,7},{8,9,10,11,12,13,14,15},{16,17,18,19,20,21,22,23},{24..., dimensions={0} | all-to-all | bytes 4718592 | tf_op jit(solution)/shard_map/all_to_all | solution.py:152
  75.6 2.0 copy.46
  77.6 4.6 %all-to-all-start.1 = ((bf16[8,2,96,8,128]{4,3,2,1,0:T(8,128)(2,1)}), bf16[8,2,96,8,128]{4,3,2,1,0:T(8,128)(2,1)}, u32[]{:S(2)}, u32[]{:S(2)}) async-start(bf16[8,2,96,8,128]{4,3,2,1,0:T(8,128)(2,1)} %copy.46), calls=%async_computation.1 | async-start | bytes 6291456 | tf_op jit(solution)/shard_map/all_to_all | solution.py:152
  83.7 3.6 shard_map.128
  87.3 2.2 collective-permute-start.6
  89.4 1.2 shard_map.130
  90.6 1.9 collective-permute-start.7
  92.6 55.0 %all-to-all-done.1 = bf16[8,2,96,8,128]{4,3,2,1,0:T(8,128)(2,1)} async-done(((bf16[8,2,96,8,128]{4,3,2,1,0:T(8,128)(2,1)}), bf16[8,2,96,8,128]{4,3,2,1,0:T(8,128)(2,1)}, u32[]{:S(2)}, u32[]{:S(2)}) %all-to-all-start.1) | async-done | bytes 3145760 | tf_op jit(solution)/shard_map/all_to_all | solution.py:152
  147.6 2.7 copy.47
  150.3 4.3 %all-to-all-start.2 = ((bf16[8,2,48,8,128]{4,3,2,1,0:T(8,128)(2,1)}), bf16[8,2,48,8,128]{4,3,2,1,0:T(8,128)(2,1)}, u32[]{:S(2)}, u32[]{:S(2)}) async-start(bf16[8,2,48,8,128]{4,3,2,1,0:T(8,128)(2,1)} %copy.47), calls=%async_computation.2 | async-start | bytes 3145728 | tf_op jit(solution)/shard_map/all_to_all | solution.py:152
  156.8 2.2 slice.34
  159.1 3.9 shard_map.129
  164.2 2.6 slice.35
  167.5 5.2 %shard_map.134 = bf16[16,72,8,128]{3,2,1,0:T(8,128)(2,1)S(1)} custom-call(s32[16]{0:T(128)S(1)} %compare_select_fusion.index_ref, bf16[16,72,8,128]{3,2,1,0:T(8,128)(2,1)} %get-tuple-element.500, bf16[9,72,8,128]{3,2,1,0:T(8,128)(2,1)S(1)} %collective-permute-done.6.refs_1_, bf16[7,72,8,128]{3,2,1,0:T(8,128)(2,1)} %get-tuple-element.301.refs_2_), custom_call_target="tpu_custom_call" | custom-call | tf_op jit(solution)/shard_map/pallas_call | solution.py:80
  172.8 1.4 copy-done.1
  174.7 4.6 %all-to-all-start.3 = ((bf16[8,2,72,8,128]{4,3,2,1,0:T(8,128)(2,1)}), bf16[8,2,72,8,128]{4,3,2,1,0:T(8,128)(2,1)}, u32[]{:S(2)}, u32[]{:S(2)}) async-start(bf16[8,2,72,8,128]{4,3,2,1,0:T(8,128)(2,1)} %bitcast.76), calls=%async_computation.3 | async-start | bytes 4718592 | tf_op jit(solution)/shard_map/all_to_all | solution.py:152
  179.4 4.4 %all-gather.5.cloned.1.call-done.refs_1_ = bf16[2,384,1024]{2,1,0:T(8,128)(2,1)} async-done(((bf16[2,192,1024]{2,1,0:T(8,128)(2,1)}), bf16[2,384,1024]{2,1,0:T(8,128)(2,1)}) %all-gather.5.cloned.1.call-update) | async-done | bytes 1572880 | tf_op jit(solution)/shard_map/all_gather | solution.py:227
  183.9 3.7 collective-permute-done.10.refs_3_
  187.5 1.4 copy-done.2
  188.9 1.3 copy-done.4
  190.2 9.4 %shard_map.132 = bf16[512,1024]{1,0:T(8,128)(2,1)S(1)} custom-call(s32[2]{0:T(128)S(1)} %add_multiply_fusion.first_ref, bf16[512,1152]{1,0:T(8,128)(2,1)S(1)} %bitcast.78, bf16[2,1024,768]{2,1,0:T(8,128)(2,1)S(1)} %copy-done, bf16[2,384,1024]{2,1,0:T(8,128)(2,1)S(1)} %copy-done.2, bf16[2,1024,768]{2,1,0:T(8,128)(2,1)} %collective-permute-done.9.refs_2_, ...), custom_call_target="tpu_custom_call" | custom-call | tf_op jit(solution)/shard_map/pallas_call | solution.py:129
  199.6 9.7 %shard_map.133 = bf16[512,1024]{1,0:T(8,128)(2,1)S(1)} custom-call(s32[2]{0:T(128)S(1)} %add_multiply_fusion.first_ref, bf16[512,1152]{1,0:T(8,128)(2,1)} %collective-permute-done.7.x_ref, bf16[2,1024,768]{2,1,0:T(8,128)(2,1)S(1)} %copy-done, bf16[2,384,1024]{2,1,0:T(8,128)(2,1)S(1)} %copy-done.2, bf16[2,1024,768]{2,1,0:T(8,128)(2,1)} %collective-permute-done.9.refs_2_, ...), custom_call_target="tpu_custom_call" | custom-call | tf_op jit(solution)/shard_map/pallas_call | solution.py:129
  209.3 2.7 shard_map.131
  212.0 47.4 %collective-permute-done.8.refs_1_ = bf16[9,96,8,128]{3,2,1,0:T(8,128)(2,1)} collective-permute-done((bf16[9,96,8,128]{3,2,1,0:T(8,128)(2,1)}, bf16[9,96,8,128]{3,2,1,0:T(8,128)(2,1)}, u32[]{:S(2)}, u32[]{:S(2)}) %collective-permute-start.8) | collective-permute-done | bytes 1769504 | tf_op jit(solution)/shard_map/ppermute | solution.py:280
  259.4 1.7 collective-permute-start.12
  262.2 21.7 %collective-permute-done.12 = bf16[512,1024]{1,0:T(8,128)(2,1)S(1)} collective-permute-done((bf16[512,1024]{1,0:T(8,128)(2,1)S(1)}, bf16[512,1024]{1,0:T(8,128)(2,1)S(1)}, u32[]{:S(2)}, u32[]{:S(2)}) %collective-permute-start.12) | collective-permute-done | bytes 1048608 | tf_op jit(solution)/shard_map/ppermute | solution.py:160
  284.0 1.4 add_convert_fusion
  285.4 15.0 %collective-permute-done.11.refs_1_ = bf16[9,48,8,128]{3,2,1,0:T(8,128)(2,1)S(1)} collective-permute-done((bf16[9,48,8,128]{3,2,1,0:T(8,128)(2,1)S(1)}, bf16[9,48,8,128]{3,2,1,0:T(8,128)(2,1)S(1)}, u32[]{:S(2)}, u32[]{:S(2)}) %collective-permute-start.11) | collective-permute-done | bytes 884768 | tf_op jit(solution)/shard_map/ppermute | solution.py:288
  301.1 3.4 shard_map.136
  304.5 3.7 all-to-all-start.5
  308.3 4.2 %shard_map.135 = bf16[16,96,8,128]{3,2,1,0:T(8,128)(2,1)} custom-call(s32[16]{0:T(128)S(1)} %compare_select_fusion.index_ref, bf16[16,96,8,128]{3,2,1,0:T(8,128)(2,1)} %bitcast.19.refs_0_, bf16[9,96,8,128]{3,2,1,0:T(8,128)(2,1)} %collective-permute-done.8.refs_1_, bf16[7,96,8,128]{3,2,1,0:T(8,128)(2,1)S(1)} %copy-done.11), custom_call_target="tpu_custom_call" | custom-call | tf_op jit(solution)/shard_map/pallas_call | solution.py:80
  312.5 15.8 %all-to-all-done.5 = bf16[8,2,48,8,128]{4,3,2,1,0:T(8,128)(2,1)S(1)} async-done(((bf16[8,2,48,8,128]{4,3,2,1,0:T(8,128)(2,1)}), bf16[8,2,48,8,128]{4,3,2,1,0:T(8,128)(2,1)S(1)}, u32[]{:S(2)}, u32[]{:S(2)}) %all-to-all-start.5) | async-done | bytes 1572896 | tf_op jit(solution)/shard_map/all_to_all | solution.py:152
  329.4 3.7 all-to-all-start.4
  334.2 1.5 collective-permute-start.14
  335.7 2.9 collective-permute-start.15
  338.6 1.5 slice.42
  340.1 1.3 copy.52
  343.5 30.2 %collective-permute-done.14 = bf16[128,1024]{1,0:T(8,128)(2,1)S(1)} collective-permute-done((bf16[128,1024]{1,0:T(8,128)(2,1)S(1)}, bf16[128,1024]{1,0:T(8,128)(2,1)S(1)}, u32[]{:S(2)}, u32[]{:S(2)}) %collective-permute-start.14) | collective-permute-done | bytes 262176 | tf_op jit(solution)/shard_map/ppermute | solution.py:160
  373.7 8.8 %collective-permute-done.15 = bf16[128,1024]{1,0:T(8,128)(2,1)S(1)} collective-permute-done((bf16[128,1024]{1,0:T(8,128)(2,1)S(1)}, bf16[128,1024]{1,0:T(8,128)(2,1)S(1)}, u32[]{:S(2)}, u32[]{:S(2)}) %collective-permute-start.15) | collective-permute-done | bytes 262176 | tf_op jit(solution)/shard_map/ppermute | solution.py:160
  382.5 4.3 %collective-permute-done.13 = bf16[128,1024]{1,0:T(8,128)(2,1)S(1)} collective-permute-done((bf16[128,1024]{1,0:T(8,128)(2,1)S(1)}, bf16[128,1024]{1,0:T(8,128)(2,1)S(1)}, u32[]{:S(2)}, u32[]{:S(2)}) %collective-permute-start.13) | collective-permute-done | bytes 262176 | tf_op jit(solution)/shard_map/ppermute | solution.py:160
  386.8 1.8 add_convert_fusion.1
  388.6 1.2 copy.51
  389.9 1.9 copy.50
  (78 shorter events, 17.7 us)
Async XLA Ops:
  7.2 10.2 %copy-start.12 = (bf16[2,192,1024]{2,1,0:T(8,128)(2,1)S(1)}, bf16[2,192,1024]{2,1,0:T(8,128)(2,1)}, u32[]{:S(2)}) copy-start(bf16[2,192,1024]{2,1,0:T(8,128)(2,1)} %param.15) | copy-start | bytes 2359300
  11.7 15.6 %collective-permute-start.3 = (bf16[128,1152]{1,0:T(8,128)(2,1)S(1)}, bf16[128,1152]{1,0:T(8,128)(2,1)S(1)}, u32[]{:S(2)}, u32[]{:S(2)}) collective-permute-start(bf16[128,1152]{1,0:T(8,128)(2,1)S(1)} %concatenate.7), channel_id=1, source_target_pairs={{0,4},{1,5},{2,6},{3,7},{4,0},{5,1},{6,2},{7,3},{8,12},{9,13},{10,... | collective-permute-start | bytes 884744 | tf_op jit(solution)/shard_map/ppermute | solution.py:160
  14.8 23.5 %collective-permute-start.4 = (bf16[128,1152]{1,0:T(8,128)(2,1)S(1)}, bf16[128,1152]{1,0:T(8,128)(2,1)S(1)}, u32[]{:S(2)}, u32[]{:S(2)}) collective-permute-start(bf16[128,1152]{1,0:T(8,128)(2,1)S(1)} %concatenate.7), channel_id=1, source_target_pairs={{0,8},{1,9},{2,10},{3,11},{4,12},{5,13},{6,14},{7,15},{8,0},{9,1},... | collective-permute-start | bytes 884744 | tf_op jit(solution)/shard_map/ppermute | solution.py:160
  17.4 20.9 %collective-permute-start.5 = (bf16[128,1152]{1,0:T(8,128)(2,1)S(1)}, bf16[128,1152]{1,0:T(8,128)(2,1)S(1)}, u32[]{:S(2)}, u32[]{:S(2)}) collective-permute-start(bf16[128,1152]{1,0:T(8,128)(2,1)S(1)} %concatenate.7), channel_id=1, source_target_pairs={{0,12},{1,13},{2,14},{3,15},{4,8},{5,9},{6,10},{7,11},{8,4},{9,5},... | collective-permute-start | bytes 884744 | tf_op jit(solution)/shard_map/ppermute | solution.py:160
  38.2 0.7 copy-start.6
  39.0 36.7 %copy-start.13 = (bf16[2,2,512,768]{3,2,1,0:T(8,128)(2,1)S(1)}, bf16[2,2,512,768]{3,2,1,0:T(8,128)(2,1)}, u32[]{:S(2)}) copy-start(bf16[2,2,512,768]{3,2,1,0:T(8,128)(2,1)} %param.16) | copy-start | bytes 9437188
  77.6 6.0 %copy-start.8 = (bf16[8,2,72,8,128]{4,3,2,1,0:T(8,128)(2,1)S(1)}, bf16[8,2,72,8,128]{4,3,2,1,0:T(8,128)(2,1)}, u32[]{:S(2)}) copy-start(bf16[8,2,72,8,128]{4,3,2,1,0:T(8,128)(2,1)} %all_to_all.30) | copy-start | bytes 7077892
  77.6 70.0 %all-to-all-start.1 = ((bf16[8,2,96,8,128]{4,3,2,1,0:T(8,128)(2,1)}), bf16[8,2,96,8,128]{4,3,2,1,0:T(8,128)(2,1)}, u32[]{:S(2)}, u32[]{:S(2)}) async-start(bf16[8,2,96,8,128]{4,3,2,1,0:T(8,128)(2,1)} %copy.46), calls=%async_computation.1 | async-start | bytes 6291456 | tf_op jit(solution)/shard_map/all_to_all | solution.py:152
  82.2 0.8 copy-start.14
  82.2 0.8 copy-start.15
  82.2 74.2 %all-gather.3.cloned.1.call-start = ((), (), s32[]{:S(2)}) async-start(), calls=%async_computation.6 | async-start | bytes 4718592 | tf_op jit(solution)/shard_map/all_gather | solution.py:226
  83.7 5.8 %copy-start.7 = (bf16[128,1152]{1,0:T(8,128)(2,1)S(1)}, bf16[128,1152]{1,0:T(8,128)(2,1)}, u32[]{:S(2)}) copy-start(bf16[128,1152]{1,0:T(8,128)(2,1)} %copy-done.6) | copy-start | bytes 884740
  87.3 79.6 %collective-permute-start.6 = (bf16[9,72,8,128]{3,2,1,0:T(8,128)(2,1)}, bf16[9,72,8,128]{3,2,1,0:T(8,128)(2,1)S(1)}, u32[]{:S(2)}, u32[]{:S(2)}) collective-permute-start(bf16[9,72,8,128]{3,2,1,0:T(8,128)(2,1)} %shard_map.128), channel_id=1, source_target_pairs={{0,8},{1,9},{2,10},{3,11},{4,12},{5,13},{6,14},{7,15},{8,0},{9,1},... | collective-permute-start | bytes 3981320 | tf_op jit(solution)/shard_map/ppermute | solution.py:270
  90.6 59.7 %copy-start.3 = (bf16[4,128,1152]{2,1,0:T(8,128)(2,1)}, bf16[4,128,1152]{2,1,0:T(8,128)(2,1)S(1)}, u32[]{:S(2)}) copy-start(bf16[4,128,1152]{2,1,0:T(8,128)(2,1)S(1)} %shard_map.130) | copy-start | bytes 3538948
  90.6 76.2 %collective-permute-start.7 = (bf16[512,1152]{1,0:T(8,128)(2,1)S(1)}, bf16[512,1152]{1,0:T(8,128)(2,1)}, u32[]{:S(2)}, u32[]{:S(2)}) collective-permute-start(bf16[512,1152]{1,0:T(8,128)(2,1)S(1)} %bitcast.77), channel_id=1, source_target_pairs={{0,2},{1,3},{2,0},{3,1},{4,6},{5,7},{6,4},{7,5},{8,10},{9,11},{10,... | collective-permute-start | bytes 3538952 | tf_op jit(solution)/shard_map/ppermute | solution.py:160
  150.3 24.4 %all-to-all-start.2 = ((bf16[8,2,48,8,128]{4,3,2,1,0:T(8,128)(2,1)}), bf16[8,2,48,8,128]{4,3,2,1,0:T(8,128)(2,1)}, u32[]{:S(2)}, u32[]{:S(2)}) async-start(bf16[8,2,48,8,128]{4,3,2,1,0:T(8,128)(2,1)} %copy.47), calls=%async_computation.2 | async-start | bytes 3145728 | tf_op jit(solution)/shard_map/all_to_all | solution.py:152
  154.6 29.2 %all-gather.5.cloned.1.call-start = ((), (), s32[]{:S(2)}) async-start(), calls=%async_computation.7 | async-start | bytes 2359296 | tf_op jit(solution)/shard_map/all_gather | solution.py:227
  156.4 31.1 %collective-permute-start.9 = (bf16[2,1024,768]{2,1,0:T(8,128)(2,1)}, bf16[2,1024,768]{2,1,0:T(8,128)(2,1)}, u32[]{:S(2)}, u32[]{:S(2)}) collective-permute-start(bf16[2,1024,768]{2,1,0:T(8,128)(2,1)} %all-gather.3.cloned.1.call-done.refs_0_), channel_id=1, source_target_pairs={{0,1},{1,0},{2,3},{3,2},{4,5},{5,4},{6,7},{7,6},{8,9},{9,8},{10,11... | collective-permute-start | bytes 9437192 | tf_op jit(solution)/shard_map/ppermute | solution.py:160
  163.0 1.2 copy-start.5
  172.8 1.4 copy-start.1
  174.7 12.9 %copy-start = (bf16[2,1024,768]{2,1,0:T(8,128)(2,1)S(1)}, bf16[2,1024,768]{2,1,0:T(8,128)(2,1)}, u32[]{:S(2)}) copy-start(bf16[2,1024,768]{2,1,0:T(8,128)(2,1)} %all-gather.3.cloned.1.call-done.refs_0_) | copy-start | bytes 9437188
  174.7 129.8 %all-to-all-start.3 = ((bf16[8,2,72,8,128]{4,3,2,1,0:T(8,128)(2,1)}), bf16[8,2,72,8,128]{4,3,2,1,0:T(8,128)(2,1)}, u32[]{:S(2)}, u32[]{:S(2)}) async-start(bf16[8,2,72,8,128]{4,3,2,1,0:T(8,128)(2,1)} %bitcast.76), calls=%async_computation.3 | async-start | bytes 4718592 | tf_op jit(solution)/shard_map/all_to_all | solution.py:152
  179.3 80.1 %collective-permute-start.8 = (bf16[9,96,8,128]{3,2,1,0:T(8,128)(2,1)}, bf16[9,96,8,128]{3,2,1,0:T(8,128)(2,1)}, u32[]{:S(2)}, u32[]{:S(2)}) collective-permute-start(bf16[9,96,8,128]{3,2,1,0:T(8,128)(2,1)} %copy-done.5), channel_id=1, source_target_pairs={{0,8},{1,9},{2,10},{3,11},{4,12},{5,13},{6,14},{7,15},{8,0},{9,1},... | collective-permute-start | bytes 5308424 | tf_op jit(solution)/shard_map/ppermute | solution.py:280
  183.8 3.8 collective-permute-start.10
  187.5 1.4 copy-start.2
  188.9 1.3 copy-start.4
  259.4 24.6 %collective-permute-start.12 = (bf16[512,1024]{1,0:T(8,128)(2,1)S(1)}, bf16[512,1024]{1,0:T(8,128)(2,1)S(1)}, u32[]{:S(2)}, u32[]{:S(2)}) collective-permute-start(bf16[512,1024]{1,0:T(8,128)(2,1)S(1)} %shard_map.133), channel_id=1, source_target_pairs={{0,2},{1,3},{2,0},{3,1},{4,6},{5,7},{6,4},{7,5},{8,10},{9,11},{10,... | collective-permute-start | bytes 3145736 | tf_op jit(solution)/shard_map/ppermute | solution.py:160
  261.1 39.3 %collective-permute-start.11 = (bf16[9,48,8,128]{3,2,1,0:T(8,128)(2,1)S(1)}, bf16[9,48,8,128]{3,2,1,0:T(8,128)(2,1)S(1)}, u32[]{:S(2)}, u32[]{:S(2)}) collective-permute-start(bf16[9,48,8,128]{3,2,1,0:T(8,128)(2,1)S(1)} %shard_map.131), channel_id=1, source_target_pairs={{0,8},{1,9},{2,10},{3,11},{4,12},{5,13},{6,14},{7,15},{8,0},{9,1},... | collective-permute-start | bytes 2654216 | tf_op jit(solution)/shard_map/ppermute | solution.py:288
  304.5 3.7 copy-start.11
  304.5 23.7 %all-to-all-start.5 = ((bf16[8,2,48,8,128]{4,3,2,1,0:T(8,128)(2,1)}), bf16[8,2,48,8,128]{4,3,2,1,0:T(8,128)(2,1)S(1)}, u32[]{:S(2)}, u32[]{:S(2)}) async-start(bf16[8,2,48,8,128]{4,3,2,1,0:T(8,128)(2,1)} %bitcast.42), calls=%async_computation.5 | async-start | bytes 3145728 | tf_op jit(solution)/shard_map/all_to_all | solution.py:152
  328.2 1.1 copy-start.9
  329.4 60.5 %all-to-all-start.4 = ((bf16[8,2,96,8,128]{4,3,2,1,0:T(8,128)(2,1)}), bf16[8,2,96,8,128]{4,3,2,1,0:T(8,128)(2,1)S(1)}, u32[]{:S(2)}, u32[]{:S(2)}) async-start(bf16[8,2,96,8,128]{4,3,2,1,0:T(8,128)(2,1)} %bitcast.37), calls=%async_computation.4 | async-start | bytes 6291456 | tf_op jit(solution)/shard_map/all_to_all | solution.py:152
  334.2 39.4 %collective-permute-start.14 = (bf16[128,1024]{1,0:T(8,128)(2,1)S(1)}, bf16[128,1024]{1,0:T(8,128)(2,1)S(1)}, u32[]{:S(2)}, u32[]{:S(2)}) collective-permute-start(bf16[128,1024]{1,0:T(8,128)(2,1)S(1)} %get-tuple-element.335), channel_id=1, source_target_pairs={{0,8},{1,9},{2,10},{3,11},{4,12},{5,13},{6,14},{7,15},{8,0},{9,1},... | collective-permute-start | bytes 786440 | tf_op jit(solution)/shard_map/ppermute | solution.py:160
  335.7 46.8 %collective-permute-start.15 = (bf16[128,1024]{1,0:T(8,128)(2,1)S(1)}, bf16[128,1024]{1,0:T(8,128)(2,1)S(1)}, u32[]{:S(2)}, u32[]{:S(2)}) collective-permute-start(bf16[128,1024]{1,0:T(8,128)(2,1)S(1)} %get-tuple-element.334), channel_id=1, source_target_pairs={{0,12},{1,13},{2,14},{3,15},{4,8},{5,9},{6,10},{7,11},{8,4},{9,5},... | collective-permute-start | bytes 786440 | tf_op jit(solution)/shard_map/ppermute | solution.py:160
  342.5 46.1 %copy-start.10 = (bf16[8,2,48,8,128]{4,3,2,1,0:T(8,128)(2,1)S(1)}, bf16[8,2,48,8,128]{4,3,2,1,0:T(8,128)(2,1)}, u32[]{:S(2)}) copy-start(bf16[8,2,48,8,128]{4,3,2,1,0:T(8,128)(2,1)} %copy-done.9) | copy-start | bytes 4718596
  343.5 43.3 %collective-permute-start.13 = (bf16[128,1024]{1,0:T(8,128)(2,1)S(1)}, bf16[128,1024]{1,0:T(8,128)(2,1)S(1)}, u32[]{:S(2)}, u32[]{:S(2)}) collective-permute-start(bf16[128,1024]{1,0:T(8,128)(2,1)S(1)} %get-tuple-element.302), channel_id=1, source_target_pairs={{0,4},{1,5},{2,6},{3,7},{4,0},{5,1},{6,2},{7,3},{8,12},{9,13},{10,... | collective-permute-start | bytes 786440 | tf_op jit(solution)/shard_map/ppermute | solution.py:160
Sparse Core Ops, SparseCore 0:
  84.6 45.9 all-gather.2
  157.0 26.7 all-gather.4

commit v4 on v3

--- a/solution.py
+++ b/solution.py
@@ -236,9 +236,9 @@
     def spread_out(packed):
         return exchange(packed, devices).reshape((held,) + packed.shape[2:])
 
-    def collect(spread, arrived, extra):
+    def stay(spread, arrived, extra):
         picked = pick(index, spread, arrived, extra)
-        return exchange(picked.reshape((half, slots) + picked.shape[1:]), devices)
+        return picked.reshape((half, slots) + picked.shape[1:])
 
     def beyond(*spreads):
         def more(state):
@@ -278,7 +278,7 @@
 
     extra_a, extra_b = beyond(spread_a, spread_b)
     arrived_b = lax.ppermute(sent_b, "exp", across)
-    landed_a = collect(spread_a, arrived_a, extra_a)
+    landed_a = exchange(stay(spread_a, arrived_a, extra_a), devices)
     me = lax.axis_index("exp").astype(jnp.int32)
     first = jnp.stack([me, me ^ 1]) * slots
     parts = [experts(x, first, weights) for x in blocks]
@@ -286,11 +286,14 @@
 
     (extra_c,) = beyond(spread_c)
     arrived_c = lax.ppermute(sent_c, "exp", across)
-    landed_b = collect(spread_b, arrived_b, extra_b)
+    landed_b = exchange(stay(spread_b, arrived_b, extra_b), devices)
     partial = add_up([flip(x, "exp", i) for i, x in zip(steps, parts)])
     arrived_c, partial = lax.optimization_barrier((arrived_c, partial))
 
-    landed_c = collect(spread_c, arrived_c, extra_c)
+    landed_b, picked_c = lax.optimization_barrier(
+        (landed_b, stay(spread_c, arrived_c, extra_c))
+    )
+    landed_c = exchange(picked_c, devices)
     size = tokens.shape[0]
     pieces = [partial[n * size : (n + 1) * size] for n in range(len(outer))]
     outs_a, pieces[1] = lax.optimization_barrier((unpack(landed_a, chunk_a), pieces[1]))

time: 400 us -> 434 us (1.085)
  waiting for transfers between devices: 227 us -> 271 us
    all_gather x1, waiting for transfers between devices: 0.01 us -> 46.3 us  [on_device(): full_in = lax.all_gather(w_in, 'grp', axis=1, tiled=True)]
    all_to_all x5, waiting for transfers between devices: 71.3 us -> 32.2 us  [swap(): lax.all_to_all(x, axis, split_axis=0, concat_axis=0, axis_index_groups=gr...]
    ppermute x10, waiting for transfers between devices: 88 us -> 121 us  [flip(): lax.ppermute(x, axis, [(d, d ^ bits) for d in range(lax.axis_size(axis))])]
    ppermute x1, waiting for transfers between devices: 0.01 us -> 19.2 us  [on_device(): arrived_a = lax.ppermute(leave(spread_a), 'exp', across)]
    ppermute x1, waiting for transfers between devices: 15 us -> 0.01 us  [on_device(): arrived_c = lax.ppermute(sent_c, 'exp', across)]
    all_gather x1, waiting for transfers between devices: 4.36 us -> 0.01 us  [on_device(): full_out = lax.all_gather(w_out, 'grp', axis=1, tiled=True)]
    unnamed x34 -> x36, local copies, waits for them, and re-layouts: 9.2 us -> 4.89 us
  transfers between devices with their start and end apart: 20 -> 20, of which waited for: 13 -> 11; matrix products, arithmetic and copies ran while one was open for 6% -> 5% of each run, Pallas kernels for 11% -> 8%
where the time goes in v4:
time: 434 us; the launch traced here: 433 us
  waiting for transfers between devices  271 us (62%)
  Pallas kernels  40 us (9%)
  starting transfers between devices  37.4 us (9%)
  blocking collectives  36.6 us (8%)
  local copies, waits for them, and re-layouts  25.3 us (6%)
  between operations  14.4 us (3%)
  other arithmetic  7.6 us (2%)
    ppermute x10, waiting for transfers between devices, flip(): lax.ppermute(x, axis, [(d, d ^ bits) for d in range(lax.axis_size(axis))])  121 us
    ppermute x1, waiting for transfers between devices, on_device(): arrived_b = lax.ppermute(sent_b, 'exp', across)  50.8 us
    all_gather x1, waiting for transfers between devices, on_device(): full_in = lax.all_gather(w_in, 'grp', axis=1, tiled=True)  46.3 us
    all_to_all x1, blocking collectives, swap(): lax.all_to_all(x, axis, split_axis=0, concat_axis=0, axis_index_groups=gr...  36.6 us
    all_to_all x5, waiting for transfers between devices, swap(): lax.all_to_all(x, axis, split_axis=0, concat_axis=0, axis_index_groups=gr...  32.2 us
    pallas_call x7, Pallas kernels, pick(): pl.pallas_call(pick_kernel, in_specs=[pl.BlockSpec(memory_space=pltpu.SME...  22.6 us
    all_to_all x5, starting transfers between devices, swap(): lax.all_to_all(x, axis, split_axis=0, concat_axis=0, axis_index_groups=gr...  21.3 us
    ppermute x1, waiting for transfers between devices, on_device(): arrived_a = lax.ppermute(leave(spread_a), 'exp', across)  19.2 us
  transfers between devices with their start and end apart: 20, of which 11 were waited for; matrix products, arithmetic and copies ran while one was open for 5% of the time, Pallas kernels for 8%

profile of v4, /device:TPU:0, one launch (start us, length us, event | category | flops | bytes accessed | tf_op | source)
XLA Modules:
  0.0 433.2 jit_solution(11141880133223875862)
XLA Ops:
  8.6 0.9 fusion.4
  10.6 1.1 concatenate.7
  11.7 3.1 collective-permute-start.3
  14.8 2.6 collective-permute-start.4
  17.4 1.6 pad_maximum_fusion
  19.0 8.3 %collective-permute-done.3 = bf16[128,1152]{1,0:T(8,128)(2,1)S(1)} collective-permute-done((bf16[128,1152]{1,0:T(8,128)(2,1)S(1)}, bf16[128,1152]{1,0:T(8,128)(2,1)S(1)}, u32[]{:S(2)}, u32[]{:S(2)}) %collective-permute-start.3) | collective-permute-done | bytes 294944 | tf_op jit(solution)/shard_map/ppermute | solution.py:160
  27.3 10.9 %collective-permute-done.4 = bf16[128,1152]{1,0:T(8,128)(2,1)S(1)} collective-permute-done((bf16[128,1152]{1,0:T(8,128)(2,1)S(1)}, bf16[128,1152]{1,0:T(8,128)(2,1)S(1)}, u32[]{:S(2)}, u32[]{:S(2)}) %collective-permute-start.4) | collective-permute-done | bytes 294944 | tf_op jit(solution)/shard_map/ppermute | solution.py:160
  39.1 36.6 %all_to_all.30 = bf16[8,2,72,8,128]{4,3,2,1,0:T(8,128)(2,1)} all-to-all(bf16[8,2,72,8,128]{4,3,2,1,0:T(8,128)(2,1)S(1)} %copy.45), channel_id=1, replica_groups={{0,1,2,3,4,5,6,7},{8,9,10,11,12,13,14,15},{16,17,18,19,20,21,22,23},{24..., dimensions={0} | all-to-all | bytes 4718592 | tf_op jit(solution)/shard_map/all_to_all | solution.py:152
  75.7 2.0 copy.46
  77.6 4.4 %all-to-all-start.1 = ((bf16[8,2,96,8,128]{4,3,2,1,0:T(8,128)(2,1)}), bf16[8,2,96,8,128]{4,3,2,1,0:T(8,128)(2,1)}, u32[]{:S(2)}, u32[]{:S(2)}) async-start(bf16[8,2,96,8,128]{4,3,2,1,0:T(8,128)(2,1)} %copy.46), calls=%async_computation.1 | async-start | bytes 6291456 | tf_op jit(solution)/shard_map/all_to_all | solution.py:152
  84.2 46.3 %all-gather.3.cloned.1.call-done.refs_0_ = bf16[2,1024,768]{2,1,0:T(8,128)(2,1)} async-done(((bf16[2,512,768]{2,1,0:T(8,128)(2,1)}), bf16[2,1024,768]{2,1,0:T(8,128)(2,1)}) %all-gather.3.cloned.1.call-update) | async-done | bytes 3145744 | tf_op jit(solution)/shard_map/all_gather | solution.py:226
  130.6 2.8 shard_map.128
  133.4 2.5 collective-permute-start.6
  135.9 2.0 shard_map.130
  137.9 1.5 collective-permute-start.7
  139.4 2.8 copy.47
  142.2 4.3 all-to-all-start.2
  146.5 2.9 shard_map.129
  149.4 26.1 %collective-permute-done.7.x_ref = bf16[512,1152]{1,0:T(8,128)(2,1)} collective-permute-done((bf16[512,1152]{1,0:T(8,128)(2,1)}, bf16[512,1152]{1,0:T(8,128)(2,1)}, u32[]{:S(2)}, u32[]{:S(2)}) %collective-permute-start.7) | collective-permute-done | bytes 1179680 | tf_op jit(solution)/shard_map/ppermute | solution.py:160
  175.5 19.2 %collective-permute-done.6.refs_1_ = bf16[9,72,8,128]{3,2,1,0:T(8,128)(2,1)} collective-permute-done((bf16[9,72,8,128]{3,2,1,0:T(8,128)(2,1)}, bf16[9,72,8,128]{3,2,1,0:T(8,128)(2,1)}, u32[]{:S(2)}, u32[]{:S(2)}) %collective-permute-start.6) | collective-permute-done | bytes 1327136 | tf_op jit(solution)/shard_map/ppermute | solution.py:270
  195.8 2.4 slice.34
  198.2 2.6 slice.35
  200.9 8.7 %shard_map.132 = bf16[512,1024]{1,0:T(8,128)(2,1)S(1)} custom-call(s32[2]{0:T(128)S(1)} %add_multiply_fusion.first_ref, bf16[512,1152]{1,0:T(8,128)(2,1)} %bitcast.24.x_ref, bf16[2,1024,768]{2,1,0:T(8,128)(2,1)S(1)} %copy-done, bf16[2,384,1024]{2,1,0:T(8,128)(2,1)S(1)} %copy-done.1, bf16[2,1024,768]{2,1,0:T(8,128)(2,1)S(1)} %collective-permute-done.9.refs_2_, ...), custom_call_target="tpu_custom_call" | custom-call | tf_op jit(solution)/shard_map/pallas_call | solution.py:129
  209.6 1.0 copy-done.2
  210.6 8.7 %shard_map.133 = bf16[512,1024]{1,0:T(8,128)(2,1)S(1)} custom-call(s32[2]{0:T(128)S(1)} %add_multiply_fusion.first_ref, bf16[512,1152]{1,0:T(8,128)(2,1)} %collective-permute-done.7.x_ref, bf16[2,1024,768]{2,1,0:T(8,128)(2,1)S(1)} %copy-done, bf16[2,384,1024]{2,1,0:T(8,128)(2,1)S(1)} %copy-done.1, bf16[2,1024,768]{2,1,0:T(8,128)(2,1)S(1)} %collective-permute-done.9.refs_2_, ...), custom_call_target="tpu_custom_call" | custom-call | tf_op jit(solution)/shard_map/pallas_call | solution.py:129
  219.3 1.0 copy-done.4
  220.3 2.9 shard_map.131
  223.2 50.8 %collective-permute-done.8.refs_1_ = bf16[9,96,8,128]{3,2,1,0:T(8,128)(2,1)} collective-permute-done((bf16[9,96,8,128]{3,2,1,0:T(8,128)(2,1)}, bf16[9,96,8,128]{3,2,1,0:T(8,128)(2,1)}, u32[]{:S(2)}, u32[]{:S(2)}) %collective-permute-start.8) | collective-permute-done | bytes 1769504 | tf_op jit(solution)/shard_map/ppermute | solution.py:280
  274.7 4.1 shard_map.135
  278.8 4.5 %all-to-all-start.4 = ((bf16[8,2,96,8,128]{4,3,2,1,0:T(8,128)(2,1)}), bf16[8,2,96,8,128]{4,3,2,1,0:T(8,128)(2,1)}, u32[]{:S(2)}, u32[]{:S(2)}) async-start(bf16[8,2,96,8,128]{4,3,2,1,0:T(8,128)(2,1)} %bitcast.37), calls=%async_computation.4 | async-start | bytes 6291456 | tf_op jit(solution)/shard_map/all_to_all | solution.py:152
  283.3 4.7 %shard_map.134 = bf16[16,72,8,128]{3,2,1,0:T(8,128)(2,1)} custom-call(s32[16]{0:T(128)S(1)} %compare_select_fusion.index_ref, bf16[16,72,8,128]{3,2,1,0:T(8,128)(2,1)S(1)} %get-tuple-element.500, bf16[9,72,8,128]{3,2,1,0:T(8,128)(2,1)} %collective-permute-done.6.refs_1_, bf16[7,72,8,128]{3,2,1,0:T(8,128)(2,1)} %get-tuple-element.303.refs_2_), custom_call_target="tpu_custom_call" | custom-call | tf_op jit(solution)/shard_map/pallas_call | solution.py:80
  288.0 32.2 %all-to-all-done.4 = bf16[8,2,96,8,128]{4,3,2,1,0:T(8,128)(2,1)} async-done(((bf16[8,2,96,8,128]{4,3,2,1,0:T(8,128)(2,1)}), bf16[8,2,96,8,128]{4,3,2,1,0:T(8,128)(2,1)}, u32[]{:S(2)}, u32[]{:S(2)}) %all-to-all-start.4) | async-done | bytes 3145760 | tf_op jit(solution)/shard_map/all_to_all | solution.py:152
  320.2 4.5 %all-to-all-start.3 = ((bf16[8,2,72,8,128]{4,3,2,1,0:T(8,128)(2,1)}), bf16[8,2,72,8,128]{4,3,2,1,0:T(8,128)(2,1)}, u32[]{:S(2)}, u32[]{:S(2)}) async-start(bf16[8,2,72,8,128]{4,3,2,1,0:T(8,128)(2,1)} %bitcast.28), calls=%async_computation.3 | async-start | bytes 4718592 | tf_op jit(solution)/shard_map/all_to_all | solution.py:152
  324.8 1.9 collective-permute-start.12
  326.7 1.1 slice.44
  327.9 47.7 %collective-permute-done.12 = bf16[512,1024]{1,0:T(8,128)(2,1)S(1)} collective-permute-done((bf16[512,1024]{1,0:T(8,128)(2,1)S(1)}, bf16[512,1024]{1,0:T(8,128)(2,1)S(1)}, u32[]{:S(2)}, u32[]{:S(2)}) %collective-permute-start.12) | collective-permute-done | bytes 1048608 | tf_op jit(solution)/shard_map/ppermute | solution.py:160
  376.7 3.2 shard_map.136
  379.9 3.6 all-to-all-start.5
  383.9 4.0 collective-permute-start.15
  387.9 1.5 slice.42
  389.5 1.3 copy.52
  390.7 1.2 slice.43
  391.9 0.9 copy.53
  392.9 14.4 %collective-permute-done.14 = bf16[128,1024]{1,0:T(8,128)(2,1)S(1)} collective-permute-done((bf16[128,1024]{1,0:T(8,128)(2,1)S(1)}, bf16[128,1024]{1,0:T(8,128)(2,1)S(1)}, u32[]{:S(2)}, u32[]{:S(2)}) %collective-permute-start.14) | collective-permute-done | bytes 262176 | tf_op jit(solution)/shard_map/ppermute | solution.py:160
  407.3 7.7 %collective-permute-done.15 = bf16[128,1024]{1,0:T(8,128)(2,1)S(1)} collective-permute-done((bf16[128,1024]{1,0:T(8,128)(2,1)S(1)}, bf16[128,1024]{1,0:T(8,128)(2,1)S(1)}, u32[]{:S(2)}, u32[]{:S(2)}) %collective-permute-start.15) | collective-permute-done | bytes 262176 | tf_op jit(solution)/shard_map/ppermute | solution.py:160
  414.9 5.4 %collective-permute-done.13 = bf16[128,1024]{1,0:T(8,128)(2,1)S(1)} collective-permute-done((bf16[128,1024]{1,0:T(8,128)(2,1)S(1)}, bf16[128,1024]{1,0:T(8,128)(2,1)S(1)}, u32[]{:S(2)}, u32[]{:S(2)}) %collective-permute-start.13) | collective-permute-done | bytes 262176 | tf_op jit(solution)/shard_map/ppermute | solution.py:160
  421.2 3.9 copy.50
  425.1 1.3 copy.51
  (80 shorter events, 9.5 us)
Async XLA Ops:
  7.2 10.2 %copy-start.13 = (bf16[2,192,1024]{2,1,0:T(8,128)(2,1)S(1)}, bf16[2,192,1024]{2,1,0:T(8,128)(2,1)}, u32[]{:S(2)}) copy-start(bf16[2,192,1024]{2,1,0:T(8,128)(2,1)} %param.15) | copy-start | bytes 2359300
  11.7 15.6 %collective-permute-start.3 = (bf16[128,1152]{1,0:T(8,128)(2,1)S(1)}, bf16[128,1152]{1,0:T(8,128)(2,1)S(1)}, u32[]{:S(2)}, u32[]{:S(2)}) collective-permute-start(bf16[128,1152]{1,0:T(8,128)(2,1)S(1)} %concatenate.7), channel_id=1, source_target_pairs={{0,4},{1,5},{2,6},{3,7},{4,0},{5,1},{6,2},{7,3},{8,12},{9,13},{10,... | collective-permute-start | bytes 884744 | tf_op jit(solution)/shard_map/ppermute | solution.py:160
  14.8 23.5 %collective-permute-start.4 = (bf16[128,1152]{1,0:T(8,128)(2,1)S(1)}, bf16[128,1152]{1,0:T(8,128)(2,1)S(1)}, u32[]{:S(2)}, u32[]{:S(2)}) collective-permute-start(bf16[128,1152]{1,0:T(8,128)(2,1)S(1)} %concatenate.7), channel_id=1, source_target_pairs={{0,8},{1,9},{2,10},{3,11},{4,12},{5,13},{6,14},{7,15},{8,0},{9,1},... | collective-permute-start | bytes 884744 | tf_op jit(solution)/shard_map/ppermute | solution.py:160
  17.4 20.9 %collective-permute-start.5 = (bf16[128,1152]{1,0:T(8,128)(2,1)S(1)}, bf16[128,1152]{1,0:T(8,128)(2,1)S(1)}, u32[]{:S(2)}, u32[]{:S(2)}) collective-permute-start(bf16[128,1152]{1,0:T(8,128)(2,1)S(1)} %concatenate.7), channel_id=1, source_target_pairs={{0,12},{1,13},{2,14},{3,15},{4,8},{5,9},{6,10},{7,11},{8,4},{9,5},... | collective-permute-start | bytes 884744 | tf_op jit(solution)/shard_map/ppermute | solution.py:160
  27.3 11.1 %copy-start.6 = (bf16[128,1152]{1,0:T(8,128)(2,1)}, bf16[128,1152]{1,0:T(8,128)(2,1)S(1)}, u32[]{:S(2)}) copy-start(bf16[128,1152]{1,0:T(8,128)(2,1)S(1)} %collective-permute-done.3) | copy-start | bytes 884740
  38.2 0.7 copy-start.8
  38.3 0.8 copy-start.10
  39.1 36.6 %copy-start.14 = (bf16[2,2,512,768]{3,2,1,0:T(8,128)(2,1)S(1)}, bf16[2,2,512,768]{3,2,1,0:T(8,128)(2,1)}, u32[]{:S(2)}) copy-start(bf16[2,2,512,768]{3,2,1,0:T(8,128)(2,1)} %param.16) | copy-start | bytes 9437188
  77.6 61.8 %all-to-all-start.1 = ((bf16[8,2,96,8,128]{4,3,2,1,0:T(8,128)(2,1)}), bf16[8,2,96,8,128]{4,3,2,1,0:T(8,128)(2,1)}, u32[]{:S(2)}, u32[]{:S(2)}) async-start(bf16[8,2,96,8,128]{4,3,2,1,0:T(8,128)(2,1)} %copy.46), calls=%async_computation.1 | async-start | bytes 6291456 | tf_op jit(solution)/shard_map/all_to_all | solution.py:152
  82.1 1.5 copy-start.15
  82.1 1.5 copy-start.16
  82.1 48.4 %all-gather.3.cloned.1.call-start = ((), (), s32[]{:S(2)}) async-start(), calls=%async_computation.6 | async-start | bytes 4718592 | tf_op jit(solution)/shard_map/all_gather | solution.py:226
  82.8 111.8 %all-gather.5.cloned.1.call-start = ((), (), s32[]{:S(2)}) async-start(), calls=%async_computation.7 | async-start | bytes 2359296 | tf_op jit(solution)/shard_map/all_gather | solution.py:227
  130.5 70.4 %collective-permute-start.9 = (bf16[2,1024,768]{2,1,0:T(8,128)(2,1)}, bf16[2,1024,768]{2,1,0:T(8,128)(2,1)S(1)}, u32[]{:S(2)}, u32[]{:S(2)}) collective-permute-start(bf16[2,1024,768]{2,1,0:T(8,128)(2,1)} %all-gather.3.cloned.1.call-done.refs_0_), channel_id=1, source_target_pairs={{0,1},{1,0},{2,3},{3,2},{4,5},{5,4},{6,7},{7,6},{8,9},{9,8},{10,11... | collective-permute-start | bytes 9437192 | tf_op jit(solution)/shard_map/ppermute | solution.py:160
  130.6 5.3 %copy-start.7 = (bf16[128,1152]{1,0:T(8,128)(2,1)S(1)}, bf16[128,1152]{1,0:T(8,128)(2,1)}, u32[]{:S(2)}) copy-start(bf16[128,1152]{1,0:T(8,128)(2,1)} %copy-done.6) | copy-start | bytes 884740
  130.6 5.3 %copy-start.9 = (bf16[128,1152]{1,0:T(8,128)(2,1)S(1)}, bf16[128,1152]{1,0:T(8,128)(2,1)}, u32[]{:S(2)}) copy-start(bf16[128,1152]{1,0:T(8,128)(2,1)} %copy-done.8) | copy-start | bytes 884740
  130.6 5.3 %copy-start.11 = (bf16[128,1152]{1,0:T(8,128)(2,1)S(1)}, bf16[128,1152]{1,0:T(8,128)(2,1)}, u32[]{:S(2)}) copy-start(bf16[128,1152]{1,0:T(8,128)(2,1)} %copy-done.10) | copy-start | bytes 884740
  133.4 61.3 %collective-permute-start.6 = (bf16[9,72,8,128]{3,2,1,0:T(8,128)(2,1)}, bf16[9,72,8,128]{3,2,1,0:T(8,128)(2,1)}, u32[]{:S(2)}, u32[]{:S(2)}) collective-permute-start(bf16[9,72,8,128]{3,2,1,0:T(8,128)(2,1)} %shard_map.128), channel_id=1, source_target_pairs={{0,8},{1,9},{2,10},{3,11},{4,12},{5,13},{6,14},{7,15},{8,0},{9,1},... | collective-permute-start | bytes 3981320 | tf_op jit(solution)/shard_map/ppermute | solution.py:270
  137.9 37.6 %collective-permute-start.7 = (bf16[512,1152]{1,0:T(8,128)(2,1)}, bf16[512,1152]{1,0:T(8,128)(2,1)}, u32[]{:S(2)}, u32[]{:S(2)}) collective-permute-start(bf16[512,1152]{1,0:T(8,128)(2,1)} %bitcast.24.x_ref), channel_id=1, source_target_pairs={{0,2},{1,3},{2,0},{3,1},{4,6},{5,7},{6,4},{7,5},{8,10},{9,11},{10,... | collective-permute-start | bytes 3538952 | tf_op jit(solution)/shard_map/ppermute | solution.py:160
  142.2 78.1 %all-to-all-start.2 = ((bf16[8,2,48,8,128]{4,3,2,1,0:T(8,128)(2,1)}), bf16[8,2,48,8,128]{4,3,2,1,0:T(8,128)(2,1)}, u32[]{:S(2)}, u32[]{:S(2)}) async-start(bf16[8,2,48,8,128]{4,3,2,1,0:T(8,128)(2,1)} %copy.47), calls=%async_computation.2 | async-start | bytes 3145728 | tf_op jit(solution)/shard_map/all_to_all | solution.py:152
  194.7 79.4 %collective-permute-start.8 = (bf16[9,96,8,128]{3,2,1,0:T(8,128)(2,1)}, bf16[9,96,8,128]{3,2,1,0:T(8,128)(2,1)}, u32[]{:S(2)}, u32[]{:S(2)}) collective-permute-start(bf16[9,96,8,128]{3,2,1,0:T(8,128)(2,1)} %shard_map.129), channel_id=1, source_target_pairs={{0,8},{1,9},{2,10},{3,11},{4,12},{5,13},{6,14},{7,15},{8,0},{9,1},... | collective-permute-start | bytes 5308424 | tf_op jit(solution)/shard_map/ppermute | solution.py:280
  194.7 6.2 %collective-permute-start.10 = (bf16[2,384,1024]{2,1,0:T(8,128)(2,1)}, bf16[2,384,1024]{2,1,0:T(8,128)(2,1)}, u32[]{:S(2)}, u32[]{:S(2)}) collective-permute-start(bf16[2,384,1024]{2,1,0:T(8,128)(2,1)} %all-gather.5.cloned.1.call-done.refs_1_), channel_id=1, source_target_pairs={{0,1},{1,0},{2,3},{3,2},{4,5},{5,4},{6,7},{7,6},{8,9},{9,8},{10,11... | collective-permute-start | bytes 4718600 | tf_op jit(solution)/shard_map/ppermute | solution.py:160
  195.8 5.1 %copy-start = (bf16[2,1024,768]{2,1,0:T(8,128)(2,1)S(1)}, bf16[2,1024,768]{2,1,0:T(8,128)(2,1)}, u32[]{:S(2)}) copy-start(bf16[2,1024,768]{2,1,0:T(8,128)(2,1)} %all-gather.3.cloned.1.call-done.refs_0_) | copy-start | bytes 9437188
  198.2 2.6 copy-start.1
  209.6 1.1 copy-start.2
  219.3 1.0 copy-start.4
  220.3 53.7 %copy-start.12 = (bf16[8,2,72,8,128]{4,3,2,1,0:T(8,128)(2,1)S(1)}, bf16[8,2,72,8,128]{4,3,2,1,0:T(8,128)(2,1)}, u32[]{:S(2)}) copy-start(bf16[8,2,72,8,128]{4,3,2,1,0:T(8,128)(2,1)} %all_to_all.30) | copy-start | bytes 7077892
  278.8 41.4 %all-to-all-start.4 = ((bf16[8,2,96,8,128]{4,3,2,1,0:T(8,128)(2,1)}), bf16[8,2,96,8,128]{4,3,2,1,0:T(8,128)(2,1)}, u32[]{:S(2)}, u32[]{:S(2)}) async-start(bf16[8,2,96,8,128]{4,3,2,1,0:T(8,128)(2,1)} %bitcast.37), calls=%async_computation.4 | async-start | bytes 6291456 | tf_op jit(solution)/shard_map/all_to_all | solution.py:152
  320.2 4.5 %copy-start.5 = (bf16[512,1024]{1,0:T(8,128)(2,1)S(1)}, bf16[512,1024]{1,0:T(8,128)(2,1)}, u32[]{:S(2)}) copy-start(bf16[512,1024]{1,0:T(8,128)(2,1)} %copy-done.4) | copy-start | bytes 3145732
  320.2 59.7 %all-to-all-start.3 = ((bf16[8,2,72,8,128]{4,3,2,1,0:T(8,128)(2,1)}), bf16[8,2,72,8,128]{4,3,2,1,0:T(8,128)(2,1)}, u32[]{:S(2)}, u32[]{:S(2)}) async-start(bf16[8,2,72,8,128]{4,3,2,1,0:T(8,128)(2,1)} %bitcast.28), calls=%async_computation.3 | async-start | bytes 4718592 | tf_op jit(solution)/shard_map/all_to_all | solution.py:152
  324.8 50.8 %copy-start.3 = (bf16[512,1024]{1,0:T(8,128)(2,1)S(1)}, bf16[512,1024]{1,0:T(8,128)(2,1)}, u32[]{:S(2)}) copy-start(bf16[512,1024]{1,0:T(8,128)(2,1)} %copy-done.2) | copy-start | bytes 3145732
  324.8 50.8 %collective-permute-start.12 = (bf16[512,1024]{1,0:T(8,128)(2,1)S(1)}, bf16[512,1024]{1,0:T(8,128)(2,1)S(1)}, u32[]{:S(2)}, u32[]{:S(2)}) collective-permute-start(bf16[512,1024]{1,0:T(8,128)(2,1)S(1)} %copy-done.5), channel_id=1, source_target_pairs={{0,2},{1,3},{2,0},{3,1},{4,6},{5,7},{6,4},{7,5},{8,10},{9,11},{10,... | collective-permute-start | bytes 3145736 | tf_op jit(solution)/shard_map/ppermute | solution.py:160
  326.7 49.3 %collective-permute-start.11 = (bf16[9,48,8,128]{3,2,1,0:T(8,128)(2,1)S(1)}, bf16[9,48,8,128]{3,2,1,0:T(8,128)(2,1)S(1)}, u32[]{:S(2)}, u32[]{:S(2)}) collective-permute-start(bf16[9,48,8,128]{3,2,1,0:T(8,128)(2,1)S(1)} %shard_map.131), channel_id=1, source_target_pairs={{0,8},{1,9},{2,10},{3,11},{4,12},{5,13},{6,14},{7,15},{8,0},{9,1},... | collective-permute-start | bytes 2654216 | tf_op jit(solution)/shard_map/ppermute | solution.py:288
  379.9 45.2 %all-to-all-start.5 = ((bf16[8,2,48,8,128]{4,3,2,1,0:T(8,128)(2,1)}), bf16[8,2,48,8,128]{4,3,2,1,0:T(8,128)(2,1)S(1)}, u32[]{:S(2)}, u32[]{:S(2)}) async-start(bf16[8,2,48,8,128]{4,3,2,1,0:T(8,128)(2,1)} %bitcast.38), calls=%async_computation.5 | async-start | bytes 3145728 | tf_op jit(solution)/shard_map/all_to_all | solution.py:152
  383.6 23.7 %collective-permute-start.14 = (bf16[128,1024]{1,0:T(8,128)(2,1)S(1)}, bf16[128,1024]{1,0:T(8,128)(2,1)S(1)}, u32[]{:S(2)}, u32[]{:S(2)}) collective-permute-start(bf16[128,1024]{1,0:T(8,128)(2,1)S(1)} %get-tuple-element.339), channel_id=1, source_target_pairs={{0,8},{1,9},{2,10},{3,11},{4,12},{5,13},{6,14},{7,15},{8,0},{9,1},... | collective-permute-start | bytes 786440 | tf_op jit(solution)/shard_map/ppermute | solution.py:160
  383.9 31.0 %collective-permute-start.15 = (bf16[128,1024]{1,0:T(8,128)(2,1)S(1)}, bf16[128,1024]{1,0:T(8,128)(2,1)S(1)}, u32[]{:S(2)}, u32[]{:S(2)}) collective-permute-start(bf16[128,1024]{1,0:T(8,128)(2,1)S(1)} %get-tuple-element.338), channel_id=1, source_target_pairs={{0,12},{1,13},{2,14},{3,15},{4,8},{5,9},{6,10},{7,11},{8,4},{9,5},... | collective-permute-start | bytes 786440 | tf_op jit(solution)/shard_map/ppermute | solution.py:160
  392.8 27.5 %collective-permute-start.13 = (bf16[128,1024]{1,0:T(8,128)(2,1)S(1)}, bf16[128,1024]{1,0:T(8,128)(2,1)S(1)}, u32[]{:S(2)}, u32[]{:S(2)}) collective-permute-start(bf16[128,1024]{1,0:T(8,128)(2,1)S(1)} %get-tuple-element.304), channel_id=1, source_target_pairs={{0,4},{1,5},{2,6},{3,7},{4,0},{5,1},{6,2},{7,3},{8,12},{9,13},{10,... | collective-permute-start | bytes 786440 | tf_op jit(solution)/shard_map/ppermute | solution.py:160
Sparse Core Ops, SparseCore 0:
  84.5 45.9 all-gather.2
  132.0 27.2 all-gather.4

commit v5 on v1

--- a/solution.py
+++ b/solution.py
@@ -91,6 +91,11 @@
         compiler_params=pltpu.CompilerParams(vmem_limit_bytes=16 * 1024 * 1024),
         cost_estimate=pl.CostEstimate(flops=0, bytes_accessed=0, transcendentals=0),
     )(index, *tables)
+
+
+def lay(blocks):
+    laid = pick(jnp.arange(len(blocks), dtype=jnp.int32), *(x[None] for x in blocks))
+    return laid.reshape((-1,) + blocks[0].shape[1:])
 
 
 def expert_kernel(first_ref, x_ref, *refs):
@@ -222,12 +227,12 @@
     full_out = lax.all_gather(w_out, "grp", axis=1, tiled=True)
 
     rows = weighted_rows(tokens, expert_ids, route_weights, old_plan)
-    rows, *firsts = lax.optimization_barrier((rows, *chunk_a))
     inner = plane_size(devices)
     outer = range(0, devices, inner)
     column = [flip(rows, "exp", i) for i in outer]
-    packed_a = pack(firsts, half)
+    packed_a, column = lax.optimization_barrier((pack(chunk_a, half), column))
     spread_a = exchange(packed_a, devices).reshape((held,) + packed_a.shape[2:])
+    rows = lay(column)
 
     *plan, number = crossing(old_plan, new_plan)
     most = -(-held * FIXED // 16)
@@ -239,9 +244,7 @@
     packed_b = pack(chunk_b, half)
     spread_b = exchange(packed_b, devices).reshape((held,) + packed_b.shape[2:])
     sent_b = pick(sent_index[:most], spread_b)
-    column, _ = lax.optimization_barrier((column, sent_a))
     steps = range(0, inner, 2)
-    rows = jnp.concatenate(column, axis=0)
     blocks = [flip(rows, "exp", i) for i in steps]
     weights = [full_in, full_out, flip(full_in, "exp", 1), flip(full_out, "exp", 1)]
     me = lax.axis_index("exp").astype(jnp.int32)
@@ -259,10 +262,10 @@
             out.append(lax.dynamic_update_slice_in_dim(table, row, place - most, axis=0))
         return place + 1, *out
 
-    arrived_a, sent_b, parts = lax.optimization_barrier((arrived_a, sent_b, parts))
     extra = [
         jnp.zeros((max(held - most, 1),) + x.shape[1:], x.dtype) for x in (spread_a, spread_b)
     ]
+    arrived_a, sent_b, parts, extra = lax.optimization_barrier((arrived_a, sent_b, parts, extra))
     _, *extra = lax.while_loop(
         lambda state: state[0] < number, more, (jnp.int32(most), *extra)
     )
@@ -275,9 +278,11 @@
 
     picked_b = pick(index, spread_b, arrived_b, extra[1])
     (new_moments_in,) = unpack(exchange(picked_b.reshape(packed_b.shape), devices), chunk_b)
-    new_w_in, new_w_out, new_moments_out = unpack(landed_a, chunk_a)
     size = tokens.shape[0]
-    mixed = add_up([flip(partial[n * size : (n + 1) * size], "exp", i) for n, i in enumerate(outer)])
+    pieces = [partial[n * size : (n + 1) * size] for n in range(len(outer))]
+    outs_a, pieces[1] = lax.optimization_barrier((unpack(landed_a, chunk_a), pieces[1]))
+    new_w_in, new_w_out, new_moments_out = outs_a
+    mixed = add_up([flip(x, "exp", i) for i, x in zip(outer, pieces)])
     return mixed, new_w_in, new_w_out, new_moments_in, new_moments_out
 
 

time: 379 us -> 377 us (level)
  waiting for transfers between devices: 253 us -> 243 us
  starting transfers between devices: 36.1 us -> 42.8 us
    ppermute x10, waiting for transfers between devices: 179 us -> 112 us  [flip(): lax.ppermute(x, axis, [(d, d ^ bits) for d in range(lax.axis_size(axis))])]
    all_to_all x4, waiting for transfers between devices: 42.8 us -> 70.5 us  [swap(): lax.all_to_all(x, axis, split_axis=0, concat_axis=0, axis_index_groups=gr...]
    all_gather x1, waiting for transfers between devices: 0.01 us -> 23.5 us  [on_device(): full_out = lax.all_gather(w_out, 'grp', axis=1, tiled=True)]
    ppermute x1, waiting for transfers between devices: 1.1 us -> 6.07 us  [on_device(): arrived_a = lax.ppermute(sent_a, 'exp', across)]
    concatenate x2 -> x0, local copies, waits for them, and re-layouts: 3.83 us -> none  [the longest x1 2.13 us: pack(): return jnp.concatenate([in_parts(t, parts) for t in tiles], axis=2)]
    pallas_call x4 -> x5, Pallas kernels: 18.6 us -> 20.7 us  [pick(): pl.pallas_call(pick_kernel, in_specs=[pl.BlockSpec(memory_space=pltpu.SME...]
    unnamed x30 -> x39, local copies, waits for them, and re-layouts: 12.7 us -> 13.5 us
  transfers between devices with their start and end apart: 18 -> 18, of which waited for: 8 -> 12; matrix products, arithmetic and copies ran while one was open for 5% -> 5% of each run, Pallas kernels for 8% -> 8%
where the time goes in v5:
time: 377 us; the launch traced here: 376 us
  waiting for transfers between devices  243 us (64%)
  starting transfers between devices  42.8 us (11%)
  Pallas kernels  38.1 us (10%)
  local copies, waits for them, and re-layouts  27 us (7%)
  between operations  14.3 us (4%)
  other arithmetic  10.1 us (3%)
    ppermute x10, waiting for transfers between devices, flip(): lax.ppermute(x, axis, [(d, d ^ bits) for d in range(lax.axis_size(axis))])  112 us
    all_to_all x4, waiting for transfers between devices, swap(): lax.all_to_all(x, axis, split_axis=0, concat_axis=0, axis_index_groups=gr...  70.5 us
    ppermute x1, waiting for transfers between devices, on_device(): arrived_b = lax.ppermute(sent_b, 'exp', across)  28.9 us
    all_gather x1, waiting for transfers between devices, on_device(): full_out = lax.all_gather(w_out, 'grp', axis=1, tiled=True)  23.5 us
    all_to_all x4, starting transfers between devices, swap(): lax.all_to_all(x, axis, split_axis=0, concat_axis=0, axis_index_groups=gr...  23.1 us
    pallas_call x5, Pallas kernels, pick(): pl.pallas_call(pick_kernel, in_specs=[pl.BlockSpec(memory_space=pltpu.SME...  20.7 us
    pallas_call x2, Pallas kernels, experts(): pl.pallas_call(expert_kernel, grid=(rows // block,), in_specs=[pl.BlockSp...  17.4 us
    ppermute x10, starting transfers between devices, flip(): lax.ppermute(x, axis, [(d, d ^ bits) for d in range(lax.axis_size(axis))])  14.1 us
  transfers between devices with their start and end apart: 18, of which 12 were waited for; matrix products, arithmetic and copies ran while one was open for 5% of the time, Pallas kernels for 8%

profile of v5, /device:TPU:0, one launch (start us, length us, event | category | flops | bytes accessed | tf_op | source)
XLA Modules:
  0.0 375.8 jit_solution(14448609663517251553)
XLA Ops:
  10.5 1.1 concatenate.7
  11.6 3.1 collective-permute-start.2
  14.7 2.6 collective-permute-start.3
  17.3 2.3 pad_maximum_fusion
  19.6 7.7 %collective-permute-done.2 = bf16[128,1152]{1,0:T(8,128)(2,1)S(1)} collective-permute-done((bf16[128,1152]{1,0:T(8,128)(2,1)S(1)}, bf16[128,1152]{1,0:T(8,128)(2,1)S(1)}, u32[]{:S(2)}, u32[]{:S(2)}) %collective-permute-start.2) | collective-permute-done | bytes 294944 | tf_op jit(solution)/shard_map/ppermute | solution.py:160
  28.0 10.2 %collective-permute-done.3 = bf16[128,1152]{1,0:T(8,128)(2,1)S(1)} collective-permute-done((bf16[128,1152]{1,0:T(8,128)(2,1)S(1)}, bf16[128,1152]{1,0:T(8,128)(2,1)S(1)}, u32[]{:S(2)}, u32[]{:S(2)}) %collective-permute-start.3) | collective-permute-done | bytes 294944 | tf_op jit(solution)/shard_map/ppermute | solution.py:160
  39.6 2.1 copy.41
  41.7 7.2 %all-to-all-start = ((bf16[8,2,120,8,128]{4,3,2,1,0:T(8,128)(2,1)}), bf16[8,2,120,8,128]{4,3,2,1,0:T(8,128)(2,1)}, u32[]{:S(2)}, u32[]{:S(2)}) async-start(bf16[8,2,120,8,128]{4,3,2,1,0:T(8,128)(2,1)} %copy.41), calls=%async_computation | async-start | bytes 7864320 | tf_op jit(solution)/shard_map/all_to_all | solution.py:152
  49.7 1.9 copy.42
  51.6 42.8 %all-to-all-done = bf16[8,2,120,8,128]{4,3,2,1,0:T(8,128)(2,1)} async-done(((bf16[8,2,120,8,128]{4,3,2,1,0:T(8,128)(2,1)}), bf16[8,2,120,8,128]{4,3,2,1,0:T(8,128)(2,1)}, u32[]{:S(2)}, u32[]{:S(2)}) %all-to-all-start) | async-done | bytes 3932192 | tf_op jit(solution)/shard_map/all_to_all | solution.py:152
  94.4 4.5 %all-to-all-start.1 = ((bf16[8,2,96,8,128]{4,3,2,1,0:T(8,128)(2,1)}), bf16[8,2,96,8,128]{4,3,2,1,0:T(8,128)(2,1)}, u32[]{:S(2)}, u32[]{:S(2)}) async-start(bf16[8,2,96,8,128]{4,3,2,1,0:T(8,128)(2,1)} %copy.42), calls=%async_computation.1 | async-start | bytes 6291456 | tf_op jit(solution)/shard_map/all_to_all | solution.py:152
  100.8 3.2 shard_map.128
  104.0 3.3 collective-permute-start.5
  107.3 23.5 %all-gather.5.cloned.1.call-done.refs_1_ = bf16[2,384,1024]{2,1,0:T(8,128)(2,1)} async-done(((bf16[2,192,1024]{2,1,0:T(8,128)(2,1)}), bf16[2,384,1024]{2,1,0:T(8,128)(2,1)}) %all-gather.5.cloned.1.call-update) | async-done | bytes 1572880 | tf_op jit(solution)/shard_map/all_gather | solution.py:227
  130.8 1.0 copy-done.9
  133.7 2.0 shard_map.129
  135.6 1.5 collective-permute-start.6
  138.2 27.7 %all-to-all-done.1 = bf16[8,2,96,8,128]{4,3,2,1,0:T(8,128)(2,1)} async-done(((bf16[8,2,96,8,128]{4,3,2,1,0:T(8,128)(2,1)}), bf16[8,2,96,8,128]{4,3,2,1,0:T(8,128)(2,1)}, u32[]{:S(2)}, u32[]{:S(2)}) %all-to-all-start.1) | async-done | bytes 3145760 | tf_op jit(solution)/shard_map/all_to_all | solution.py:152
  165.9 4.2 %shard_map.130 = bf16[9,96,8,128]{3,2,1,0:T(8,128)(2,1)S(1)} custom-call(s32[9]{0:T(128)S(1)} %bitcast.85, bf16[16,96,8,128]{3,2,1,0:T(8,128)(2,1)} %bitcast.23.refs_0_), custom_call_target="tpu_custom_call" | custom-call | tf_op jit(solution)/shard_map/pallas_call | solution.py:80
  170.1 1.2 copy-done.5
  171.3 6.7 %collective-permute-done.6.x_ref = bf16[512,1152]{1,0:T(8,128)(2,1)} collective-permute-done((bf16[512,1152]{1,0:T(8,128)(2,1)}, bf16[512,1152]{1,0:T(8,128)(2,1)}, u32[]{:S(2)}, u32[]{:S(2)}) %collective-permute-start.6) | collective-permute-done | bytes 1179680 | tf_op jit(solution)/shard_map/ppermute | solution.py:160
  178.0 8.7 %shard_map.131 = bf16[512,1024]{1,0:T(8,128)(2,1)S(1)} custom-call(s32[2]{0:T(128)S(1)} %add_multiply_fusion.first_ref, bf16[512,1152]{1,0:T(8,128)(2,1)} %bitcast.18.x_ref, bf16[2,1024,768]{2,1,0:T(8,128)(2,1)S(1)} %copy-done.1, bf16[2,384,1024]{2,1,0:T(8,128)(2,1)S(1)} %copy-done.2, bf16[2,1024,768]{2,1,0:T(8,128)(2,1)S(1)} %collective-permute-done.7.refs_2_, ...), custom_call_target="tpu_custom_call" | custom-call | tf_op jit(solution)/shard_map/pallas_call | solution.py:129
  187.7 8.7 %shard_map.132 = bf16[512,1024]{1,0:T(8,128)(2,1)S(1)} custom-call(s32[2]{0:T(128)S(1)} %add_multiply_fusion.first_ref, bf16[512,1152]{1,0:T(8,128)(2,1)} %collective-permute-done.6.x_ref, bf16[2,1024,768]{2,1,0:T(8,128)(2,1)S(1)} %copy-done.1, bf16[2,384,1024]{2,1,0:T(8,128)(2,1)S(1)} %copy-done.2, ...), custom_call_target="tpu_custom_call" | custom-call | tf_op jit(solution)/shard_map/pallas_call | solution.py:129
  196.4 1.0 copy-done.7
  197.4 6.1 %collective-permute-done.5.refs_1_ = bf16[9,120,8,128]{3,2,1,0:T(8,128)(2,1)} collective-permute-done((bf16[9,120,8,128]{3,2,1,0:T(8,128)(2,1)}, bf16[9,120,8,128]{3,2,1,0:T(8,128)(2,1)}, u32[]{:S(2)}, u32[]{:S(2)}) %collective-permute-start.5) | collective-permute-done | bytes 2211872 | tf_op jit(solution)/shard_map/ppermute | solution.py:243
  203.7 1.3 broadcast_in_dim.118
  205.6 6.8 %shard_map.133 = bf16[16,120,8,128]{3,2,1,0:T(8,128)(2,1)S(1)} custom-call(s32[16]{0:T(128)S(1)} %compare_select_fusion.index_ref, bf16[16,120,8,128]{3,2,1,0:T(8,128)(2,1)} %bitcast.13.refs_0_, bf16[9,120,8,128]{3,2,1,0:T(8,128)(2,1)} %collective-permute-done.5.refs_1_, bf16[7,120,8,128]{3,2,1,0:T(8,128)(2,1)S(1)} %get-tuple-element.185.refs_2_), custom_call_target="tpu_custom_call" | custom-call | tf_op jit(solution)/shard_map/pallas_call | solution.py:80
  212.4 1.9 copy-done
  214.3 4.8 %all-to-all-start.2 = ((bf16[8,2,120,8,128]{4,3,2,1,0:T(8,128)(2,1)}), bf16[8,2,120,8,128]{4,3,2,1,0:T(8,128)(2,1)}, u32[]{:S(2)}, u32[]{:S(2)}) async-start(bf16[8,2,120,8,128]{4,3,2,1,0:T(8,128)(2,1)} %bitcast.71), calls=%async_computation.2 | async-start | bytes 7864320 | tf_op jit(solution)/shard_map/all_to_all | solution.py:152
  219.1 2.3 collective-permute-start.9
  221.4 2.0 collective-permute-start.10
  223.4 46.6 %collective-permute-done.10 = bf16[512,1024]{1,0:T(8,128)(2,1)S(1)} collective-permute-done((bf16[512,1024]{1,0:T(8,128)(2,1)}, bf16[512,1024]{1,0:T(8,128)(2,1)S(1)}, u32[]{:S(2)}, u32[]{:S(2)}) %collective-permute-start.10) | collective-permute-done | bytes 1048608 | tf_op jit(solution)/shard_map/ppermute | solution.py:160
  270.0 1.4 add_convert_fusion
  271.3 28.9 %collective-permute-done.9.refs_1_ = bf16[9,96,8,128]{3,2,1,0:T(8,128)(2,1)S(1)} collective-permute-done((bf16[9,96,8,128]{3,2,1,0:T(8,128)(2,1)S(1)}, bf16[9,96,8,128]{3,2,1,0:T(8,128)(2,1)S(1)}, u32[]{:S(2)}, u32[]{:S(2)}) %collective-permute-start.9) | collective-permute-done | bytes 1769504 | tf_op jit(solution)/shard_map/ppermute | solution.py:273
  300.2 4.6 %shard_map.134 = bf16[16,96,8,128]{3,2,1,0:T(8,128)(2,1)} custom-call(s32[16]{0:T(128)S(1)} %compare_select_fusion.index_ref, bf16[16,96,8,128]{3,2,1,0:T(8,128)(2,1)} %bitcast.23.refs_0_, bf16[9,96,8,128]{3,2,1,0:T(8,128)(2,1)S(1)} %collective-permute-done.9.refs_1_, bf16[7,96,8,128]{3,2,1,0:T(8,128)(2,1)S(1)} %copy-done.14), custom_call_target="tpu_custom_call" | custom-call | tf_op jit(solution)/shard_map/pallas_call | solution.py:80
  304.8 6.6 %all-to-all-start.3 = ((bf16[8,2,96,8,128]{4,3,2,1,0:T(8,128)(2,1)}), bf16[8,2,96,8,128]{4,3,2,1,0:T(8,128)(2,1)S(1)}, u32[]{:S(2)}, u32[]{:S(2)}) async-start(bf16[8,2,96,8,128]{4,3,2,1,0:T(8,128)(2,1)} %bitcast.39), calls=%async_computation.3 | async-start | bytes 6291456 | tf_op jit(solution)/shard_map/all_to_all | solution.py:152
  311.4 1.2 fusion.7
  312.6 2.3 collective-permute-start.13
  314.9 1.2 collective-permute-start.12
  316.1 2.2 fusion.6
  318.3 1.3 copy.47
  319.6 1.2 slice.34
  321.7 1.3 copy.49
  323.9 30.8 %collective-permute-done.13 = bf16[128,1024]{1,0:T(8,128)(2,1)S(1)} collective-permute-done((bf16[128,1024]{1,0:T(8,128)(2,1)S(1)}, bf16[128,1024]{1,0:T(8,128)(2,1)S(1)}, u32[]{:S(2)}, u32[]{:S(2)}) %collective-permute-start.13) | collective-permute-done | bytes 262176 | tf_op jit(solution)/shard_map/ppermute | solution.py:160
  354.7 3.0 collective-permute-done.12
  357.7 7.6 %collective-permute-done.11 = bf16[128,1024]{1,0:T(8,128)(2,1)S(1)} collective-permute-done((bf16[128,1024]{1,0:T(8,128)(2,1)S(1)}, bf16[128,1024]{1,0:T(8,128)(2,1)S(1)}, u32[]{:S(2)}, u32[]{:S(2)}) %collective-permute-start.11) | collective-permute-done | bytes 262176 | tf_op jit(solution)/shard_map/ppermute | solution.py:160
  365.2 1.8 add_convert_fusion.1
  367.1 1.9 copy.46
  (72 shorter events, 14.7 us)
Async XLA Ops:
  11.6 15.6 %collective-permute-start.2 = (bf16[128,1152]{1,0:T(8,128)(2,1)S(1)}, bf16[128,1152]{1,0:T(8,128)(2,1)S(1)}, u32[]{:S(2)}, u32[]{:S(2)}) collective-permute-start(bf16[128,1152]{1,0:T(8,128)(2,1)S(1)} %concatenate.7), channel_id=1, source_target_pairs={{0,4},{1,5},{2,6},{3,7},{4,0},{5,1},{6,2},{7,3},{8,12},{9,13},{10,... | collective-permute-start | bytes 884744 | tf_op jit(solution)/shard_map/ppermute | solution.py:160
  14.7 23.5 %collective-permute-start.3 = (bf16[128,1152]{1,0:T(8,128)(2,1)S(1)}, bf16[128,1152]{1,0:T(8,128)(2,1)S(1)}, u32[]{:S(2)}, u32[]{:S(2)}) collective-permute-start(bf16[128,1152]{1,0:T(8,128)(2,1)S(1)} %concatenate.7), channel_id=1, source_target_pairs={{0,8},{1,9},{2,10},{3,11},{4,12},{5,13},{6,14},{7,15},{8,0},{9,1},... | collective-permute-start | bytes 884744 | tf_op jit(solution)/shard_map/ppermute | solution.py:160
  17.3 21.6 %collective-permute-start.4 = (bf16[128,1152]{1,0:T(8,128)(2,1)S(1)}, bf16[128,1152]{1,0:T(8,128)(2,1)S(1)}, u32[]{:S(2)}, u32[]{:S(2)}) collective-permute-start(bf16[128,1152]{1,0:T(8,128)(2,1)S(1)} %concatenate.7), channel_id=1, source_target_pairs={{0,12},{1,13},{2,14},{3,15},{4,8},{5,9},{6,10},{7,11},{8,4},{9,5},... | collective-permute-start | bytes 884744 | tf_op jit(solution)/shard_map/ppermute | solution.py:160
  27.2 0.7 copy-start.8
  38.2 0.7 copy-start.10
  38.9 0.7 copy-start.12
  41.7 7.9 %copy-start.15 = (bf16[2,2,512,768]{3,2,1,0:T(8,128)(2,1)S(1)}, bf16[2,2,512,768]{3,2,1,0:T(8,128)(2,1)}, u32[]{:S(2)}) copy-start(bf16[2,2,512,768]{3,2,1,0:T(8,128)(2,1)} %param.14) | copy-start | bytes 9437188
  41.7 52.7 %all-to-all-start = ((bf16[8,2,120,8,128]{4,3,2,1,0:T(8,128)(2,1)}), bf16[8,2,120,8,128]{4,3,2,1,0:T(8,128)(2,1)}, u32[]{:S(2)}, u32[]{:S(2)}) async-start(bf16[8,2,120,8,128]{4,3,2,1,0:T(8,128)(2,1)} %copy.41), calls=%async_computation | async-start | bytes 7864320 | tf_op jit(solution)/shard_map/all_to_all | solution.py:152
  49.0 50.7 %all-gather.3.cloned.1.call-start = ((), (), s32[]{:S(2)}) async-start(), calls=%async_computation.4 | async-start | bytes 4718592 | tf_op jit(solution)/shard_map/all_gather | solution.py:226
  51.6 48.6 %copy-start.16 = (s32[32]{0:T(128)S(1)}, s32[32]{0:T(128)}, u32[]{:S(2)}) copy-start(s32[32]{0:T(128)} %param.18) | copy-start | bytes 388
  51.6 48.6 %copy-start.17 = (s32[32]{0:T(128)S(1)}, s32[32]{0:T(128)}, u32[]{:S(2)}) copy-start(s32[32]{0:T(128)} %param.19) | copy-start | bytes 388
  94.4 71.5 %all-to-all-start.1 = ((bf16[8,2,96,8,128]{4,3,2,1,0:T(8,128)(2,1)}), bf16[8,2,96,8,128]{4,3,2,1,0:T(8,128)(2,1)}, u32[]{:S(2)}, u32[]{:S(2)}) async-start(bf16[8,2,96,8,128]{4,3,2,1,0:T(8,128)(2,1)} %copy.42), calls=%async_computation.1 | async-start | bytes 6291456 | tf_op jit(solution)/shard_map/all_to_all | solution.py:152
  98.9 31.8 %all-gather.5.cloned.1.call-start = ((), (), s32[]{:S(2)}) async-start(), calls=%async_computation.5 | async-start | bytes 2359296 | tf_op jit(solution)/shard_map/all_gather | solution.py:227
  99.7 78.3 %collective-permute-start.7 = (bf16[2,1024,768]{2,1,0:T(8,128)(2,1)}, bf16[2,1024,768]{2,1,0:T(8,128)(2,1)S(1)}, u32[]{:S(2)}, u32[]{:S(2)}) collective-permute-start(bf16[2,1024,768]{2,1,0:T(8,128)(2,1)} %all-gather.3.cloned.1.call-done.refs_0_), channel_id=1, source_target_pairs={{0,1},{1,0},{2,3},{3,2},{4,5},{5,4},{6,7},{7,6},{8,9},{9,8},{10,11... | collective-permute-start | bytes 9437192 | tf_op jit(solution)/shard_map/ppermute | solution.py:160
  104.0 99.5 %collective-permute-start.5 = (bf16[9,120,8,128]{3,2,1,0:T(8,128)(2,1)}, bf16[9,120,8,128]{3,2,1,0:T(8,128)(2,1)}, u32[]{:S(2)}, u32[]{:S(2)}) collective-permute-start(bf16[9,120,8,128]{3,2,1,0:T(8,128)(2,1)} %shard_map.128), channel_id=1, source_target_pairs={{0,8},{1,9},{2,10},{3,11},{4,12},{5,13},{6,14},{7,15},{8,0},{9,1},... | collective-permute-start | bytes 6635528 | tf_op jit(solution)/shard_map/ppermute | solution.py:243
  130.8 47.2 %collective-permute-start.8 = (bf16[2,384,1024]{2,1,0:T(8,128)(2,1)}, bf16[2,384,1024]{2,1,0:T(8,128)(2,1)}, u32[]{:S(2)}, u32[]{:S(2)}) collective-permute-start(bf16[2,384,1024]{2,1,0:T(8,128)(2,1)} %all-gather.5.cloned.1.call-done.refs_1_), channel_id=1, source_target_pairs={{0,1},{1,0},{2,3},{3,2},{4,5},{5,4},{6,7},{7,6},{8,9},{9,8},{10,11... | collective-permute-start | bytes 4718600 | tf_op jit(solution)/shard_map/ppermute | solution.py:160
  130.8 1.0 copy-start.9
  131.7 1.0 copy-start.11
  132.7 1.0 copy-start.13
  135.6 42.4 %collective-permute-start.6 = (bf16[512,1152]{1,0:T(8,128)(2,1)}, bf16[512,1152]{1,0:T(8,128)(2,1)}, u32[]{:S(2)}, u32[]{:S(2)}) collective-permute-start(bf16[512,1152]{1,0:T(8,128)(2,1)} %bitcast.18.x_ref), channel_id=1, source_target_pairs={{0,2},{1,3},{2,0},{3,1},{4,6},{5,7},{6,4},{7,5},{8,10},{9,11},{10,... | collective-permute-start | bytes 3538952 | tf_op jit(solution)/shard_map/ppermute | solution.py:160
  165.9 12.1 %copy-start.1 = (bf16[2,1024,768]{2,1,0:T(8,128)(2,1)S(1)}, bf16[2,1024,768]{2,1,0:T(8,128)(2,1)}, u32[]{:S(2)}) copy-start(bf16[2,1024,768]{2,1,0:T(8,128)(2,1)} %all-gather.3.cloned.1.call-done.refs_0_) | copy-start | bytes 9437188
  165.9 12.1 %copy-start.2 = (bf16[2,384,1024]{2,1,0:T(8,128)(2,1)S(1)}, bf16[2,384,1024]{2,1,0:T(8,128)(2,1)}, u32[]{:S(2)}) copy-start(bf16[2,384,1024]{2,1,0:T(8,128)(2,1)} %all-gather.5.cloned.1.call-done.refs_1_) | copy-start | bytes 4718596
  170.1 1.2 copy-start.5
  186.7 1.0 copy-start.3
  196.4 1.0 copy-start.7
  212.4 1.9 copy-start
  214.3 4.8 %copy-start.6 = (bf16[9,96,8,128]{3,2,1,0:T(8,128)(2,1)S(1)}, bf16[9,96,8,128]{3,2,1,0:T(8,128)(2,1)}, u32[]{:S(2)}) copy-start(bf16[9,96,8,128]{3,2,1,0:T(8,128)(2,1)} %copy-done.5) | copy-start | bytes 5308420
  214.3 55.7 %copy-start.4 = (bf16[512,1024]{1,0:T(8,128)(2,1)S(1)}, bf16[512,1024]{1,0:T(8,128)(2,1)}, u32[]{:S(2)}) copy-start(bf16[512,1024]{1,0:T(8,128)(2,1)} %copy-done.3) | copy-start | bytes 3145732
  214.3 90.5 %all-to-all-start.2 = ((bf16[8,2,120,8,128]{4,3,2,1,0:T(8,128)(2,1)}), bf16[8,2,120,8,128]{4,3,2,1,0:T(8,128)(2,1)}, u32[]{:S(2)}, u32[]{:S(2)}) async-start(bf16[8,2,120,8,128]{4,3,2,1,0:T(8,128)(2,1)} %bitcast.71), calls=%async_computation.2 | async-start | bytes 7864320 | tf_op jit(solution)/shard_map/all_to_all | solution.py:152
  219.1 81.1 %copy-start.14 = (bf16[7,96,8,128]{3,2,1,0:T(8,128)(2,1)S(1)}, bf16[7,96,8,128]{3,2,1,0:T(8,128)(2,1)}, u32[]{:S(2)}) copy-start(bf16[7,96,8,128]{3,2,1,0:T(8,128)(2,1)} %get-tuple-element.190.refs_2_) | copy-start | bytes 4128772
  219.1 81.1 %collective-permute-start.9 = (bf16[9,96,8,128]{3,2,1,0:T(8,128)(2,1)S(1)}, bf16[9,96,8,128]{3,2,1,0:T(8,128)(2,1)S(1)}, u32[]{:S(2)}, u32[]{:S(2)}) collective-permute-start(bf16[9,96,8,128]{3,2,1,0:T(8,128)(2,1)S(1)} %copy-done.6), channel_id=1, source_target_pairs={{0,8},{1,9},{2,10},{3,11},{4,12},{5,13},{6,14},{7,15},{8,0},{9,1},... | collective-permute-start | bytes 5308424 | tf_op jit(solution)/shard_map/ppermute | solution.py:273
  221.4 48.6 %collective-permute-start.10 = (bf16[512,1024]{1,0:T(8,128)(2,1)}, bf16[512,1024]{1,0:T(8,128)(2,1)S(1)}, u32[]{:S(2)}, u32[]{:S(2)}) collective-permute-start(bf16[512,1024]{1,0:T(8,128)(2,1)} %copy-done.7), channel_id=1, source_target_pairs={{0,2},{1,3},{2,0},{3,1},{4,6},{5,7},{6,4},{7,5},{8,10},{9,11},{10,... | collective-permute-start | bytes 3145736 | tf_op jit(solution)/shard_map/ppermute | solution.py:160
  304.8 62.2 %all-to-all-start.3 = ((bf16[8,2,96,8,128]{4,3,2,1,0:T(8,128)(2,1)}), bf16[8,2,96,8,128]{4,3,2,1,0:T(8,128)(2,1)S(1)}, u32[]{:S(2)}, u32[]{:S(2)}) async-start(bf16[8,2,96,8,128]{4,3,2,1,0:T(8,128)(2,1)} %bitcast.39), calls=%async_computation.3 | async-start | bytes 6291456 | tf_op jit(solution)/shard_map/all_to_all | solution.py:152
  312.6 42.1 %collective-permute-start.13 = (bf16[128,1024]{1,0:T(8,128)(2,1)S(1)}, bf16[128,1024]{1,0:T(8,128)(2,1)S(1)}, u32[]{:S(2)}, u32[]{:S(2)}) collective-permute-start(bf16[128,1024]{1,0:T(8,128)(2,1)S(1)} %get-tuple-element.209), channel_id=1, source_target_pairs={{0,12},{1,13},{2,14},{3,15},{4,8},{5,9},{6,10},{7,11},{8,4},{9,5},... | collective-permute-start | bytes 786440 | tf_op jit(solution)/shard_map/ppermute | solution.py:160
  314.9 42.8 %collective-permute-start.12 = (bf16[128,1024]{1,0:T(8,128)(2,1)S(1)}, bf16[128,1024]{1,0:T(8,128)(2,1)S(1)}, u32[]{:S(2)}, u32[]{:S(2)}) collective-permute-start(bf16[128,1024]{1,0:T(8,128)(2,1)S(1)} %get-tuple-element.210), channel_id=1, source_target_pairs={{0,8},{1,9},{2,10},{3,11},{4,12},{5,13},{6,14},{7,15},{8,0},{9,1},... | collective-permute-start | bytes 786440 | tf_op jit(solution)/shard_map/ppermute | solution.py:160
  323.0 42.2 %collective-permute-start.11 = (bf16[128,1024]{1,0:T(8,128)(2,1)S(1)}, bf16[128,1024]{1,0:T(8,128)(2,1)S(1)}, u32[]{:S(2)}, u32[]{:S(2)}) collective-permute-start(bf16[128,1024]{1,0:T(8,128)(2,1)S(1)} %get-tuple-element.186), channel_id=1, source_target_pairs={{0,4},{1,5},{2,6},{3,7},{4,0},{5,1},{6,2},{7,3},{8,12},{9,13},{10,... | collective-permute-start | bytes 786440 | tf_op jit(solution)/shard_map/ppermute | solution.py:160
Sparse Core Ops, SparseCore 0:
  51.3 47.2 all-gather.2
  101.3 29.4 all-gather.4
